TPU v7x, 32 devices: a whole 2x2x4 slice. The times are simulated.
32 devices in a mesh: tile: 2 (over x), expert: 16 (over z, y, core).
Axes of the slice: x: 2, y: 2, z: 4, core: 2. Of those that a mesh axis runs over, the one named last changes fastest.
Arguments:
- patches: bfloat16 [16, 8, 32, 1152], P('expert', 'tile'), may hold values from -6 to 6
- norm1_gain: float32 [1152], replicated, may hold values from 0.1 to 1.9
- qkv_weight: bfloat16 [1152, 3, 1152], P(None, None, 'tile'), may hold values from -8 to 8
- qkv_bias: float32 [3, 1152], P(None, 'tile'), may hold values from -3 to 3
- out_weight: bfloat16 [1152, 1152], P('tile'), may hold values from -0.1875 to 0.1875
- out_bias: float32 [1152], replicated, may hold values from -3 to 3
- norm2_gain: float32 [1152], replicated, may hold values from 0.1 to 1.9
- proj_weight: bfloat16 [4608, 2048], P('expert', 'tile'), may hold values from -0.09375 to 0.09375
- moe_gain: float32 [2048], replicated, may hold values from 0.1 to 1.9
- expert_in: bfloat16 [16, 2048, 2, 1408], P('expert', None, None, 'tile'), may hold values from -0.125 to 0.125
- expert_out: bfloat16 [16, 1408, 2048], P('expert', 'tile'), may hold values from -0.15625 to 0.15625
- shared_in: bfloat16 [2048, 2, 1408], P(None, None, 'tile'), may hold values from -0.125 to 0.125
- shared_out: bfloat16 [1408, 2048], P('tile'), may hold values from -0.15625 to 0.15625
- routes: int32 [16, 4, 16, 6], P('expert'), may hold values from 0 to 15, all different within a row; in each aligned block of 32 rows (0 to 31, 32 to 63, ..., all dimensions but the last counted through in order) at most 24 rows name the same one
- gates: float32 [16, 4, 16, 6], P('expert', 'tile'), may hold values from 0.1 to 1
Outputs:
- moe_tokens: bfloat16 [16, 4, 16, 2048], P('expert', 'tile')
Inputs may be any that keep to these rules, and one draw needn't show every extreme that they name: `routes`: each merged token names 6 different experts. Flattening the merged tokens in the order page, row, column into aligned blocks of 32 (the merged tokens of one device), no expert is named more than 24 times in a block, a bound that some block reaches.
All inputs are finite; a program needn't handle non-finite values.
Results may differ from a plain program's by a relative error of at most 0.02.
Values may be sent and summed in bfloat16 or wider, within the bound.
No kernel may reach another device: no remote copies, remote signals or barrier semaphores. Data moves between devices by JAX's collectives and lax.ppermute only.
A program may use at most 128 MiB of HBM per device.

v0:
```python
from functools import partial
import math

import jax
import jax.numpy as jnp
from jax import lax
from jax.sharding import PartitionSpec as P

HD = 72


norm_eps = 1e-06
rope_base = 10000.0


def layer_norm(values, gain_vec):
    centre = values - jnp.mean(values, axis=-1, keepdims=True)
    spread = jnp.mean(centre * centre, axis=-1, keepdims=True)
    return centre * lax.rsqrt(spread + norm_eps) * gain_vec


def rms_norm(values, gain_vec):
    return (
        values * lax.rsqrt(jnp.mean(values * values, axis=-1, keepdims=True) + norm_eps) * gain_vec
    )


def rope_tables(positions, columns, head_size):
    quarter = head_size // 4
    inverse = jnp.exp(jnp.arange(quarter).astype(jnp.float32) * (-math.log(rope_base) / quarter))
    row_angle = (positions // columns).astype(jnp.float32)[:, None] * inverse[None, :]
    col_angle = (positions % columns).astype(jnp.float32)[:, None] * inverse[None, :]
    return (jnp.cos(row_angle), jnp.sin(row_angle), jnp.cos(col_angle), jnp.sin(col_angle))


def rotate(values, tables):
    cos_row, sin_row, cos_col, sin_col = tables
    quarter = values.shape[-1] // 4
    row_a = values[..., :quarter]
    row_b = values[..., quarter : 2 * quarter]
    col_a = values[..., 2 * quarter : 3 * quarter]
    col_b = values[..., 3 * quarter :]
    return jnp.concatenate(
        [
            row_a * cos_row[:, None] - row_b * sin_row[:, None],
            row_b * cos_row[:, None] + row_a * sin_row[:, None],
            col_a * cos_col[:, None] - col_b * sin_col[:, None],
            col_b * cos_col[:, None] + col_a * sin_col[:, None],
        ],
        axis=-1,
    )


def attend(query_rows, key_rows, value_rows, divisor):
    count = query_rows.shape[0]
    width = min(count, 512)
    blocks = query_rows.reshape(count // width, width, query_rows.shape[1], query_rows.shape[2])

    def one_block(block):
        scores = (
            jnp.einsum("qhd,khd->hqk", block, key_rows, preferred_element_type=jnp.float32)
            / divisor
        )
        weights = jax.nn.softmax(scores, axis=-1).astype(jnp.bfloat16)
        return jnp.einsum(
            "hqk,khd->qhd", weights, value_rows, preferred_element_type=jnp.float32
        ).astype(jnp.bfloat16)

    return lax.map(one_block, blocks).reshape(count, -1)


def block_slots(block_routes, experts_count, capacity):
    picks = block_routes.reshape(-1)
    onehot = (picks[:, None] == jnp.arange(experts_count)[None, :]).astype(jnp.int32)
    earlier = jnp.cumsum(onehot, axis=0) - onehot
    ranks = jnp.sum(earlier * onehot, axis=1)
    owners_flat = jnp.arange(picks.shape[0]) // block_routes.shape[1]
    table = (
        jnp.full((experts_count * capacity,), -1, dtype=jnp.int32)
        .at[picks * capacity + ranks]
        .set(owners_flat)
    )
    return (ranks.reshape(block_routes.shape), table.reshape(experts_count, capacity))


def per_device(
    patches,
    norm1_gain,
    qkv_weight,
    qkv_bias,
    out_weight,
    out_bias,
    norm2_gain,
    proj_weight,
    moe_gain,
    expert_in,
    expert_out,
    shared_in,
    shared_out,
    routes,
    gates,
):
    tiles = lax.axis_size("tile")
    experts_count = lax.axis_size("expert")
    tile_id = lax.axis_index("tile")
    row_count = patches.shape[1]
    columns = patches.shape[2]
    width_vit = patches.shape[3]
    local_rows = row_count * columns
    inputs = patches.reshape(local_rows, width_vit).astype(jnp.float32)
    normed = layer_norm(inputs, norm1_gain).astype(jnp.bfloat16)
    heads_here = qkv_weight.shape[2] // HD
    qkv_flat = qkv_weight.reshape(width_vit, -1)
    bias_rows = qkv_bias.reshape(1, 3, heads_here, HD)
    piece = lax.all_gather(normed, "tile", axis=0, tiled=True)
    mixed = (
        jnp.dot(piece, qkv_flat, preferred_element_type=jnp.float32).reshape(
            piece.shape[0], 3, heads_here, HD
        )
        + bias_rows
    )
    tables = rope_tables(jnp.arange(piece.shape[0]), columns, HD)
    page_qkv = jnp.stack(
        [rotate(mixed[:, 0], tables), rotate(mixed[:, 1], tables), mixed[:, 2]], axis=1
    ).astype(jnp.bfloat16)
    attended = attend(page_qkv[:, 0], page_qkv[:, 1], page_qkv[:, 2], math.sqrt(HD))
    mixed_heads = lax.psum_scatter(
        jnp.dot(attended, out_weight, preferred_element_type=jnp.float32).astype(jnp.bfloat16),
        "tile",
        scatter_dimension=0,
        tiled=True,
    ).astype(jnp.float32)
    hidden = inputs + mixed_heads + out_bias
    normed_out = layer_norm(hidden, norm2_gain).astype(jnp.bfloat16)
    merged = (
        normed_out.reshape(row_count // 2, 2, columns // 2, 2, width_vit)
        .transpose(0, 2, 1, 3, 4)
        .reshape(-1, 4 * width_vit)
    )
    merged_count = merged.shape[0]
    group_merged = lax.all_gather(merged, "tile", axis=0, tiled=True)
    projected = jnp.dot(
        group_merged,
        lax.all_gather(proj_weight, "expert", axis=0, tiled=True),
        preferred_element_type=jnp.float32,
    ).astype(jnp.bfloat16)
    tokens_moe = lax.all_to_all(projected, "tile", split_axis=0, concat_axis=1, tiled=True)
    width_moe = tokens_moe.shape[1]
    moe_in = rms_norm(tokens_moe.astype(jnp.float32), moe_gain).astype(jnp.bfloat16)
    group_in = lax.all_gather(moe_in, "tile", axis=0, tiled=True)
    shared_gated = jnp.dot(
        group_in, shared_in.reshape(width_moe, -1), preferred_element_type=jnp.float32
    ).reshape(group_in.shape[0], 2, -1)
    shared_hidden = (jax.nn.silu(shared_gated[:, 0]) * shared_gated[:, 1]).astype(jnp.bfloat16)
    shared_part = lax.psum_scatter(
        jnp.dot(shared_hidden, shared_out, preferred_element_type=jnp.float32).astype(jnp.bfloat16),
        "tile",
        scatter_dimension=0,
        tiled=True,
    ).astype(jnp.float32)
    top_count = routes.shape[-1]
    capacity = max(2, min(merged_count, 2 * merged_count * top_count // experts_count))
    group_routes = routes.reshape(tiles, merged_count, top_count)
    group_ranks, group_owners = jax.vmap(
        partial(block_slots, experts_count=experts_count, capacity=capacity)
    )(group_routes)
    own_routes = lax.dynamic_index_in_dim(group_routes, tile_id, 0, keepdims=False)
    own_ranks = lax.dynamic_index_in_dim(group_ranks, tile_id, 0, keepdims=False)
    empty_value = jnp.zeros((), jnp.bfloat16)
    table = lax.dynamic_index_in_dim(group_owners, tile_id, 0, keepdims=False)
    used = table >= 0
    outgoing = jnp.where(used[..., None], moe_in[jnp.where(used, table, 0)], empty_value)
    received = lax.all_to_all(outgoing, "expert", split_axis=0, concat_axis=0, tiled=True)
    arrived = lax.all_gather(received[:, None], "tile", axis=1, tiled=True)
    slot_rows = arrived.reshape(-1, width_moe)
    gated = jnp.dot(
        slot_rows, expert_in.reshape(width_moe, -1), preferred_element_type=jnp.float32
    ).reshape(slot_rows.shape[0], 2, -1)
    expert_hidden = (jax.nn.silu(gated[:, 0]) * gated[:, 1]).astype(jnp.bfloat16)
    partial_out = (
        jnp.dot(
            expert_hidden,
            expert_out.reshape(expert_hidden.shape[1], width_moe),
            preferred_element_type=jnp.float32,
        )
        .astype(jnp.bfloat16)
        .reshape(arrived.shape)
    )
    came_back = lax.all_to_all(partial_out, "expert", split_axis=0, concat_axis=0, tiled=True)
    returned = lax.psum_scatter(
        came_back.astype(jnp.float32).astype(jnp.bfloat16), "tile", scatter_dimension=1, tiled=True
    )
    results_flat = returned.reshape(experts_count * capacity, width_moe)
    pick_index = own_routes * capacity + own_ranks
    gate_rows = gates.reshape(merged_count, top_count)
    routed = jnp.zeros((merged_count, width_moe), jnp.float32)
    for position in range(top_count):
        routed = routed + gate_rows[:, position : position + 1] * results_flat[
            pick_index[:, position]
        ].astype(jnp.float32)
    output = tokens_moe.astype(jnp.float32) + shared_part + routed
    return output.astype(jnp.bfloat16).reshape(1, row_count // 2, columns // 2, width_moe)


def solution(mesh):
    placed = (
        P("expert", "tile", None, None),
        P(),
        P(None, None, "tile"),
        P(None, "tile"),
        P("tile", None),
        P(),
        P(),
        P("expert", "tile"),
        P(),
        P("expert", None, None, "tile"),
        P("expert", "tile", None),
        P(None, None, "tile"),
        P("tile", None),
        P("expert", None, None, None),
        P("expert", "tile", None, None),
    )
    return jax.shard_map(
        per_device,
        mesh=mesh,
        in_specs=placed,
        out_specs=P("expert", "tile", None, None),
        check_vma=False,
    )
```

profile of v0, /device:TPU:0, one launch (start us, length us, event | category | flops | bytes accessed | tf_op | source)
XLA Modules:
  0.0 423.1 jit_solution(9806178425398681026)
XLA Ops:
  11.2 10.6 %all_gather.15 = bf16[256,1152]{1,0:T(8,128)(2,1)S(1)} all-gather(bf16[128,1152]{1,0:T(8,128)(2,1)S(1)} %fusion.16), channel_id=1, replica_groups=mesh['tile'=2,'expert'=16] {'tile'}, dimensions={0}, use_global_device_ids=true | all-gather | bytes 884736 | tf_op jit(solution)/shard_map/all_gather | solution.py:115
  22.6 3.5 convolution_add_fusion
  27.5 3.1 fusion.74
  37.2 19.6 %scatter_fusion = s32[2,384]{1,0:T(2,128)S(1)} fusion(s32[2,384]{1,0:T(2,128)S(1)} %broadcast_in_dim.19, s32[384]{0:T(512)S(1)} %reshape.402, s32[384]{0:T(512)S(1)} %reshape.404), kind=kCustom, calls=%fused_computation.7 | custom fusion | bytes 7680 | tf_op jit(solution)/shard_map/vmap()/scatter | solution.py:81
  61.8 9.1 %all_gather.16 = bf16[64,4608]{1,0:T(8,128)(2,1)S(1)} all-gather(bf16[32,4608]{1,0:T(8,128)(2,1)} %reshape.329), channel_id=1, replica_groups=mesh['tile'=2,'expert'=16] {'tile'}, dimensions={0}, use_global_device_ids=true | all-gather | bytes 884736 | tf_op jit(solution)/shard_map/all_gather | solution.py:141
  70.9 49.1 %all-gather.4.cloned.1.call-done = bf16[4608,1024]{1,0:T(8,128)(2,1)} async-done(((bf16[288,1024]{1,0:T(8,128)(2,1)}), bf16[4608,1024]{1,0:T(8,128)(2,1)}) %all-gather.4.cloned.1.call-update) | async-done | bytes 9437200 | tf_op jit(solution)/shard_map/all_gather | solution.py:144
  120.0 6.1 %convolution_convert_fusion.4 = bf16[64,1024]{1,0:T(8,128)(2,1)} fusion(bf16[64,4608]{1,0:T(8,128)(2,1)S(1)} %all_gather.16, bf16[4608,1024]{1,0:T(8,128)(2,1)} %all-gather.4.cloned.1.call-done), kind=kOutput, calls=%fused_computation.26 | convolution fusion | flops 604045312 | bytes 10158080 | tf_op jit(solution)/shard_map/dot_general | solution.py:142
  126.1 3.4 all-to-all-start
  129.5 4.4 %all-to-all-done = bf16[2,32,1024]{2,1,0:T(8,128)(2,1)S(1)} async-done(((bf16[2,32,1024]{2,1,0:T(8,128)(2,1)}), bf16[2,32,1024]{2,1,0:T(8,128)(2,1)S(1)}, u32[]{:S(2)}, u32[]{:S(2)}) %all-to-all-start) | async-done | bytes 131104 | tf_op jit(solution)/shard_map/all_to_all | solution.py:147
  134.2 3.1 gather_fusion
  138.9 39.3 %all_to_all.23 = bf16[16,24,2048]{2,1,0:T(8,128)(2,1)} all-to-all(bf16[16,24,2048]{2,1,0:T(8,128)(2,1)S(1)} %broadcast_select_fusion), channel_id=1, replica_groups=mesh['tile'=2,'expert'=16] {'expert'}, dimensions={0} | all-to-all | bytes 3145728 | tf_op jit(solution)/shard_map/all_to_all | solution.py:173
  178.5 44.2 %all-gather.6.cloned.1.call-done = bf16[16,48,2048]{2,1,0:T(8,128)(2,1)} async-done(((bf16[16,24,2048]{2,1,0:T(8,128)(2,1)}), bf16[16,48,2048]{2,1,0:T(8,128)(2,1)}) %all-gather.6.cloned.1.call-update) | async-done | bytes 3145744 | tf_op jit(solution)/shard_map/all_gather | solution.py:174
  222.7 7.7 %fusion.1 = f32[768,2,704]{0,2,1:T(8,128)S(1)} fusion(bf16[768,2048,1]{1,0,2:T(8,128)(2,1)} %bitcast.156, bf16[1,2048,2,704]{1,3,2,0:T(8,128)(2,1)} %param.24), kind=kOutput, calls=%fused_computation.9 | convolution fusion | flops 4429185024 | bytes 13238272 | tf_op jit(solution)/shard_map/dot_general | solution.py:176
  230.4 3.0 convolution_convert_fusion
  233.4 75.3 %all_to_all.24 = bf16[16,2,24,2048]{3,2,1,0:T(8,128)(2,1)} all-to-all(bf16[16,2,24,2048]{3,2,1,0:T(8,128)(2,1)S(1)} %bitcast.149), channel_id=1, replica_groups=mesh['tile'=2,'expert'=16] {'expert'}, dimensions={0} | all-to-all | bytes 6291456 | tf_op jit(solution)/shard_map/all_to_all | solution.py:189
  309.2 7.0 %all_gather.18 = bf16[64,2048]{1,0:T(8,128)(2,1)S(1)} all-gather(bf16[32,2048]{1,0:T(8,128)(2,1)S(1)} %multiply_convert_fusion.1), channel_id=1, replica_groups=mesh['tile'=2,'expert'=16] {'tile'}, dimensions={0}, use_global_device_ids=true | all-gather | bytes 393216 | tf_op jit(solution)/shard_map/all_gather | solution.py:150
  316.2 4.6 %fusion.3 = f32[64,2,704]{2,0,1:T(8,128)S(1)} fusion(bf16[2048,2,704]{0,2,1:T(8,128)(2,1)} %param.26, bf16[64,2048]{1,0:T(8,128)(2,1)S(1)} %all_gather.18), kind=kOutput, calls=%fused_computation.11 | convolution fusion | flops 369098752 | bytes 6389760 | tf_op jit(solution)/shard_map/dot_general | solution.py:151
  323.5 70.8 %all-reduce.4.cloned.1.call-done = bf16[16,2,24,2048]{3,2,1,0:T(8,128)(2,1)} async-done(((bf16[16,2,24,2048]{3,2,1,0:T(8,128)(2,1)}), bf16[16,2,24,2048]{3,2,1,0:T(8,128)(2,1)}) %all-reduce.4.cloned.1.call-update) | async-done | bytes 3145744
  394.3 3.4 constant_dynamic-slice_fusion
  400.0 2.4 gather_fusion.2
  402.4 2.4 gather_fusion.3
  404.8 3.0 gather_fusion.4
  407.8 3.0 gather_fusion.5
  410.9 3.0 gather_fusion.6
  (104 shorter events, 26.9 us)
Async XLA Ops:
  7.4 223.0 %copy-start = (bf16[1,704,2048]{2,1,0:T(8,128)(2,1)S(1)}, bf16[1,704,2048]{2,1,0:T(8,128)(2,1)}, u32[]{:S(2)}) copy-start(bf16[1,704,2048]{2,1,0:T(8,128)(2,1)} %param.25) | copy-start | bytes 8650756
  7.4 49.7 %reduce-scatter.4.cloned.1.call-start = ((), (), s32[]{:S(2)}) async-start(), calls=%async_computation.5 | async-start | bytes 884736 | tf_op jit(solution)/shard_map/reduce_scatter | solution.py:127
  26.1 1.4 copy-start.3
  30.6 2.2 copy-start.11
  32.8 2.1 copy-start.5
  34.4 85.6 %all-gather.4.cloned.1.call-start = ((), (), s32[]{:S(2)}) async-start(), calls=%async_computation.6 | async-start | bytes 10027008 | tf_op jit(solution)/shard_map/all_gather | solution.py:144
  37.2 19.9 %copy-start.1 = (bf16[1,4,32,1152]{3,2,1,0:T(8,128)(2,1)S(1)}, bf16[1,4,32,1152]{3,2,1,0:T(8,128)(2,1)}, u32[]{:S(2)}) copy-start(bf16[1,4,32,1152]{3,2,1,0:T(8,128)(2,1)} %param.15) | copy-start | bytes 884740
  37.2 19.9 %copy-start.4 = (f32[1152]{0:T(1024)S(1)}, f32[1152]{0:T(1024)}, u32[]{:S(2)}) copy-start(f32[1152]{0:T(1024)} %param.20) | copy-start | bytes 13828
  37.2 22.3 %copy-start.6 = (f32[1152]{0:T(1024)S(1)}, f32[1152]{0:T(1024)}, u32[]{:S(2)}) copy-start(f32[1152]{0:T(1024)} %param.21) | copy-start | bytes 13828
  70.9 63.2 %copy-start.7 = (f32[2048]{0:T(1024)S(1)}, f32[2048]{0:T(1024)}, u32[]{:S(2)}) copy-start(f32[2048]{0:T(1024)} %param.23) | copy-start | bytes 24580
  126.1 7.8 %all-to-all-start = ((bf16[2,32,1024]{2,1,0:T(8,128)(2,1)}), bf16[2,32,1024]{2,1,0:T(8,128)(2,1)S(1)}, u32[]{:S(2)}, u32[]{:S(2)}) async-start(bf16[2,32,1024]{2,1,0:T(8,128)(2,1)} %bitcast.153), calls=%async_computation.1 | async-start | bytes 262144 | tf_op jit(solution)/shard_map/all_to_all | solution.py:147
  129.5 93.2 %all-gather.6.cloned.1.call-start = ((), (), s32[]{:S(2)}) async-start(), calls=%async_computation.8 | async-start | bytes 4718592 | tf_op jit(solution)/shard_map/all_gather | solution.py:174
  178.3 216.0 %all-reduce.4.cloned.1.call-start = ((), (), s32[]{:S(2)}) async-start(), calls=%async_computation.9 | async-start | bytes 6291456
  308.8 105.1 %reduce-scatter.6.cloned.1.call-start = ((), (), s32[]{:S(2)}) async-start(), calls=%async_computation.7 | async-start | bytes 393216 | tf_op jit(solution)/shard_map/reduce_scatter | solution.py:155
  316.2 4.6 %copy-start.2 = (bf16[704,2048]{1,0:T(8,128)(2,1)S(1)}, bf16[704,2048]{1,0:T(8,128)(2,1)}, u32[]{:S(2)}) copy-start(bf16[704,2048]{1,0:T(8,128)(2,1)} %param.27) | copy-start | bytes 8650756
  320.8 1.4 copy-start.8
  320.8 1.5 copy-start.12
  404.8 9.1 %copy-start.9 = (f32[32]{0:T(128)S(1)}, f32[32]{0:T(128)}, u32[]{:S(2)}) copy-start(f32[32]{0:T(128)} %get-tuple-element.40) | copy-start | bytes 388
  407.8 6.1 %copy-start.10 = (f32[32]{0:T(128)S(1)}, f32[32]{0:T(128)}, u32[]{:S(2)}) copy-start(f32[32]{0:T(128)} %get-tuple-element.41) | copy-start | bytes 388
Sparse Core Ops, SparseCore 0:
  34.5 16.7 reduce-scatter.3
  178.4 44.2 all-gather.5
  308.9 85.3 all-reduce.3
  396.3 11.6 reduce-scatter.5
Sparse Core Ops, SparseCore 1:
  37.4 82.5 all-gather.3
where the time goes:
time: 424 us; the launch traced here: 423 us
  waiting for transfers between devices  169 us (40%)
  blocking collectives  141 us (33%)
  local copies, waits for them, and re-layouts  47 us (11%)
  matrix products  33.1 us (8%)
  between operations  15 us (4%)
  other arithmetic  13.9 us (3%)
    all_to_all x1, blocking collectives, per_device(): lax.all_to_all(partial_out, 'expert', split_axis=0, concat_axis=0, tiled=...  75.3 us
    unnamed x6, waiting for transfers between devices  71.4 us
    all_gather x1, waiting for transfers between devices, per_device(): lax.all_gather(proj_weight, 'expert', axis=0, tiled=True)  49.1 us
    all_gather x1, waiting for transfers between devices, per_device(): arrived = lax.all_gather(received[:, None], 'tile', axis=1, tiled=True)  44.2 us
    all_to_all x1, blocking collectives, per_device(): lax.all_to_all(outgoing, 'expert', split_axis=0, concat_axis=0, tiled=True)  39.3 us
    scatter x2, local copies, waits for them, and re-layouts, block_slots(): table = jnp.full((experts_count * capacity,), -1, dtype=jnp.int32).at[pic...  19.7 us
    gather x6, local copies, waits for them, and re-layouts, per_device(): results_flat[pick_index[:, position]].astype(jnp.float32)  16.2 us
    all_gather x1, blocking collectives, per_device(): piece = lax.all_gather(normed, 'tile', axis=0, tiled=True)  10.6 us
  transfers between devices with their start and end apart: 6, of which 4 were waited for; matrix products, arithmetic and copies ran while one was open for 13% of the time, Pallas kernels for 0%

commit v1 on v0

--- a/solution.py
+++ b/solution.py
@@ -83,7 +83,7 @@
     return (ranks.reshape(block_routes.shape), table.reshape(experts_count, capacity))
 
 
-def per_device(
+def per_device_slots(
     patches,
     norm1_gain,
     qkv_weight,
@@ -202,6 +202,255 @@
     return output.astype(jnp.bfloat16).reshape(1, row_count // 2, columns // 2, width_moe)
 
 
+def near_shift(values, grid, moved):
+    tiles, outer, inner, cores = grid
+    pairs = []
+    for source in range(tiles * outer * inner * cores):
+        place, rest = [], source
+        for size in reversed(grid):
+            place.append(rest % size)
+            rest //= size
+        target = 0
+        for spot, size, step in zip(reversed(place), grid, moved):
+            target = target * size + (spot + step) % size
+        pairs.append((source, target))
+    return lax.ppermute(values, ("tile", "expert"), pairs)
+
+
+def rope_tables_at(rows, columns, head_size):
+    quarter = head_size // 4
+    inverse = jnp.exp(jnp.arange(quarter).astype(jnp.float32) * (-math.log(rope_base) / quarter))
+    row_angle = rows.astype(jnp.float32)[:, None] * inverse[None, :]
+    col_angle = columns.astype(jnp.float32)[:, None] * inverse[None, :]
+    return (jnp.cos(row_angle), jnp.sin(row_angle), jnp.cos(col_angle), jnp.sin(col_angle))
+
+
+def attend_rows(query_rows, key_rows, value_rows, divisor):
+    scores = (
+        jnp.einsum("qhd,khd->hqk", query_rows, key_rows, preferred_element_type=jnp.float32)
+        / divisor
+    )
+    weights = jax.nn.softmax(scores, axis=-1).astype(jnp.bfloat16)
+    return (
+        jnp.einsum("hqk,khd->qhd", weights, value_rows, preferred_element_type=jnp.float32)
+        .astype(jnp.bfloat16)
+        .reshape(query_rows.shape[0], -1)
+    )
+
+
+def per_device_near(
+    patches,
+    norm1_gain,
+    qkv_weight,
+    qkv_bias,
+    out_weight,
+    out_bias,
+    norm2_gain,
+    proj_weight,
+    moe_gain,
+    expert_in,
+    expert_out,
+    shared_in,
+    shared_out,
+    routes,
+    gates,
+):
+    experts_count = lax.axis_size("expert")
+    outer = experts_count // 4
+    grid = (2, outer, 2, 2)
+    shift = partial(near_shift, grid=grid)
+    tile_id = lax.axis_index("tile")
+    expert_id = lax.axis_index("expert")
+    outer_id, inner_id, core_id = expert_id // 4, (expert_id // 2) % 2, expert_id % 2
+    row_count, columns, width_vit = patches.shape[1:]
+    local_rows = row_count * columns
+    token_count = local_rows // 4
+    heads_here = qkv_weight.shape[2] // HD
+
+    def by_tile(mine, other):
+        first = tile_id == 0
+        return jnp.where(first, mine, other), jnp.where(first, other, mine)
+
+    own_patches = (
+        patches.reshape(row_count // 2, 2, columns // 2, 2, width_vit)
+        .transpose(1, 3, 0, 2, 4)
+        .reshape(local_rows, width_vit)
+    )
+    other_patches = shift(own_patches, moved=(1, 0, 0, 0))
+
+    proj_rows = [proj_weight] + [
+        shift(proj_weight, moved=(0, step, 0, 0)) for step in range(1, outer)
+    ]
+    proj_pairs = [(rows, shift(rows, moved=(0, 0, 0, 1))) for rows in proj_rows]
+
+    top_count = routes.shape[-1]
+    page_routes = routes.reshape(2, token_count, top_count)
+    own_routes = lax.dynamic_index_in_dim(page_routes, tile_id, 0, keepdims=False)
+    own_gates = gates.reshape(token_count, top_count)
+    dense_gates = jnp.sum(
+        jnp.where(
+            own_routes[:, :, None] == jnp.arange(experts_count)[None, None, :],
+            own_gates[:, :, None],
+            0.0,
+        ),
+        axis=1,
+    )
+    all_gates = lax.all_gather(dense_gates, ("expert", "tile"), axis=0, tiled=True)
+    expert_gates = jnp.sum(
+        jnp.where(jnp.arange(experts_count)[None, :] == expert_id, all_gates, 0.0), axis=1
+    ).reshape(experts_count, 2 * token_count)
+
+    place = jnp.arange(local_rows)
+    pair_size = token_count
+    parity, within = place // pair_size, place % pair_size
+    patch_rows = 2 * (within // (columns // 2)) + parity // 2
+    patch_cols = 2 * (within % (columns // 2)) + parity % 2
+
+    def project_qkv(rows, tile):
+        normed = layer_norm(rows.astype(jnp.float32), norm1_gain).astype(jnp.bfloat16)
+        mixed = jnp.dot(
+            normed, qkv_weight.reshape(width_vit, -1), preferred_element_type=jnp.float32
+        ).reshape(rows.shape[0], 3, heads_here, HD) + qkv_bias.reshape(1, 3, heads_here, HD)
+        tables = rope_tables_at(tile * row_count + patch_rows, patch_cols, HD)
+        return (
+            rotate(mixed[:, 0], tables).astype(jnp.bfloat16),
+            rotate(mixed[:, 1], tables).astype(jnp.bfloat16),
+            mixed[:, 2].astype(jnp.bfloat16),
+        )
+
+    own_query, own_key, own_value = project_qkv(own_patches, tile_id)
+    other_query, other_key, other_value = project_qkv(other_patches, 1 - tile_id)
+    keys = jnp.concatenate([own_key, other_key], axis=0)
+    values = jnp.concatenate([own_value, other_value], axis=0)
+    other_part = jnp.dot(
+        attend_rows(other_query, keys, values, math.sqrt(HD)),
+        out_weight,
+        preferred_element_type=jnp.float32,
+    ).astype(jnp.bfloat16)
+    arrived_part = shift(other_part, moved=(1, 0, 0, 0))
+    own_part = jnp.dot(
+        attend_rows(own_query, keys, values, math.sqrt(HD)),
+        out_weight,
+        preferred_element_type=jnp.float32,
+    )
+    hidden = (
+        own_patches.astype(jnp.float32) + own_part + arrived_part.astype(jnp.float32) + out_bias
+    )
+    normed_out = layer_norm(hidden, norm2_gain).astype(jnp.bfloat16)
+
+    half = width_vit // 2
+    low_half, high_half = normed_out[:, :half], normed_out[:, half:]
+    kept = jnp.where(inner_id == 0, low_half, high_half).reshape(4, token_count, half)
+    given = jnp.where(inner_id == 0, high_half, low_half).reshape(4, token_count, half)
+    from_tile = shift(kept, moved=(1, 0, 0, 0))
+    from_inner = shift(given, moved=(0, 0, 1, 0))
+    from_both = shift(given, moved=(1, 0, 1, 0))
+    features = jnp.concatenate(
+        [*by_tile(kept, from_tile), *by_tile(from_inner, from_both)], axis=1
+    )
+    quarter = half // 2
+    low_quarter, high_quarter = features[:, :, :quarter], features[:, :, quarter:]
+    own_quarter = jnp.where(core_id == 0, low_quarter, high_quarter)
+    other_quarter = jnp.where(core_id == 0, high_quarter, low_quarter)
+    projected = 0.0
+    for step, (own_rows, core_rows) in enumerate(proj_pairs):
+        window = (outer_id - step) % outer
+        for side, weight in ((own_quarter, own_rows), (other_quarter, core_rows)):
+            projected = projected + jnp.dot(
+                lax.dynamic_index_in_dim(side, window, 0, keepdims=False),
+                weight,
+                preferred_element_type=jnp.float32,
+            )
+    page_tokens = 2 * token_count
+    inner_part = shift(projected[page_tokens:].astype(jnp.bfloat16), moved=(0, 0, 1, 0))
+    tokens_half = (projected[:page_tokens] + inner_part.astype(jnp.float32)).astype(jnp.bfloat16)
+
+    width_moe = 2 * tokens_half.shape[1]
+    shared_flat = shared_in.reshape(width_moe, -1)
+    expert_flat = expert_in.reshape(width_moe, -1)
+    expert_back = expert_out.reshape(-1, width_moe)
+    contributions = []
+    residual = None
+    halves_by_step = [tokens_half] + [
+        shift(tokens_half, moved=(0, step, 0, 0)) for step in range(1, outer)
+    ]
+    for step, held in enumerate(halves_by_step):
+        over_tile = shift(held, moved=(1, 0, 0, 0))
+        over_inner = shift(held, moved=(0, 0, 1, 0))
+        over_both = shift(held, moved=(1, 0, 1, 0))
+        block = jnp.stack([held, over_tile, over_inner, over_both])
+        core_block = shift(block, moved=(0, 0, 0, 1))
+        mine = jnp.concatenate([block[0], block[2], core_block[0], core_block[2]], axis=0)
+        tiles_other = jnp.concatenate([block[1], block[3], core_block[1], core_block[3]], axis=0)
+        tokens = jnp.concatenate(by_tile(mine, tiles_other), axis=1)
+        moe_in = rms_norm(tokens.astype(jnp.float32), moe_gain).astype(jnp.bfloat16)
+        gated = jnp.dot(moe_in, expert_flat, preferred_element_type=jnp.float32)
+        units = gated.shape[1] // 2
+        hidden_units = (jax.nn.silu(gated[:, :units]) * gated[:, units:]).astype(jnp.bfloat16)
+        result = jnp.dot(hidden_units, expert_back, preferred_element_type=jnp.float32)
+        outer_page = (outer_id - step) % outer
+        step_gates = jnp.concatenate(
+            [
+                lax.dynamic_index_in_dim(
+                    expert_gates,
+                    outer_page * 4 + (inner_id ^ other_inner) * 2 + (core_id ^ other_core),
+                    0,
+                    keepdims=False,
+                )
+                for other_core in range(2)
+                for other_inner in range(2)
+            ]
+        )
+        result = result * step_gates[:, None]
+        if step == 0:
+            residual = lax.dynamic_slice_in_dim(
+                tokens[:page_tokens], tile_id * token_count, token_count, 0
+            )
+            shared_gated = jnp.dot(
+                moe_in[:page_tokens], shared_flat, preferred_element_type=jnp.float32
+            )
+            shared_units = shared_gated.shape[1] // 2
+            shared_hidden = (
+                jax.nn.silu(shared_gated[:, :shared_units]) * shared_gated[:, shared_units:]
+            ).astype(jnp.bfloat16)
+            shared_part = jnp.dot(shared_hidden, shared_out, preferred_element_type=jnp.float32)
+            result = jnp.concatenate(
+                [result[:page_tokens] + shared_part, result[page_tokens:]], axis=0
+            )
+        contributions.append(result.astype(jnp.bfloat16))
+
+    total = residual.astype(jnp.float32)
+    for step, result in enumerate(contributions):
+        across = shift(result[2 * page_tokens :], moved=(0, 0, 0, 1))
+        summed = (
+            (result[: 2 * page_tokens].astype(jnp.float32) + across.astype(jnp.float32))
+            .astype(jnp.bfloat16)
+            .reshape(2, 2, token_count, width_moe)
+        )
+        here, there = summed[:, 0], summed[:, 1]
+        stays = jnp.where(tile_id == 0, here, there)
+        leaves = jnp.where(tile_id == 0, there, here)
+        step_total = (
+            stays[0].astype(jnp.float32)
+            + shift(leaves[0], moved=(1, 0, 0, 0)).astype(jnp.float32)
+            + shift(stays[1], moved=(0, 0, 1, 0)).astype(jnp.float32)
+            + shift(leaves[1], moved=(1, 0, 1, 0)).astype(jnp.float32)
+        )
+        if step:
+            step_total = shift(
+                step_total.astype(jnp.bfloat16), moved=(0, outer - step, 0, 0)
+            ).astype(jnp.float32)
+        total = total + step_total
+    return total.astype(jnp.bfloat16).reshape(1, row_count // 2, columns // 2, width_moe)
+
+
+def per_device(*arguments):
+    experts_count = lax.axis_size("expert")
+    if lax.axis_size("tile") == 2 and experts_count % 4 == 0 and experts_count == 16:
+        return per_device_near(*arguments)
+    return per_device_slots(*arguments)
+
+
 def solution(mesh):
     placed = (
         P("expert", "tile", None, None),

time: 424 us -> 232 us (0.55)
  waiting for transfers between devices: 169 us -> 43.9 us
  blocking collectives: 141 us -> 65.3 us
  starting transfers between devices: 3.73 us -> 52.8 us
  local copies, waits for them, and re-layouts: 47 us -> 8.59 us
  between operations: 15 us -> 1.15 us
  matrix products: 33.1 us -> 40.5 us
    all_to_all x2 -> x0, blocking collectives: 115 us -> none  [the longest x1 75.3 us: per_device(): lax.all_to_all(partial_out, 'expert', split_axis=0, concat_axis=0, tiled=...]
    all_gather x2 -> x0, waiting for transfers between devices: 93.3 us -> none  [the longest x1 49.1 us: per_device(): lax.all_gather(proj_weight, 'expert', axis=0, tiled=True)]
    unnamed x6 -> x0, waiting for transfers between devices: 71.4 us -> none
    ppermute x0 -> x51, starting transfers between devices: none -> 52.8 us  [near_shift(): return lax.ppermute(values, ('tile', 'expert'), pairs)]
    ppermute x0 -> x51, waiting for transfers between devices: none -> 43.9 us  [near_shift(): return lax.ppermute(values, ('tile', 'expert'), pairs)]
    all_gather x3 -> x1, blocking collectives: 26.7 us -> 65.3 us  [per_device_near(): lax.all_gather(dense_gates, ('expert', 'tile'), axis=0, tiled=True)]
    scatter x2 -> x0, local copies, waits for them, and re-layouts: 19.7 us -> none  [block_slots(): table = jnp.full((experts_count * capacity,), -1, dtype=jnp.int32).at[pic...]
    gather x7 -> x0, local copies, waits for them, and re-layouts: 19.4 us -> none  [the longest x6 16.2 us: per_device(): results_flat[pick_index[:, position]].astype(jnp.float32)]
  transfers between devices with their start and end apart: 6 -> 51, of which waited for: 4 -> 20; matrix products, arithmetic and copies ran while one was open for 13% -> 27% of each run, Pallas kernels for 0% -> 0%
where the time goes in v1:
time: 232 us; the launch traced here: 230 us
  blocking collectives  65.3 us (28%)
  starting transfers between devices  52.8 us (23%)
  waiting for transfers between devices  43.9 us (19%)
  matrix products  40.5 us (17%)
  other arithmetic  17.7 us (8%)
  local copies, waits for them, and re-layouts  8.59 us (4%)
    all_gather x1, blocking collectives, per_device_near(): lax.all_gather(dense_gates, ('expert', 'tile'), axis=0, tiled=True)  65.3 us
    ppermute x51, starting transfers between devices, near_shift(): return lax.ppermute(values, ('tile', 'expert'), pairs)  52.8 us
    ppermute x51, waiting for transfers between devices, near_shift(): return lax.ppermute(values, ('tile', 'expert'), pairs)  43.9 us
    dot_general x4, matrix products, per_device_near(): gated = jnp.dot(moe_in, expert_flat, preferred_element_type=jnp.float32)  10.2 us
    dot_general x2, matrix products, project_qkv(): jnp.dot(normed, qkv_weight.reshape(width_vit, -1), preferred_element_type...  7.04 us
    dot_general x8, matrix products, per_device_near(): jnp.dot(lax.dynamic_index_in_dim(side, window, 0, keepdims=False), weight...  5.63 us
    sub x2, matrix products, attend_rows(): weights = jax.nn.softmax(scores, axis=-1).astype(jnp.bfloat16)  5.19 us
  transfers between devices with their start and end apart: 51, of which 20 were waited for; matrix products, arithmetic and copies ran while one was open for 27% of the time, Pallas kernels for 0%

profile of v1, /device:TPU:0, one launch (start us, length us, event | category | flops | bytes accessed | tf_op | source)
XLA Modules:
  0.0 230.0 jit_solution(4504211025929655885)
XLA Ops:
  0.0 3.0 %collective-permute-start.6 = (bf16[288,1024]{1,0:T(8,128)(2,1)}, bf16[288,1024]{1,0:T(8,128)(2,1)}, u32[]{:S(2)}, u32[]{:S(2)}) collective-permute-start(bf16[288,1024]{1,0:T(8,128)(2,1)} %param.22), channel_id=1, source_target_pairs={{0,4},{1,5},{2,6},{3,7},{4,8},{5,9},{6,10},{7,11},{8,12},{9,13},{1... | collective-permute-start | bytes 1769480 | tf_op jit(solution)/shard_map/ppermute | solution.py:217
  3.0 2.1 collective-permute-start.10
  11.5 3.5 %convolution_add_fusion.3 = f32[128,3,8,72]{0,3,2,1:T(8,128)S(1)} fusion(bf16[128,1152,1,1]{1,0,3,2:T(8,128)(2,1)S(1)} %bitcast.264, bf16[3,8,72,1152]{3,2,1,0:T(8,128)(2,1)} %bitcast.255, f32[3,8,72]{2,1,0:T(8,128)S(1)} %add.620), kind=kOutput, calls=%fused_computation.48 | convolution fusion | flops 509829120 | bytes 5167872 | tf_op jit(solution)/shard_map/dot_general | solution.py:311
  19.1 3.6 %convolution_add_fusion.2 = f32[128,3,8,72]{0,3,2,1:T(8,128)S(1)} fusion(bf16[3,8,72,1152]{3,2,1,0:T(8,128)(2,1)} %bitcast.256, f32[3,8,72]{2,1,0:T(8,128)S(1)} %add.620, bf16[128,1152]{1,0:T(8,128)(2,1)S(1)} %collective-permute-done, f32[1152]{0:T(1024)S(1)} %copy-done.21, f32[128]{0:T(128)S(1)} %add_rsqrt_fusion.6, f32[128]{0:T(128)S(1)} %broadcast_multiply_fusion.2), kind=kOutput, calls=%fused_computation.47 | convolution fusion | flops 510566400 | bytes 5173504 | tf_op jit(solution)/shard_map/dot_general | solution.py:311
  24.3 2.6 %fusion.201 = (f32[8,128]{1,0:T(8,128)S(1)}, f32[8,128,256]{2,1,0:T(8,128)}) fusion(bf16[128,8,18]{0,2,1:T(8,128)(2,1)} %get-tuple-element.71, bf16[128,8,18]{0,2,1:T(8,128)(2,1)} %get-tuple-element.72, bf16[128,8,18]{0,2,1:T(8,128)(2,1)} %get-tuple-element.60, bf16[128,8,18]{0,2,1:T(8,128)(2,1)} %get-tuple-element.59, ...), kind=kOutput, calls=%fused_computation.376 | convolution fusion | flops 41484544 | bytes 1495040 | tf_op jit(solution)/shard_map/sub | solution.py:233
  29.6 2.6 %fusion.204 = (f32[8,128]{1,0:T(8,128)S(1)}, f32[8,128,256]{2,1,0:T(8,128)}) fusion(bf16[128,8,18]{0,2,1:T(8,128)(2,1)} %get-tuple-element.65, bf16[128,8,18]{0,2,1:T(8,128)(2,1)} %get-tuple-element.66, bf16[128,8,18]{0,2,1:T(8,128)(2,1)} %get-tuple-element.48, bf16[128,8,18]{0,2,1:T(8,128)(2,1)S(1)} %get-tuple-element.47, ...), kind=kOutput, calls=%fused_computation.377 | convolution fusion | flops 41484544 | bytes 1495040 | tf_op jit(solution)/shard_map/sub | solution.py:233
  34.1 2.6 %collective-permute-done.1 = bf16[128,1152]{1,0:T(8,128)(2,1)S(1)} collective-permute-done((bf16[128,1152]{1,0:T(8,128)(2,1)S(1)}, bf16[128,1152]{1,0:T(8,128)(2,1)S(1)}, u32[]{:S(2)}, u32[]{:S(2)}) %collective-permute-start.1) | collective-permute-done | bytes 294944 | tf_op jit(solution)/shard_map/ppermute | solution.py:217
  39.5 2.5 %collective-permute-start.4 = (bf16[4,32,576]{2,1,0:T(8,128)(2,1)S(1)}, bf16[4,32,576]{2,1,0:T(8,128)(2,1)S(1)}, u32[]{:S(2)}, u32[]{:S(2)}) collective-permute-start(bf16[4,32,576]{2,1,0:T(8,128)(2,1)S(1)} %bitcast.275), channel_id=1, source_target_pairs={{0,18},{1,19},{2,16},{3,17},{4,22},{5,23},{6,20},{7,21},{8,26},{9,... | collective-permute-start | bytes 442376 | tf_op jit(solution)/shard_map/ppermute | solution.py:217
  42.0 2.6 %collective-permute-done.2 = bf16[4,32,576]{2,1,0:T(8,128)(2,1)S(1)} collective-permute-done((bf16[4,32,576]{2,1,0:T(8,128)(2,1)S(1)}, bf16[4,32,576]{2,1,0:T(8,128)(2,1)S(1)}, u32[]{:S(2)}, u32[]{:S(2)}) %collective-permute-start.2) | collective-permute-done | bytes 147488 | tf_op jit(solution)/shard_map/ppermute | solution.py:217
  46.8 9.8 %collective-permute-done.8 = bf16[288,1024]{1,0:T(8,128)(2,1)} collective-permute-done((bf16[288,1024]{1,0:T(8,128)(2,1)}, bf16[288,1024]{1,0:T(8,128)(2,1)}, u32[]{:S(2)}, u32[]{:S(2)}) %collective-permute-start.8) | collective-permute-done | bytes 589856 | tf_op jit(solution)/shard_map/ppermute | solution.py:217
  65.4 3.4 %collective-permute-done.12 = bf16[64,1024]{1,0:T(8,128)(2,1)} collective-permute-done((bf16[64,1024]{1,0:T(8,128)(2,1)S(1)}, bf16[64,1024]{1,0:T(8,128)(2,1)}, u32[]{:S(2)}, u32[]{:S(2)}) %collective-permute-start.12) | collective-permute-done | bytes 131104 | tf_op jit(solution)/shard_map/ppermute | solution.py:217
  71.4 2.4 %collective-permute-start.15 = (bf16[64,1024]{1,0:T(8,128)(2,1)S(1)}, bf16[64,1024]{1,0:T(8,128)(2,1)S(1)}, u32[]{:S(2)}, u32[]{:S(2)}) collective-permute-start(bf16[64,1024]{1,0:T(8,128)(2,1)S(1)} %fusion.91), channel_id=1, source_target_pairs={{0,18},{1,19},{2,16},{3,17},{4,22},{5,23},{6,20},{7,21},{8,26},{9,... | collective-permute-start | bytes 393224 | tf_op jit(solution)/shard_map/ppermute | solution.py:217
  73.9 65.3 %all-gather = f32[32,32,16]{1,2,0:T(8,128)S(1)} all-gather(f32[1,32,16]{1,2,0:T(8,128)S(1)} %bitcast.279), channel_id=1, replica_groups=mesh['tile'=2,'expert'=16] {'expert','tile'}, dimensions={0}, use_global_device_ids=true | all-gather | bytes 67584 | tf_op jit(solution)/shard_map/all_gather | solution.py:298
  139.4 2.3 %collective-permute-start.14 = (bf16[64,1024]{1,0:T(8,128)(2,1)S(1)}, bf16[64,1024]{1,0:T(8,128)(2,1)S(1)}, u32[]{:S(2)}, u32[]{:S(2)}) collective-permute-start(bf16[64,1024]{1,0:T(8,128)(2,1)S(1)} %fusion.91), channel_id=1, source_target_pairs={{0,16},{1,17},{2,18},{3,19},{4,20},{5,21},{6,22},{7,23},{8,24},{9,... | collective-permute-start | bytes 393224 | tf_op jit(solution)/shard_map/ppermute | solution.py:217
  145.6 2.5 %collective-permute-start.43 = (bf16[64,1024]{1,0:T(8,128)(2,1)}, bf16[64,1024]{1,0:T(8,128)(2,1)}, u32[]{:S(2)}, u32[]{:S(2)}) collective-permute-start(bf16[64,1024]{1,0:T(8,128)(2,1)} %collective-permute-done.41), channel_id=1, source_target_pairs={{0,16},{1,17},{2,18},{3,19},{4,20},{5,21},{6,22},{7,23},{8,24},{9,... | collective-permute-start | bytes 393224 | tf_op jit(solution)/shard_map/ppermute | solution.py:217
  156.5 3.2 %collective-permute-done.42 = bf16[64,1024]{1,0:T(8,128)(2,1)} collective-permute-done((bf16[64,1024]{1,0:T(8,128)(2,1)}, bf16[64,1024]{1,0:T(8,128)(2,1)}, u32[]{:S(2)}, u32[]{:S(2)}) %collective-permute-start.42) | collective-permute-done | bytes 131104 | tf_op jit(solution)/shard_map/ppermute | solution.py:217
  168.7 4.5 %fusion.209 = f32[256,1408]{1,0:T(8,128)S(1)} fusion(bf16[256,2048]{1,0:T(8,128)(2,1)S(1)} %fusion.34, bf16[2048,1408]{0,1:T(8,128)(2,1)} %bitcast.281), kind=kOutput, calls=%fused_computation.380 | convolution fusion | flops 1476395008 | bytes 8257536 | tf_op jit(solution)/shard_map/dot_general | solution.py:387
  185.5 2.1 fusion.52
  198.9 3.1 %collective-permute-done.48 = bf16[32,2048]{1,0:T(8,128)(2,1)S(1)} collective-permute-done((bf16[32,2048]{1,0:T(8,128)(2,1)S(1)}, bf16[32,2048]{1,0:T(8,128)(2,1)S(1)}, u32[]{:S(2)}, u32[]{:S(2)}) %collective-permute-start.48) | collective-permute-done | bytes 131104 | tf_op jit(solution)/shard_map/ppermute | solution.py:217
  204.2 2.4 %collective-permute-done.49 = bf16[32,2048]{1,0:T(8,128)(2,1)S(1)} collective-permute-done((bf16[32,2048]{1,0:T(8,128)(2,1)S(1)}, bf16[32,2048]{1,0:T(8,128)(2,1)S(1)}, u32[]{:S(2)}, u32[]{:S(2)}) %collective-permute-start.49) | collective-permute-done | bytes 131104 | tf_op jit(solution)/shard_map/ppermute | solution.py:217
  210.2 2.3 %collective-permute-done.39 = bf16[32,2048]{1,0:T(8,128)(2,1)S(1)} collective-permute-done((bf16[32,2048]{1,0:T(8,128)(2,1)S(1)}, bf16[32,2048]{1,0:T(8,128)(2,1)S(1)}, u32[]{:S(2)}, u32[]{:S(2)}) %collective-permute-start.39) | collective-permute-done | bytes 131104 | tf_op jit(solution)/shard_map/ppermute | solution.py:217
  213.4 2.9 %collective-permute-done.28 = bf16[32,2048]{1,0:T(8,128)(2,1)S(1)} collective-permute-done((bf16[32,2048]{1,0:T(8,128)(2,1)S(1)}, bf16[32,2048]{1,0:T(8,128)(2,1)S(1)}, u32[]{:S(2)}, u32[]{:S(2)}) %collective-permute-start.28) | collective-permute-done | bytes 131104 | tf_op jit(solution)/shard_map/ppermute | solution.py:217
  220.0 2.9 %collective-permute-start.30 = (bf16[32,2048]{1,0:T(8,128)(2,1)S(1)}, bf16[32,2048]{1,0:T(8,128)(2,1)S(1)}, u32[]{:S(2)}, u32[]{:S(2)}) collective-permute-start(bf16[32,2048]{1,0:T(8,128)(2,1)S(1)} %fusion.100), channel_id=1, source_target_pairs={{0,12},{1,13},{2,14},{3,15},{4,0},{5,1},{6,2},{7,3},{8,4},{9,5},{1... | collective-permute-start | bytes 393224 | tf_op jit(solution)/shard_map/ppermute | solution.py:217
  224.6 4.6 %collective-permute-done.40 = bf16[32,2048]{1,0:T(8,128)(2,1)S(1)} collective-permute-done((bf16[32,2048]{1,0:T(8,128)(2,1)S(1)}, bf16[32,2048]{1,0:T(8,128)(2,1)S(1)}, u32[]{:S(2)}, u32[]{:S(2)}) %collective-permute-start.40) | collective-permute-done | bytes 131104 | tf_op jit(solution)/shard_map/ppermute | solution.py:217
  (265 shorter events, 90.1 us)
Async XLA Ops:
  0.0 46.2 %collective-permute-start.6 = (bf16[288,1024]{1,0:T(8,128)(2,1)}, bf16[288,1024]{1,0:T(8,128)(2,1)}, u32[]{:S(2)}, u32[]{:S(2)}) collective-permute-start(bf16[288,1024]{1,0:T(8,128)(2,1)} %param.22), channel_id=1, source_target_pairs={{0,4},{1,5},{2,6},{3,7},{4,8},{5,9},{6,10},{7,11},{8,12},{9,13},{1... | collective-permute-start | bytes 1769480 | tf_op jit(solution)/shard_map/ppermute | solution.py:217
  3.0 43.3 %collective-permute-start.10 = (bf16[288,1024]{1,0:T(8,128)(2,1)}, bf16[288,1024]{1,0:T(8,128)(2,1)}, u32[]{:S(2)}, u32[]{:S(2)}) collective-permute-start(bf16[288,1024]{1,0:T(8,128)(2,1)} %param.22), channel_id=1, source_target_pairs={{0,12},{1,13},{2,14},{3,15},{4,0},{5,1},{6,2},{7,3},{8,4},{9,5},{1... | collective-permute-start | bytes 1769480 | tf_op jit(solution)/shard_map/ppermute | solution.py:217
  5.1 51.5 %collective-permute-start.8 = (bf16[288,1024]{1,0:T(8,128)(2,1)}, bf16[288,1024]{1,0:T(8,128)(2,1)}, u32[]{:S(2)}, u32[]{:S(2)}) collective-permute-start(bf16[288,1024]{1,0:T(8,128)(2,1)} %param.22), channel_id=1, source_target_pairs={{0,8},{1,9},{2,10},{3,11},{4,12},{5,13},{6,14},{7,15},{8,0},{9,1},... | collective-permute-start | bytes 1769480 | tf_op jit(solution)/shard_map/ppermute | solution.py:217
  7.9 10.8 %collective-permute-start = (bf16[128,1152]{1,0:T(8,128)(2,1)}, bf16[128,1152]{1,0:T(8,128)(2,1)S(1)}, u32[]{:S(2)}, u32[]{:S(2)}) collective-permute-start(bf16[128,1152]{1,0:T(8,128)(2,1)} %bitcast.1), channel_id=1, source_target_pairs={{0,16},{1,17},{2,18},{3,19},{4,20},{5,21},{6,22},{7,23},{8,24},{9,... | collective-permute-start | bytes 884744 | tf_op jit(solution)/shard_map/ppermute | solution.py:217
  39.5 17.1 %collective-permute-start.4 = (bf16[4,32,576]{2,1,0:T(8,128)(2,1)S(1)}, bf16[4,32,576]{2,1,0:T(8,128)(2,1)S(1)}, u32[]{:S(2)}, u32[]{:S(2)}) collective-permute-start(bf16[4,32,576]{2,1,0:T(8,128)(2,1)S(1)} %bitcast.275), channel_id=1, source_target_pairs={{0,18},{1,19},{2,16},{3,17},{4,22},{5,23},{6,20},{7,21},{8,26},{9,... | collective-permute-start | bytes 442376 | tf_op jit(solution)/shard_map/ppermute | solution.py:217
  44.6 12.5 %collective-permute-start.3 = (bf16[4,32,576]{2,1,0:T(8,128)(2,1)S(1)}, bf16[4,32,576]{2,1,0:T(8,128)(2,1)S(1)}, u32[]{:S(2)}, u32[]{:S(2)}) collective-permute-start(bf16[4,32,576]{2,1,0:T(8,128)(2,1)S(1)} %bitcast.276), channel_id=1, source_target_pairs={{0,2},{1,3},{2,0},{3,1},{4,6},{5,7},{6,4},{7,5},{8,10},{9,11},{10,... | collective-permute-start | bytes 442376 | tf_op jit(solution)/shard_map/ppermute | solution.py:217
  46.2 11.5 %collective-permute-start.5 = (bf16[288,1024]{1,0:T(8,128)(2,1)}, bf16[288,1024]{1,0:T(8,128)(2,1)S(1)}, u32[]{:S(2)}, u32[]{:S(2)}) collective-permute-start(bf16[288,1024]{1,0:T(8,128)(2,1)} %param.22), channel_id=1, source_target_pairs={{0,1},{1,0},{2,3},{3,2},{4,5},{5,4},{6,7},{7,6},{8,9},{9,8},{10,11... | collective-permute-start | bytes 1769480 | tf_op jit(solution)/shard_map/ppermute | solution.py:217
  46.3 15.9 %collective-permute-start.7 = (bf16[288,1024]{1,0:T(8,128)(2,1)}, bf16[288,1024]{1,0:T(8,128)(2,1)S(1)}, u32[]{:S(2)}, u32[]{:S(2)}) collective-permute-start(bf16[288,1024]{1,0:T(8,128)(2,1)} %collective-permute-done.6), channel_id=1, source_target_pairs={{0,1},{1,0},{2,3},{3,2},{4,5},{5,4},{6,7},{7,6},{8,9},{9,8},{10,11... | collective-permute-start | bytes 1769480 | tf_op jit(solution)/shard_map/ppermute | solution.py:217
  69.7 73.0 %collective-permute-start.41 = (bf16[64,1024]{1,0:T(8,128)(2,1)S(1)}, bf16[64,1024]{1,0:T(8,128)(2,1)}, u32[]{:S(2)}, u32[]{:S(2)}) collective-permute-start(bf16[64,1024]{1,0:T(8,128)(2,1)S(1)} %fusion.91), channel_id=1, source_target_pairs={{0,12},{1,13},{2,14},{3,15},{4,0},{5,1},{6,2},{7,3},{8,4},{9,5},{1... | collective-permute-start | bytes 393224 | tf_op jit(solution)/shard_map/ppermute | solution.py:217
  71.4 71.6 %collective-permute-start.15 = (bf16[64,1024]{1,0:T(8,128)(2,1)S(1)}, bf16[64,1024]{1,0:T(8,128)(2,1)S(1)}, u32[]{:S(2)}, u32[]{:S(2)}) collective-permute-start(bf16[64,1024]{1,0:T(8,128)(2,1)S(1)} %fusion.91), channel_id=1, source_target_pairs={{0,18},{1,19},{2,16},{3,17},{4,22},{5,23},{6,20},{7,21},{8,26},{9,... | collective-permute-start | bytes 393224 | tf_op jit(solution)/shard_map/ppermute | solution.py:217
  142.8 9.4 %collective-permute-start.21 = (bf16[64,1024]{1,0:T(8,128)(2,1)S(1)}, bf16[64,1024]{1,0:T(8,128)(2,1)S(1)}, u32[]{:S(2)}, u32[]{:S(2)}) collective-permute-start(bf16[64,1024]{1,0:T(8,128)(2,1)S(1)} %fusion.91), channel_id=1, source_target_pairs={{0,4},{1,5},{2,6},{3,7},{4,8},{5,9},{6,10},{7,11},{8,12},{9,13},{1... | collective-permute-start | bytes 393224 | tf_op jit(solution)/shard_map/ppermute | solution.py:217
  143.0 9.8 %collective-permute-start.44 = (bf16[64,1024]{1,0:T(8,128)(2,1)}, bf16[64,1024]{1,0:T(8,128)(2,1)}, u32[]{:S(2)}, u32[]{:S(2)}) collective-permute-start(bf16[64,1024]{1,0:T(8,128)(2,1)} %collective-permute-done.41), channel_id=1, source_target_pairs={{0,18},{1,19},{2,16},{3,17},{4,22},{5,23},{6,20},{7,21},{8,26},{9,... | collective-permute-start | bytes 393224 | tf_op jit(solution)/shard_map/ppermute | solution.py:217
  149.9 17.8 %collective-permute-start.16 = (bf16[4,64,1024]{2,1,0:T(8,128)(2,1)}, bf16[4,64,1024]{2,1,0:T(8,128)(2,1)S(1)}, u32[]{:S(2)}, u32[]{:S(2)}) collective-permute-start(bf16[4,64,1024]{2,1,0:T(8,128)(2,1)} %pad_maximum_fusion.9), channel_id=1, source_target_pairs={{0,1},{1,0},{2,3},{3,2},{4,5},{5,4},{6,7},{7,6},{8,9},{9,8},{10,11... | collective-permute-start | bytes 1572872 | tf_op jit(solution)/shard_map/ppermute | solution.py:217
  150.2 9.5 %collective-permute-start.42 = (bf16[64,1024]{1,0:T(8,128)(2,1)}, bf16[64,1024]{1,0:T(8,128)(2,1)}, u32[]{:S(2)}, u32[]{:S(2)}) collective-permute-start(bf16[64,1024]{1,0:T(8,128)(2,1)} %collective-permute-done.41), channel_id=1, source_target_pairs={{0,2},{1,3},{2,0},{3,1},{4,6},{5,7},{6,4},{7,5},{8,10},{9,11},{10,... | collective-permute-start | bytes 393224 | tf_op jit(solution)/shard_map/ppermute | solution.py:217
  152.8 9.6 %collective-permute-start.33 = (bf16[64,1024]{1,0:T(8,128)(2,1)}, bf16[64,1024]{1,0:T(8,128)(2,1)}, u32[]{:S(2)}, u32[]{:S(2)}) collective-permute-start(bf16[64,1024]{1,0:T(8,128)(2,1)} %collective-permute-done.31), channel_id=1, source_target_pairs={{0,16},{1,17},{2,18},{3,19},{4,20},{5,21},{6,22},{7,23},{8,24},{9,... | collective-permute-start | bytes 393224 | tf_op jit(solution)/shard_map/ppermute | solution.py:217
  154.4 9.9 %collective-permute-start.32 = (bf16[64,1024]{1,0:T(8,128)(2,1)}, bf16[64,1024]{1,0:T(8,128)(2,1)}, u32[]{:S(2)}, u32[]{:S(2)}) collective-permute-start(bf16[64,1024]{1,0:T(8,128)(2,1)} %collective-permute-done.31), channel_id=1, source_target_pairs={{0,2},{1,3},{2,0},{3,1},{4,6},{5,7},{6,4},{7,5},{8,10},{9,11},{10,... | collective-permute-start | bytes 393224 | tf_op jit(solution)/shard_map/ppermute | solution.py:217
  164.4 14.6 %collective-permute-start.45 = (bf16[4,64,1024]{2,1,0:T(8,128)(2,1)S(1)}, bf16[4,64,1024]{2,1,0:T(8,128)(2,1)S(1)}, u32[]{:S(2)}, u32[]{:S(2)}) collective-permute-start(bf16[4,64,1024]{2,1,0:T(8,128)(2,1)S(1)} %pad_maximum_fusion.18), channel_id=1, source_target_pairs={{0,1},{1,0},{2,3},{3,2},{4,5},{5,4},{6,7},{7,6},{8,9},{9,8},{10,11... | collective-permute-start | bytes 1572872 | tf_op jit(solution)/shard_map/ppermute | solution.py:217
  165.8 18.0 %collective-permute-start.35 = (bf16[4,64,1024]{2,1,0:T(8,128)(2,1)S(1)}, bf16[4,64,1024]{2,1,0:T(8,128)(2,1)S(1)}, u32[]{:S(2)}, u32[]{:S(2)}) collective-permute-start(bf16[4,64,1024]{2,1,0:T(8,128)(2,1)S(1)} %pad_maximum_fusion.15), channel_id=1, source_target_pairs={{0,1},{1,0},{2,3},{3,2},{4,5},{5,4},{6,7},{7,6},{8,9},{9,8},{10,11... | collective-permute-start | bytes 1572872 | tf_op jit(solution)/shard_map/ppermute | solution.py:217
  167.6 21.7 %collective-permute-start.25 = (bf16[4,64,1024]{2,1,0:T(8,128)(2,1)S(1)}, bf16[4,64,1024]{2,1,0:T(8,128)(2,1)S(1)}, u32[]{:S(2)}, u32[]{:S(2)}) collective-permute-start(bf16[4,64,1024]{2,1,0:T(8,128)(2,1)S(1)} %pad_maximum_fusion.12), channel_id=1, source_target_pairs={{0,1},{1,0},{2,3},{3,2},{4,5},{5,4},{6,7},{7,6},{8,9},{9,8},{10,11... | collective-permute-start | bytes 1572872 | tf_op jit(solution)/shard_map/ppermute | solution.py:217
  177.7 15.3 %collective-permute-start.17 = (bf16[128,2048]{1,0:T(8,128)(2,1)S(1)}, bf16[128,2048]{1,0:T(8,128)(2,1)S(1)}, u32[]{:S(2)}, u32[]{:S(2)}) collective-permute-start(bf16[128,2048]{1,0:T(8,128)(2,1)S(1)} %slice.423), channel_id=1, source_target_pairs={{0,1},{1,0},{2,3},{3,2},{4,5},{5,4},{6,7},{7,6},{8,9},{9,8},{10,11... | collective-permute-start | bytes 1572872 | tf_op jit(solution)/shard_map/ppermute | solution.py:217
  183.7 10.8 %collective-permute-start.46 = (bf16[128,2048]{1,0:T(8,128)(2,1)S(1)}, bf16[128,2048]{1,0:T(8,128)(2,1)S(1)}, u32[]{:S(2)}, u32[]{:S(2)}) collective-permute-start(bf16[128,2048]{1,0:T(8,128)(2,1)S(1)} %slice.465), channel_id=1, source_target_pairs={{0,1},{1,0},{2,3},{3,2},{4,5},{5,4},{6,7},{7,6},{8,9},{9,8},{10,11... | collective-permute-start | bytes 1572872 | tf_op jit(solution)/shard_map/ppermute | solution.py:217
  193.2 26.7 %collective-permute-start.19 = (bf16[32,2048]{1,0:T(8,128)(2,1)S(1)}, bf16[32,2048]{1,0:T(8,128)(2,1)S(1)}, u32[]{:S(2)}, u32[]{:S(2)}) collective-permute-start(bf16[32,2048]{1,0:T(8,128)(2,1)S(1)} %slice_bitcast_fusion.29), channel_id=1, source_target_pairs={{0,2},{1,3},{2,0},{3,1},{4,6},{5,7},{6,4},{7,5},{8,10},{9,11},{10,... | collective-permute-start | bytes 393224 | tf_op jit(solution)/shard_map/ppermute | solution.py:217
  194.3 28.6 %collective-permute-start.18 = (bf16[32,2048]{1,0:T(8,128)(2,1)S(1)}, bf16[32,2048]{1,0:T(8,128)(2,1)S(1)}, u32[]{:S(2)}, u32[]{:S(2)}) collective-permute-start(bf16[32,2048]{1,0:T(8,128)(2,1)S(1)} %get-tuple-element.73), channel_id=1, source_target_pairs={{0,16},{1,17},{2,18},{3,19},{4,20},{5,21},{6,22},{7,23},{8,24},{9,... | collective-permute-start | bytes 393224 | tf_op jit(solution)/shard_map/ppermute | solution.py:217
  218.4 10.7 %collective-permute-start.40 = (bf16[32,2048]{1,0:T(8,128)(2,1)S(1)}, bf16[32,2048]{1,0:T(8,128)(2,1)S(1)}, u32[]{:S(2)}, u32[]{:S(2)}) collective-permute-start(bf16[32,2048]{1,0:T(8,128)(2,1)S(1)} %fusion.97), channel_id=1, source_target_pairs={{0,8},{1,9},{2,10},{3,11},{4,12},{5,13},{6,14},{7,15},{8,0},{9,1},... | collective-permute-start | bytes 393224 | tf_op jit(solution)/shard_map/ppermute | solution.py:217
  (58 other events, 482.1 us)

commit v2 on v1

--- a/solution.py
+++ b/solution.py
@@ -4,6 +4,8 @@
 import jax
 import jax.numpy as jnp
 from jax import lax
+from jax.experimental import pallas as pl
+from jax.experimental.pallas import tpu as pltpu
 from jax.sharding import PartitionSpec as P
 
 HD = 72
@@ -202,17 +204,16 @@
     return output.astype(jnp.bfloat16).reshape(1, row_count // 2, columns // 2, width_moe)
 
 
-def near_shift(values, grid, moved):
-    tiles, outer, inner, cores = grid
+def near_swap(values, grid, flips):
     pairs = []
-    for source in range(tiles * outer * inner * cores):
+    for source in range(math.prod(grid)):
         place, rest = [], source
         for size in reversed(grid):
             place.append(rest % size)
             rest //= size
         target = 0
-        for spot, size, step in zip(reversed(place), grid, moved):
-            target = target * size + (spot + step) % size
+        for spot, size, flip in zip(reversed(place), grid, flips):
+            target = target * size + (spot ^ flip)
         pairs.append((source, target))
     return lax.ppermute(values, ("tile", "expert"), pairs)
 
@@ -236,6 +237,170 @@
         .astype(jnp.bfloat16)
         .reshape(query_rows.shape[0], -1)
     )
+
+
+def unit_pieces(units):
+    cuts = list(range(0, units, 256)) + [units]
+    return list(zip(cuts[:-1], cuts[1:]))
+
+
+def fetch_units(pieces, sources, targets, arrivals):
+    copies = []
+    for number, (begin, end) in enumerate(pieces):
+        rows = pl.ds(begin, end - begin)
+        copies.append(
+            [
+                pltpu.make_async_copy(
+                    source.at[rows], target.at[rows], arrivals.at[number, which]
+                )
+                for which, (source, target) in enumerate(zip(sources, targets))
+            ]
+        )
+    for piece in copies:
+        for copy in piece:
+            copy.start()
+    return copies
+
+
+def expert_sums(pieces, copies, normed, gate_rows, up_rows, back_rows):
+    total = None
+    for (begin, end), piece in zip(pieces, copies):
+        for copy in piece:
+            copy.wait()
+        rows = pl.ds(begin, end - begin)
+        wide = (((1,), (1,)), ((), ()))
+        gate = lax.dot_general(normed, gate_rows[rows], wide, preferred_element_type=jnp.float32)
+        up = lax.dot_general(normed, up_rows[rows], wide, preferred_element_type=jnp.float32)
+        hidden = (gate / (1.0 + jnp.exp(-gate)) * up).astype(jnp.bfloat16)
+        part = jnp.dot(hidden, back_rows[rows], preferred_element_type=jnp.float32)
+        total = part if total is None else total + part
+    return total
+
+
+def norm_pages(place_ref, page_refs, gain_ref, lanes_ref, normed, weights):
+    half = normed.shape[1] // 2
+    first = pl.multiple_of(place_ref[0] * half, half)
+    second = pl.multiple_of((1 - place_ref[0]) * half, half)
+    for number, (mine_ref, other_ref) in enumerate(page_refs):
+        mine = mine_ref[:, :half].astype(jnp.float32)
+        other = other_ref[:, :half].astype(jnp.float32)
+        squares = jnp.sum(mine * mine, axis=1, keepdims=True) + jnp.sum(
+            other * other, axis=1, keepdims=True
+        )
+        scale = lax.rsqrt(squares / (2 * half) + norm_eps)
+        count = mine.shape[0]
+        rows = pl.ds(number * count, count)
+        normed[rows, pl.ds(first, half)] = (mine * scale * gain_ref[:, pl.ds(first, half)]).astype(
+            jnp.bfloat16
+        )
+        normed[rows, pl.ds(second, half)] = (
+            other * scale * gain_ref[:, pl.ds(second, half)]
+        ).astype(jnp.bfloat16)
+        if weights is not None:
+            lanes = mine_ref[:, half:].astype(jnp.float32) + other_ref[:, half:].astype(jnp.float32)
+            weights[rows] = jnp.sum(lanes * lanes_ref[...], axis=1, keepdims=True)
+
+
+def expert_kernel(pieces, extra, *refs):
+    place_ref, near_ref, across_ref, gain_ref, lanes_ref, gate_hbm, up_hbm, back_hbm = refs[:8]
+    extra_ref = refs[8] if extra else None
+    own_out, across_out, normed, weights, gate_rows, up_rows, back_rows, arrivals = refs[8 + extra :]
+    copies = fetch_units(
+        pieces, (gate_hbm, up_hbm, back_hbm), (gate_rows, up_rows, back_rows), arrivals
+    )
+    page_refs = [
+        (ref.at[inner, 0], ref.at[inner, 1]) for ref in (near_ref, across_ref) for inner in range(2)
+    ]
+    norm_pages(place_ref, page_refs, gain_ref, lanes_ref, normed, weights)
+    total = expert_sums(pieces, copies, normed[...], gate_rows, up_rows, back_rows)
+    total = total * weights[...]
+    count = total.shape[0] // 4
+    for page in range(4):
+        rows = total[page * count : (page + 1) * count]
+        if extra and page == 0:
+            rows = rows + extra_ref[...]
+        target = own_out if page < 2 else across_out
+        target[page % 2] = rows.astype(jnp.bfloat16)
+
+
+def shared_kernel(pieces, *refs):
+    place_ref, mine_ref, other_ref, gain_ref, gate_hbm, up_hbm, back_hbm = refs[:7]
+    out_ref, normed, gate_rows, up_rows, back_rows, arrivals = refs[7:]
+    copies = fetch_units(
+        pieces, (gate_hbm, up_hbm, back_hbm), (gate_rows, up_rows, back_rows), arrivals
+    )
+    norm_pages(place_ref, [(mine_ref, other_ref)], gain_ref, None, normed, None)
+    out_ref[...] = expert_sums(pieces, copies, normed[...], gate_rows, up_rows, back_rows)
+
+
+vmem_spec = pl.BlockSpec(memory_space=pltpu.VMEM)
+smem_spec = pl.BlockSpec(memory_space=pltpu.SMEM)
+any_spec = pl.BlockSpec(memory_space=pl.ANY)
+
+
+def expert_cost(rows, units, width):
+    return pl.CostEstimate(
+        flops=6 * rows * units * width,
+        bytes_accessed=6 * units * width + 4 * rows * width,
+        transcendentals=rows * units,
+    )
+
+
+def run_expert(tile_place, near, across, gain, lanes, gate_rows, up_rows, back_rows, extra):
+    units, width = back_rows.shape
+    page_rows = near.shape[2]
+    rows = 4 * page_rows
+    pieces = unit_pieces(units)
+    out = jax.ShapeDtypeStruct((2, page_rows, width), jnp.bfloat16)
+    return pl.pallas_call(
+        partial(expert_kernel, pieces, extra is not None),
+        out_shape=(out, out),
+        in_specs=[smem_spec] + [vmem_spec] * 4 + [any_spec] * 3 + [vmem_spec] * (extra is not None),
+        out_specs=(vmem_spec, vmem_spec),
+        scratch_shapes=[
+            pltpu.VMEM((rows, width), jnp.bfloat16),
+            pltpu.VMEM((rows, 1), jnp.float32),
+            pltpu.VMEM((units, width), jnp.bfloat16),
+            pltpu.VMEM((units, width), jnp.bfloat16),
+            pltpu.VMEM((units, width), jnp.bfloat16),
+            pltpu.SemaphoreType.DMA((len(pieces), 3)),
+        ],
+        compiler_params=pltpu.CompilerParams(vmem_limit_bytes=40 * 2**20),
+        cost_estimate=expert_cost(rows, units, width),
+        name="expert_units",
+    )(
+        tile_place,
+        near,
+        across,
+        gain,
+        lanes,
+        gate_rows,
+        up_rows,
+        back_rows,
+        *(() if extra is None else (extra,)),
+    )
+
+
+def run_shared(tile_place, mine, other, gain, gate_rows, up_rows, back_rows):
+    units, width = back_rows.shape
+    rows = mine.shape[0]
+    pieces = unit_pieces(units)
+    return pl.pallas_call(
+        partial(shared_kernel, pieces),
+        out_shape=jax.ShapeDtypeStruct((rows, width), jnp.float32),
+        in_specs=[smem_spec] + [vmem_spec] * 3 + [any_spec] * 3,
+        out_specs=vmem_spec,
+        scratch_shapes=[
+            pltpu.VMEM((rows, width), jnp.bfloat16),
+            pltpu.VMEM((units, width), jnp.bfloat16),
+            pltpu.VMEM((units, width), jnp.bfloat16),
+            pltpu.VMEM((units, width), jnp.bfloat16),
+            pltpu.SemaphoreType.DMA((len(pieces), 3)),
+        ],
+        compiler_params=pltpu.CompilerParams(vmem_limit_bytes=40 * 2**20),
+        cost_estimate=expert_cost(rows, units, width),
+        name="shared_units",
+    )(tile_place, mine, other, gain, gate_rows, up_rows, back_rows)
 
 
 def per_device_near(
@@ -257,8 +422,7 @@
 ):
     experts_count = lax.axis_size("expert")
     outer = experts_count // 4
-    grid = (2, outer, 2, 2)
-    shift = partial(near_shift, grid=grid)
+    swap = partial(near_swap, grid=(2, outer, 2, 2))
     tile_id = lax.axis_index("tile")
     expert_id = lax.axis_index("expert")
     outer_id, inner_id, core_id = expert_id // 4, (expert_id // 2) % 2, expert_id % 2
@@ -267,8 +431,8 @@
     token_count = local_rows // 4
     heads_here = qkv_weight.shape[2] // HD
 
-    def by_tile(mine, other):
-        first = tile_id == 0
+    def by_place(place, mine, other):
+        first = place == 0
         return jnp.where(first, mine, other), jnp.where(first, other, mine)
 
     own_patches = (
@@ -276,12 +440,22 @@
         .transpose(1, 3, 0, 2, 4)
         .reshape(local_rows, width_vit)
     )
-    other_patches = shift(own_patches, moved=(1, 0, 0, 0))
-
-    proj_rows = [proj_weight] + [
-        shift(proj_weight, moved=(0, step, 0, 0)) for step in range(1, outer)
-    ]
-    proj_pairs = [(rows, shift(rows, moved=(0, 0, 0, 1))) for rows in proj_rows]
+    other_patches = swap(own_patches, flips=(1, 0, 0, 0))
+
+    shard_rows = proj_weight.shape[0]
+    proj_half = jnp.zeros((outer * 2 * shard_rows, proj_weight.shape[1]), proj_weight.dtype)
+    for low in range(outer // 2):
+        for inner in range(2):
+            rows = swap(proj_weight, flips=(0, low, inner, 0)) if low or inner else proj_weight
+            for core, block in enumerate((rows, swap(rows, flips=(0, 0, 0, 1)))):
+                spot = (
+                    ((outer_id ^ low) % (outer // 2)) * 4
+                    + (inner_id ^ inner) * 2
+                    + (core_id ^ core)
+                )
+                proj_half = lax.dynamic_update_slice_in_dim(
+                    proj_half, block, spot * shard_rows, axis=0
+                )
 
     top_count = routes.shape[-1]
     page_routes = routes.reshape(2, token_count, top_count)
@@ -295,10 +469,15 @@
         ),
         axis=1,
     )
-    all_gates = lax.all_gather(dense_gates, ("expert", "tile"), axis=0, tiled=True)
-    expert_gates = jnp.sum(
-        jnp.where(jnp.arange(experts_count)[None, :] == expert_id, all_gates, 0.0), axis=1
-    ).reshape(experts_count, 2 * token_count)
+    gates_high = lax.reduce_precision(dense_gates, 8, 7)
+    gate_lanes = jnp.concatenate([gates_high, dense_gates - gates_high], axis=1)
+    gate_width = gate_lanes.shape[1]
+    gate_lanes = jnp.pad(gate_lanes, ((0, 0), (0, 128 - gate_width))).astype(jnp.bfloat16)
+    gate_rows = jnp.concatenate(
+        by_place(tile_id, gate_lanes, jnp.zeros_like(gate_lanes)), axis=0
+    )
+    expert_lanes = jnp.arange(128) % experts_count == expert_id
+    expert_lanes = (expert_lanes & (jnp.arange(128) < gate_width)).astype(jnp.float32)
 
     place = jnp.arange(local_rows)
     pair_size = token_count
@@ -327,7 +506,7 @@
         out_weight,
         preferred_element_type=jnp.float32,
     ).astype(jnp.bfloat16)
-    arrived_part = shift(other_part, moved=(1, 0, 0, 0))
+    arrived_part = swap(other_part, flips=(1, 0, 0, 0))
     own_part = jnp.dot(
         attend_rows(own_query, keys, values, math.sqrt(HD)),
         out_weight,
@@ -338,109 +517,96 @@
     )
     normed_out = layer_norm(hidden, norm2_gain).astype(jnp.bfloat16)
 
-    half = width_vit // 2
-    low_half, high_half = normed_out[:, :half], normed_out[:, half:]
-    kept = jnp.where(inner_id == 0, low_half, high_half).reshape(4, token_count, half)
-    given = jnp.where(inner_id == 0, high_half, low_half).reshape(4, token_count, half)
-    from_tile = shift(kept, moved=(1, 0, 0, 0))
-    from_inner = shift(given, moved=(0, 0, 1, 0))
-    from_both = shift(given, moved=(1, 0, 1, 0))
-    features = jnp.concatenate(
-        [*by_tile(kept, from_tile), *by_tile(from_inner, from_both)], axis=1
-    )
-    quarter = half // 2
-    low_quarter, high_quarter = features[:, :, :quarter], features[:, :, quarter:]
-    own_quarter = jnp.where(core_id == 0, low_quarter, high_quarter)
-    other_quarter = jnp.where(core_id == 0, high_quarter, low_quarter)
-    projected = 0.0
-    for step, (own_rows, core_rows) in enumerate(proj_pairs):
-        window = (outer_id - step) % outer
-        for side, weight in ((own_quarter, own_rows), (other_quarter, core_rows)):
-            projected = projected + jnp.dot(
-                lax.dynamic_index_in_dim(side, window, 0, keepdims=False),
-                weight,
-                preferred_element_type=jnp.float32,
+    far = outer // 2
+    parity_half = local_rows // 2
+    first, second = normed_out[:parity_half], normed_out[parity_half:]
+    upper = outer_id // far
+    kept, given = by_place(upper, first, second)
+    from_far = swap(given, flips=(0, far, 0, 0))
+    from_both = swap(given, flips=(1, far, 0, 0))
+    from_tile = swap(kept, flips=(1, 0, 0, 0))
+    page_tokens = 2 * token_count
+
+    def project(mine, other):
+        features = jnp.concatenate(by_place(tile_id, mine, other), axis=0).reshape(
+            2, 2, token_count, width_vit
+        )
+        features = jnp.concatenate([features[:, 0], features[:, 1]], axis=-1)
+        return jnp.dot(
+            features.reshape(page_tokens, 2 * width_vit),
+            proj_half,
+            preferred_element_type=jnp.float32,
+        )
+
+    far_part = swap(project(from_far, from_both).astype(jnp.bfloat16), flips=(0, far, 0, 0))
+    tokens_half = (project(kept, from_tile) + far_part.astype(jnp.float32)).astype(jnp.bfloat16)
+
+    width_moe = 2 * tokens_half.shape[1]
+    expert_gate, expert_up = expert_in[0, :, 0].T, expert_in[0, :, 1].T
+    shared_gate, shared_up = shared_in[:, 0].T, shared_in[:, 1].T
+    tile_place = tile_id.astype(jnp.int32).reshape(1)
+    gain_row, lane_row = moe_gain[None], expert_lanes[None]
+    half_moe = tokens_half.shape[1]
+    held = jnp.concatenate([tokens_half, gate_rows], axis=1)
+    held_by_step = [held] + [swap(held, flips=(0, step, 0, 0)) for step in range(1, outer)]
+    tile_flip, inner_flip, core_flip = (1, 0, 0, 0), (0, 0, 1, 0), (0, 0, 0, 1)
+    contributions = []
+    for step, held in enumerate(held_by_step):
+        extra = None
+        for flip in (inner_flip, tile_flip) if step % 2 else (tile_flip, inner_flip):
+            arrived = swap(held, flips=flip)
+            if step == 0 and flip == tile_flip:
+                extra = run_shared(
+                    tile_place, held, arrived, gain_row, shared_gate, shared_up, shared_out
+                )
+                residual = jnp.concatenate(
+                    by_place(
+                        tile_id,
+                        *(
+                            lax.dynamic_slice_in_dim(
+                                rows[:, :half_moe], tile_id * token_count, token_count, 0
+                            )
+                            for rows in (held, arrived)
+                        ),
+                    ),
+                    axis=1,
+                )
+            held = jnp.stack([held, arrived])
+        if step % 2:
+            held = held.transpose(1, 0, 2, 3)
+        contributions.append(
+            run_expert(
+                tile_place,
+                held,
+                swap(held, flips=core_flip),
+                gain_row,
+                lane_row,
+                expert_gate,
+                expert_up,
+                expert_out[0],
+                extra,
             )
-    page_tokens = 2 * token_count
-    inner_part = shift(projected[page_tokens:].astype(jnp.bfloat16), moved=(0, 0, 1, 0))
-    tokens_half = (projected[:page_tokens] + inner_part.astype(jnp.float32)).astype(jnp.bfloat16)
-
-    width_moe = 2 * tokens_half.shape[1]
-    shared_flat = shared_in.reshape(width_moe, -1)
-    expert_flat = expert_in.reshape(width_moe, -1)
-    expert_back = expert_out.reshape(-1, width_moe)
-    contributions = []
-    residual = None
-    halves_by_step = [tokens_half] + [
-        shift(tokens_half, moved=(0, step, 0, 0)) for step in range(1, outer)
-    ]
-    for step, held in enumerate(halves_by_step):
-        over_tile = shift(held, moved=(1, 0, 0, 0))
-        over_inner = shift(held, moved=(0, 0, 1, 0))
-        over_both = shift(held, moved=(1, 0, 1, 0))
-        block = jnp.stack([held, over_tile, over_inner, over_both])
-        core_block = shift(block, moved=(0, 0, 0, 1))
-        mine = jnp.concatenate([block[0], block[2], core_block[0], core_block[2]], axis=0)
-        tiles_other = jnp.concatenate([block[1], block[3], core_block[1], core_block[3]], axis=0)
-        tokens = jnp.concatenate(by_tile(mine, tiles_other), axis=1)
-        moe_in = rms_norm(tokens.astype(jnp.float32), moe_gain).astype(jnp.bfloat16)
-        gated = jnp.dot(moe_in, expert_flat, preferred_element_type=jnp.float32)
-        units = gated.shape[1] // 2
-        hidden_units = (jax.nn.silu(gated[:, :units]) * gated[:, units:]).astype(jnp.bfloat16)
-        result = jnp.dot(hidden_units, expert_back, preferred_element_type=jnp.float32)
-        outer_page = (outer_id - step) % outer
-        step_gates = jnp.concatenate(
-            [
-                lax.dynamic_index_in_dim(
-                    expert_gates,
-                    outer_page * 4 + (inner_id ^ other_inner) * 2 + (core_id ^ other_core),
-                    0,
-                    keepdims=False,
-                )
-                for other_core in range(2)
-                for other_inner in range(2)
-            ]
-        )
-        result = result * step_gates[:, None]
-        if step == 0:
-            residual = lax.dynamic_slice_in_dim(
-                tokens[:page_tokens], tile_id * token_count, token_count, 0
-            )
-            shared_gated = jnp.dot(
-                moe_in[:page_tokens], shared_flat, preferred_element_type=jnp.float32
-            )
-            shared_units = shared_gated.shape[1] // 2
-            shared_hidden = (
-                jax.nn.silu(shared_gated[:, :shared_units]) * shared_gated[:, shared_units:]
-            ).astype(jnp.bfloat16)
-            shared_part = jnp.dot(shared_hidden, shared_out, preferred_element_type=jnp.float32)
-            result = jnp.concatenate(
-                [result[:page_tokens] + shared_part, result[page_tokens:]], axis=0
-            )
-        contributions.append(result.astype(jnp.bfloat16))
+        )
+
+    def add(mine, other):
+        return (mine.astype(jnp.float32) + other.astype(jnp.float32)).astype(jnp.bfloat16)
 
     total = residual.astype(jnp.float32)
-    for step, result in enumerate(contributions):
-        across = shift(result[2 * page_tokens :], moved=(0, 0, 0, 1))
-        summed = (
-            (result[: 2 * page_tokens].astype(jnp.float32) + across.astype(jnp.float32))
-            .astype(jnp.bfloat16)
-            .reshape(2, 2, token_count, width_moe)
-        )
-        here, there = summed[:, 0], summed[:, 1]
-        stays = jnp.where(tile_id == 0, here, there)
-        leaves = jnp.where(tile_id == 0, there, here)
-        step_total = (
-            stays[0].astype(jnp.float32)
-            + shift(leaves[0], moved=(1, 0, 0, 0)).astype(jnp.float32)
-            + shift(stays[1], moved=(0, 0, 1, 0)).astype(jnp.float32)
-            + shift(leaves[1], moved=(1, 0, 1, 0)).astype(jnp.float32)
-        )
+    for step, (own_sums, across_sums) in enumerate(contributions):
+        summed = add(own_sums, swap(across_sums, flips=core_flip)).reshape(
+            2, 2, token_count, width_moe
+        )
+        if step % 2:
+            summed = add(summed[0], swap(summed[1], flips=inner_flip))
+            stays, leaves = by_place(tile_id, summed[0], summed[1])
+            summed = add(stays, swap(leaves, flips=tile_flip))
+        else:
+            stays, leaves = by_place(tile_id, summed[:, 0], summed[:, 1])
+            summed = add(stays, swap(leaves, flips=tile_flip))
+            summed = add(summed[0], swap(summed[1], flips=inner_flip))
         if step:
-            step_total = shift(
-                step_total.astype(jnp.bfloat16), moved=(0, outer - step, 0, 0)
-            ).astype(jnp.float32)
-        total = total + step_total
+            summed = swap(summed, flips=(0, step, 0, 0))
+        total = total + summed.astype(jnp.float32)
     return total.astype(jnp.bfloat16).reshape(1, row_count // 2, columns // 2, width_moe)
 
 

time: 232 us -> 169 us (0.73)
  blocking collectives: 65.3 us -> 0 us
  Pallas kernels: 0 us -> 21.7 us
  matrix products: 40.5 us -> 21.5 us
  local copies, waits for them, and re-layouts: 8.59 us -> 25.2 us
  other arithmetic: 17.7 us -> 6.47 us
  starting transfers between devices: 52.8 us -> 44 us
  waiting for transfers between devices: 43.9 us -> 49 us
    all_gather x1 -> x0, blocking collectives: 65.3 us -> none  [per_device_near(): lax.all_gather(dense_gates, ('expert', 'tile'), axis=0, tiled=True)]
    pallas_call x0 -> x5, Pallas kernels: none -> 21.7 us  [the longest x4 18 us: run_expert(): pl.pallas_call(partial(expert_kernel, pieces, extra is not None), out_sha...]
    dot_general x18 -> x2, matrix products: 22.8 us -> 7.14 us  [project(): jnp.dot(features.reshape(page_tokens, 2 * width_vit), proj_half, preferre...]
    dynamic_update_slice x0 -> x8, local copies, waits for them, and re-layouts: none -> 11.2 us  [per_device_near(): lax.dynamic_update_slice_in_dim(proj_half, block, spot * shard_rows, axis=0)]
    ppermute x51 -> x43, starting transfers between devices: 52.8 us -> 44 us  [near_swap(): return lax.ppermute(values, ('tile', 'expert'), pairs)]
    transpose x0 -> x3, local copies, waits for them, and re-layouts: none -> 7.28 us  [the longest x1 6.25 us: per_device_near(): shared_gate, shared_up = (shared_in[:, 0].T, shared_in[:, 1].T)]
    ppermute x51 -> x43, waiting for transfers between devices: 43.9 us -> 49 us  [near_swap(): return lax.ppermute(values, ('tile', 'expert'), pairs)]
    another operation x8 -> x12, other arithmetic: 6.28 us -> 1.98 us  [the longest x4 3.33 us: per_device_near(): block = jnp.stack([held, over_tile, over_inner, over_both])]
  transfers between devices with their start and end apart: 51 -> 43, of which waited for: 20 -> 12; matrix products, arithmetic and copies ran while one was open for 27% -> 26% of each run, Pallas kernels for 0% -> 13%
where the time goes in v2:
time: 169 us
  waiting for transfers between devices  49 us (29%)
  starting transfers between devices  44 us (26%)
  local copies, waits for them, and re-layouts  25.2 us (15%)
  Pallas kernels  21.7 us (13%)
  matrix products  21.5 us (13%)
  other arithmetic  6.47 us (4%)
    ppermute x43, waiting for transfers between devices, near_swap(): return lax.ppermute(values, ('tile', 'expert'), pairs)  49 us
    ppermute x43, starting transfers between devices, near_swap(): return lax.ppermute(values, ('tile', 'expert'), pairs)  44 us
    pallas_call x4, Pallas kernels, run_expert(): pl.pallas_call(partial(expert_kernel, pieces, extra is not None), out_sha...  18 us
    dynamic_update_slice x8, local copies, waits for them, and re-layouts, per_device_near(): lax.dynamic_update_slice_in_dim(proj_half, block, spot * shard_rows, axis=0)  11.2 us
    dot_general x2, matrix products, project(): jnp.dot(features.reshape(page_tokens, 2 * width_vit), proj_half, preferre...  7.14 us
    dot_general x2, matrix products, project_qkv(): jnp.dot(normed, qkv_weight.reshape(width_vit, -1), preferred_element_type...  7 us
    transpose x1, local copies, waits for them, and re-layouts, per_device_near(): shared_gate, shared_up = (shared_in[:, 0].T, shared_in[:, 1].T)  6.25 us
    pallas_call x1, Pallas kernels, run_shared(): pl.pallas_call(partial(shared_kernel, pieces), out_shape=jax.ShapeDtypeSt...  3.68 us
  transfers between devices with their start and end apart: 43, of which 12 were waited for; matrix products, arithmetic and copies ran while one was open for 26% of the time, Pallas kernels for 13%

profile of v2, /device:TPU:0, one launch (start us, length us, event | category | flops | bytes accessed | tf_op | source)
XLA Modules:
  0.0 168.8 jit_solution(14942269117432905189)
XLA Ops:
  0.5 2.6 %collective-permute-start.4 = (bf16[288,1024]{1,0:T(8,128)(2,1)}, bf16[288,1024]{1,0:T(8,128)(2,1)}, u32[]{:S(2)}, u32[]{:S(2)}) collective-permute-start(bf16[288,1024]{1,0:T(8,128)(2,1)} %param.22), channel_id=1, source_target_pairs={{0,2},{1,3},{2,0},{3,1},{4,6},{5,7},{6,4},{7,5},{8,10},{9,11},{10,... | collective-permute-start | bytes 1769480 | tf_op jit(solution)/shard_map/ppermute | solution.py:218
  11.6 3.5 %convolution_add_fusion.2 = f32[128,3,8,72]{0,3,2,1:T(8,128)S(1)} fusion(bf16[128,1152,1,1]{1,0,3,2:T(8,128)(2,1)S(1)} %bitcast.196, bf16[3,8,72,1152]{3,2,1,0:T(8,128)(2,1)} %bitcast.186, f32[3,8,72]{2,1,0:T(8,128)S(1)} %add.459), kind=kOutput, calls=%fused_computation.15 | convolution fusion | flops 509829120 | bytes 5167872 | tf_op jit(solution)/shard_map/dot_general | solution.py:490
  16.9 6.2 %slice_bitcast_fusion = (bf16[704,2048]{1,0:T(8,128)(2,1)}, bf16[704,2048]{1,0:T(8,128)(2,1)}) fusion(bf16[2048,2,704]{0,2,1:T(8,128)(2,1)} %param.26), kind=kLoop, calls=%fused_computation.2 | loop fusion | bytes 11534336 | tf_op jit(solution)/shard_map/transpose | solution.py:546
  23.1 2.8 %broadcast_in_dim.20 = bf16[2304,1024]{1,0:T(8,128)(2,1)} broadcast(bf16[]{:T(256)} %constant.180.clone.1), dimensions={} | broadcast | bytes 4718594 | tf_op jit(solution)/shard_map/broadcast_in_dim | solution.py:446
  27.3 3.6 %convolution_add_fusion.1 = f32[128,3,8,72]{0,3,2,1:T(8,128)S(1)} fusion(bf16[3,8,72,1152]{3,2,1,0:T(8,128)(2,1)} %bitcast.187, f32[3,8,72]{2,1,0:T(8,128)S(1)} %add.459, bf16[128,1152]{1,0:T(8,128)(2,1)S(1)} %collective-permute-done, f32[1152]{0:T(1024)S(1)} %copy-done.15, f32[128]{0:T(128)S(1)} %add_rsqrt_fusion.2, f32[128]{0:T(128)S(1)} %broadcast_multiply_fusion.2), kind=kOutput, calls=%fused_computation.14 | convolution fusion | flops 510566400 | bytes 5173504 | tf_op jit(solution)/shard_map/dot_general | solution.py:490
  38.2 4.9 %collective-permute-done.1 = bf16[128,1152]{1,0:T(8,128)(2,1)S(1)} collective-permute-done((bf16[128,1152]{1,0:T(8,128)(2,1)S(1)}, bf16[128,1152]{1,0:T(8,128)(2,1)S(1)}, u32[]{:S(2)}, u32[]{:S(2)}) %collective-permute-start.1) | collective-permute-done | bytes 294944 | tf_op jit(solution)/shard_map/ppermute | solution.py:218
  44.1 2.7 %collective-permute-start.10 = (bf16[64,1152]{1,0:T(8,128)(2,1)S(1)}, bf16[64,1152]{1,0:T(8,128)(2,1)S(1)}, u32[]{:S(2)}, u32[]{:S(2)}) collective-permute-start(bf16[64,1152]{1,0:T(8,128)(2,1)S(1)} %get-tuple-element.61), channel_id=1, source_target_pairs={{0,8},{1,9},{2,10},{3,11},{4,12},{5,13},{6,14},{7,15},{8,0},{9,1},... | collective-permute-start | bytes 442376 | tf_op jit(solution)/shard_map/ppermute | solution.py:218
  52.9 3.8 %collective-permute-done.10 = bf16[64,1152]{1,0:T(8,128)(2,1)S(1)} collective-permute-done((bf16[64,1152]{1,0:T(8,128)(2,1)S(1)}, bf16[64,1152]{1,0:T(8,128)(2,1)S(1)}, u32[]{:S(2)}, u32[]{:S(2)}) %collective-permute-start.10) | collective-permute-done | bytes 147488 | tf_op jit(solution)/shard_map/ppermute | solution.py:218
  65.5 3.9 %convolution_convert_fusion.3 = bf16[64,1024]{1,0:T(8,128)(2,1)S(1)} fusion(bf16[2304,1024]{1,0:T(8,128)(2,1)} %constant_dynamic-update-slice_fusion, bf16[64,1152]{1,0:T(8,128)(2,1)S(1)} %bitcast.202, bf16[64,1152]{1,0:T(8,128)(2,1)S(1)} %bitcast.201), kind=kOutput, calls=%fused_computation.20 | convolution fusion | flops 302645248 | bytes 5144576 | tf_op jit(solution)/shard_map/dot_general | solution.py:535
  69.5 8.4 %collective-permute-done.12 = bf16[64,1024]{1,0:T(8,128)(2,1)S(1)} collective-permute-done((bf16[64,1024]{1,0:T(8,128)(2,1)S(1)}, bf16[64,1024]{1,0:T(8,128)(2,1)S(1)}, u32[]{:S(2)}, u32[]{:S(2)}) %collective-permute-start.12) | collective-permute-done | bytes 131104 | tf_op jit(solution)/shard_map/ppermute | solution.py:218
  77.9 3.3 %fusion.6 = bf16[64,1024]{1,0:T(8,128)(2,1)S(1)} fusion(bf16[2304,1024]{1,0:T(8,128)(2,1)} %constant_dynamic-update-slice_fusion, bf16[64,1152]{1,0:T(8,128)(2,1)S(1)} %bitcast.204, bf16[64,1152]{1,0:T(8,128)(2,1)S(1)} %bitcast.203, bf16[64,1024]{1,0:T(8,128)(2,1)S(1)} %collective-permute-done.12), kind=kOutput, calls=%fused_computation.19 | convolution fusion | flops 302776320 | bytes 5275648 | tf_op jit(solution)/shard_map/dot_general | solution.py:535
  85.6 2.6 %collective-permute-start.35 = (bf16[64,1152]{1,0:T(8,128)(2,1)S(1)}, bf16[64,1152]{1,0:T(8,128)(2,1)S(1)}, u32[]{:S(2)}, u32[]{:S(2)}) collective-permute-start(bf16[64,1152]{1,0:T(8,128)(2,1)S(1)} %get-tuple-element.78.refs_1_), channel_id=1, source_target_pairs={{0,12},{1,13},{2,14},{3,15},{4,8},{5,9},{6,10},{7,11},{8,4},{9,5},... | collective-permute-start | bytes 442376 | tf_op jit(solution)/shard_map/ppermute | solution.py:218
  92.8 3.5 %collective-permute-done.27 = bf16[64,1152]{1,0:T(8,128)(2,1)S(1)} collective-permute-done((bf16[64,1152]{1,0:T(8,128)(2,1)S(1)}, bf16[64,1152]{1,0:T(8,128)(2,1)S(1)}, u32[]{:S(2)}, u32[]{:S(2)}) %collective-permute-start.27) | collective-permute-done | bytes 147488 | tf_op jit(solution)/shard_map/ppermute | solution.py:218
  98.4 3.7 %shared_units.1.refs_8_ = f32[64,2048]{1,0:T(8,128)S(1)} custom-call(s32[1]{0:T(128)} %bitcast.29.refs_0_, bf16[64,1152]{1,0:T(8,128)(2,1)S(1)} %get-tuple-element.78.refs_1_, bf16[64,1152]{1,0:T(8,128)(2,1)S(1)} %collective-permute-done.13.refs_2_, f32[1,2048]{1,0:T(1,128)S(1)} %bitcast.181, bf16[704,2048]{1,0:T(8,128)(2,1)S(1)} %copy-done.4, ...), custom_call_target="tpu_custom_call" | custom-call | flops 553648128 | bytes 9175040 | tf_op jit(solution)/shard_map/shared_units/pallas_call | solution.py:388
  105.1 5.8 %collective-permute-done.21 = bf16[2,64,1152]{2,1,0:T(8,128)(2,1)S(1)} collective-permute-done((bf16[2,64,1152]{2,1,0:T(8,128)(2,1)S(1)}, bf16[2,64,1152]{2,1,0:T(8,128)(2,1)S(1)}, u32[]{:S(2)}, u32[]{:S(2)}) %collective-permute-start.21) | collective-permute-done | bytes 294944 | tf_op jit(solution)/shard_map/ppermute | solution.py:218
  114.3 4.4 %expert_units.4 = (bf16[2,64,2048]{2,1,0:T(8,128)(2,1)S(1)}, bf16[2,64,2048]{2,1,0:T(8,128)(2,1)S(1)}) custom-call(s32[1]{0:T(128)} %bitcast.29.refs_0_, bf16[2,2,64,1152]{3,2,1,0:T(8,128)(2,1)S(1)} %pad_maximum_fusion.refs_1_, bf16[2,2,64,1152]{3,2,1,0:T(8,128)(2,1)S(1)} %collective-permute-done.15.refs_2_, f32[1,2048]{1,0:T(1,128)S(1)} %bitcast.182, ...), custom_call_target="tpu_custom_call" | custom-call | flops 2214592512 | bytes 10747904 | tf_op jit(solution)/shard_map/expert_units/pallas_call | solution.py:355
  119.3 4.4 %expert_units.5 = (bf16[2,64,2048]{2,1,0:T(8,128)(2,1)S(1)}, bf16[2,64,2048]{2,1,0:T(8,128)(2,1)S(1)}) custom-call(s32[1]{0:T(128)} %bitcast.29.refs_0_, bf16[2,2,64,1152]{3,2,1,0:T(8,128)(2,1)S(1)} %copy.57.refs_1_, bf16[2,2,64,1152]{3,2,1,0:T(8,128)(2,1)S(1)} %copy.58.refs_2_, f32[1,2048]{1,0:T(1,128)S(1)} %bitcast.183, ...), custom_call_target="tpu_custom_call" | custom-call | flops 2214592512 | bytes 10747904 | tf_op jit(solution)/shard_map/expert_units/pallas_call | solution.py:355
  123.9 4.7 %expert_units.6 = (bf16[2,64,2048]{2,1,0:T(8,128)(2,1)S(1)}, bf16[2,64,2048]{2,1,0:T(8,128)(2,1)S(1)}) custom-call(s32[1]{0:T(128)} %bitcast.29.refs_0_, bf16[2,2,64,1152]{3,2,1,0:T(8,128)(2,1)S(1)} %pad_maximum_fusion.1.refs_1_, bf16[2,2,64,1152]{3,2,1,0:T(8,128)(2,1)S(1)} %collective-permute-done.30.refs_2_, f32[1,2048]{1,0:T(1,128)S(1)} %bitcast.184, ...), custom_call_target="tpu_custom_call" | custom-call | flops 2214592512 | bytes 10747904 | tf_op jit(solution)/shard_map/expert_units/pallas_call | solution.py:355
  129.1 4.4 %expert_units.7 = (bf16[2,64,2048]{2,1,0:T(8,128)(2,1)S(1)}, bf16[2,64,2048]{2,1,0:T(8,128)(2,1)S(1)}) custom-call(s32[1]{0:T(128)} %bitcast.29.refs_0_, bf16[2,2,64,1152]{3,2,1,0:T(8,128)(2,1)S(1)} %maximum_bitcast_fusion.1.refs_1_, bf16[2,2,64,1152]{3,2,1,0:T(8,128)(2,1)S(1)} %collective-permute-done.38.refs_2_, f32[1,2048]{1,0:T(1,128)S(1)} %bitcast.185, ...), custom_call_target="tpu_custom_call" | custom-call | flops 2214592512 | bytes 10747904 | tf_op jit(solution)/shard_map/expert_units/pallas_call | solution.py:355
  138.7 4.3 %collective-permute-done.17 = bf16[2,32,2048]{2,1,0:T(8,128)(2,1)S(1)} collective-permute-done((bf16[2,32,2048]{2,1,0:T(8,128)(2,1)S(1)}, bf16[2,32,2048]{2,1,0:T(8,128)(2,1)S(1)}, u32[]{:S(2)}, u32[]{:S(2)}) %collective-permute-start.17) | collective-permute-done | bytes 262176 | tf_op jit(solution)/shard_map/ppermute | solution.py:218
  145.4 3.1 %collective-permute-done.32 = bf16[2,32,2048]{2,1,0:T(8,128)(2,1)S(1)} collective-permute-done((bf16[2,32,2048]{2,1,0:T(8,128)(2,1)S(1)}, bf16[2,32,2048]{2,1,0:T(8,128)(2,1)S(1)}, u32[]{:S(2)}, u32[]{:S(2)}) %collective-permute-start.32) | collective-permute-done | bytes 262176 | tf_op jit(solution)/shard_map/ppermute | solution.py:218
  151.1 3.4 %collective-permute-start.26 = (bf16[32,2048]{1,0:T(8,128)(2,1)S(1)}, bf16[32,2048]{1,0:T(8,128)(2,1)S(1)}, u32[]{:S(2)}, u32[]{:S(2)}) collective-permute-start(bf16[32,2048]{1,0:T(8,128)(2,1)S(1)} %fusion.34), channel_id=1, source_target_pairs={{0,4},{1,5},{2,6},{3,7},{4,0},{5,1},{6,2},{7,3},{8,12},{9,13},{10,... | collective-permute-start | bytes 393224 | tf_op jit(solution)/shard_map/ppermute | solution.py:218
  155.2 2.9 %collective-permute-start.34 = (bf16[32,2048]{1,0:T(8,128)(2,1)S(1)}, bf16[32,2048]{1,0:T(8,128)(2,1)S(1)}, u32[]{:S(2)}, u32[]{:S(2)}) collective-permute-start(bf16[32,2048]{1,0:T(8,128)(2,1)S(1)} %fusion.33), channel_id=1, source_target_pairs={{0,8},{1,9},{2,10},{3,11},{4,12},{5,13},{6,14},{7,15},{8,0},{9,1},... | collective-permute-start | bytes 393224 | tf_op jit(solution)/shard_map/ppermute | solution.py:218
  160.3 7.7 %collective-permute-done.34 = bf16[32,2048]{1,0:T(8,128)(2,1)S(1)} collective-permute-done((bf16[32,2048]{1,0:T(8,128)(2,1)S(1)}, bf16[32,2048]{1,0:T(8,128)(2,1)S(1)}, u32[]{:S(2)}, u32[]{:S(2)}) %collective-permute-start.34) | collective-permute-done | bytes 131104 | tf_op jit(solution)/shard_map/ppermute | solution.py:218
  (208 shorter events, 67.4 us)
Async XLA Ops:
  0.0 46.8 %collective-permute-start.3 = (bf16[288,1024]{1,0:T(8,128)(2,1)}, bf16[288,1024]{1,0:T(8,128)(2,1)}, u32[]{:S(2)}, u32[]{:S(2)}) collective-permute-start(bf16[288,1024]{1,0:T(8,128)(2,1)} %param.22), channel_id=1, source_target_pairs={{0,1},{1,0},{2,3},{3,2},{4,5},{5,4},{6,7},{7,6},{8,9},{9,8},{10,11... | collective-permute-start | bytes 1769480 | tf_op jit(solution)/shard_map/ppermute | solution.py:218
  0.5 48.4 %collective-permute-start.4 = (bf16[288,1024]{1,0:T(8,128)(2,1)}, bf16[288,1024]{1,0:T(8,128)(2,1)}, u32[]{:S(2)}, u32[]{:S(2)}) collective-permute-start(bf16[288,1024]{1,0:T(8,128)(2,1)} %param.22), channel_id=1, source_target_pairs={{0,2},{1,3},{2,0},{3,1},{4,6},{5,7},{6,4},{7,5},{8,10},{9,11},{10,... | collective-permute-start | bytes 1769480 | tf_op jit(solution)/shard_map/ppermute | solution.py:218
  3.0 49.4 %collective-permute-start.6 = (bf16[288,1024]{1,0:T(8,128)(2,1)}, bf16[288,1024]{1,0:T(8,128)(2,1)}, u32[]{:S(2)}, u32[]{:S(2)}) collective-permute-start(bf16[288,1024]{1,0:T(8,128)(2,1)} %param.22), channel_id=1, source_target_pairs={{0,4},{1,5},{2,6},{3,7},{4,0},{5,1},{6,2},{7,3},{8,12},{9,13},{10,... | collective-permute-start | bytes 1769480 | tf_op jit(solution)/shard_map/ppermute | solution.py:218
  4.6 47.8 %collective-permute-start.8 = (bf16[288,1024]{1,0:T(8,128)(2,1)}, bf16[288,1024]{1,0:T(8,128)(2,1)}, u32[]{:S(2)}, u32[]{:S(2)}) collective-permute-start(bf16[288,1024]{1,0:T(8,128)(2,1)} %param.22), channel_id=1, source_target_pairs={{0,6},{1,7},{2,4},{3,5},{4,2},{5,3},{6,0},{7,1},{8,14},{9,15},{10,... | collective-permute-start | bytes 1769480 | tf_op jit(solution)/shard_map/ppermute | solution.py:218
  5.7 21.2 %collective-permute-start = (bf16[128,1152]{1,0:T(8,128)(2,1)S(1)}, bf16[128,1152]{1,0:T(8,128)(2,1)S(1)}, u32[]{:S(2)}, u32[]{:S(2)}) collective-permute-start(bf16[128,1152]{1,0:T(8,128)(2,1)S(1)} %bitcast.194), channel_id=1, source_target_pairs={{0,16},{1,17},{2,18},{3,19},{4,20},{5,21},{6,22},{7,23},{8,24},{9,... | collective-permute-start | bytes 884744 | tf_op jit(solution)/shard_map/ppermute | solution.py:218
  44.1 12.6 %collective-permute-start.10 = (bf16[64,1152]{1,0:T(8,128)(2,1)S(1)}, bf16[64,1152]{1,0:T(8,128)(2,1)S(1)}, u32[]{:S(2)}, u32[]{:S(2)}) collective-permute-start(bf16[64,1152]{1,0:T(8,128)(2,1)S(1)} %get-tuple-element.61), channel_id=1, source_target_pairs={{0,8},{1,9},{2,10},{3,11},{4,12},{5,13},{6,14},{7,15},{8,0},{9,1},... | collective-permute-start | bytes 442376 | tf_op jit(solution)/shard_map/ppermute | solution.py:218
  46.8 12.1 %collective-permute-start.11 = (bf16[64,1152]{1,0:T(8,128)(2,1)S(1)}, bf16[64,1152]{1,0:T(8,128)(2,1)S(1)}, u32[]{:S(2)}, u32[]{:S(2)}) collective-permute-start(bf16[64,1152]{1,0:T(8,128)(2,1)S(1)} %get-tuple-element.61), channel_id=1, source_target_pairs={{0,24},{1,25},{2,26},{3,27},{4,28},{5,29},{6,30},{7,31},{8,16},{9,... | collective-permute-start | bytes 442376 | tf_op jit(solution)/shard_map/ppermute | solution.py:218
  48.9 10.0 %collective-permute-start.2 = (bf16[64,1152]{1,0:T(8,128)(2,1)S(1)}, bf16[64,1152]{1,0:T(8,128)(2,1)S(1)}, u32[]{:S(2)}, u32[]{:S(2)}) collective-permute-start(bf16[64,1152]{1,0:T(8,128)(2,1)S(1)} %get-tuple-element.62), channel_id=1, source_target_pairs={{0,16},{1,17},{2,18},{3,19},{4,20},{5,21},{6,22},{7,23},{8,24},{9,... | collective-permute-start | bytes 442376 | tf_op jit(solution)/shard_map/ppermute | solution.py:218
  52.4 9.4 %collective-permute-start.7 = (bf16[288,1024]{1,0:T(8,128)(2,1)}, bf16[288,1024]{1,0:T(8,128)(2,1)S(1)}, u32[]{:S(2)}, u32[]{:S(2)}) collective-permute-start(bf16[288,1024]{1,0:T(8,128)(2,1)} %collective-permute-done.6), channel_id=1, source_target_pairs={{0,1},{1,0},{2,3},{3,2},{4,5},{5,4},{6,7},{7,6},{8,9},{9,8},{10,11... | collective-permute-start | bytes 1769480 | tf_op jit(solution)/shard_map/ppermute | solution.py:218
  81.2 11.0 %collective-permute-start.13 = (bf16[64,1152]{1,0:T(8,128)(2,1)S(1)}, bf16[64,1152]{1,0:T(8,128)(2,1)S(1)}, u32[]{:S(2)}, u32[]{:S(2)}) collective-permute-start(bf16[64,1152]{1,0:T(8,128)(2,1)S(1)} %get-tuple-element.78.refs_1_), channel_id=1, source_target_pairs={{0,16},{1,17},{2,18},{3,19},{4,20},{5,21},{6,22},{7,23},{8,24},{9,... | collective-permute-start | bytes 442376 | tf_op jit(solution)/shard_map/ppermute | solution.py:218
  83.8 12.5 %collective-permute-start.27 = (bf16[64,1152]{1,0:T(8,128)(2,1)S(1)}, bf16[64,1152]{1,0:T(8,128)(2,1)S(1)}, u32[]{:S(2)}, u32[]{:S(2)}) collective-permute-start(bf16[64,1152]{1,0:T(8,128)(2,1)S(1)} %get-tuple-element.78.refs_1_), channel_id=1, source_target_pairs={{0,8},{1,9},{2,10},{3,11},{4,12},{5,13},{6,14},{7,15},{8,0},{9,1},... | collective-permute-start | bytes 442376 | tf_op jit(solution)/shard_map/ppermute | solution.py:218
  85.6 11.2 %collective-permute-start.35 = (bf16[64,1152]{1,0:T(8,128)(2,1)S(1)}, bf16[64,1152]{1,0:T(8,128)(2,1)S(1)}, u32[]{:S(2)}, u32[]{:S(2)}) collective-permute-start(bf16[64,1152]{1,0:T(8,128)(2,1)S(1)} %get-tuple-element.78.refs_1_), channel_id=1, source_target_pairs={{0,12},{1,13},{2,14},{3,15},{4,8},{5,9},{6,10},{7,11},{8,4},{9,5},... | collective-permute-start | bytes 442376 | tf_op jit(solution)/shard_map/ppermute | solution.py:218
  90.7 11.4 %collective-permute-start.20 = (bf16[64,1152]{1,0:T(8,128)(2,1)S(1)}, bf16[64,1152]{1,0:T(8,128)(2,1)S(1)}, u32[]{:S(2)}, u32[]{:S(2)}) collective-permute-start(bf16[64,1152]{1,0:T(8,128)(2,1)S(1)} %collective-permute-done.19), channel_id=1, source_target_pairs={{0,2},{1,3},{2,0},{3,1},{4,6},{5,7},{6,4},{7,5},{8,10},{9,11},{10,... | collective-permute-start | bytes 442376 | tf_op jit(solution)/shard_map/ppermute | solution.py:218
  92.3 12.7 %collective-permute-start.14 = (bf16[2,64,1152]{2,1,0:T(8,128)(2,1)S(1)}, bf16[2,64,1152]{2,1,0:T(8,128)(2,1)S(1)}, u32[]{:S(2)}, u32[]{:S(2)}) collective-permute-start(bf16[2,64,1152]{2,1,0:T(8,128)(2,1)S(1)} %get-tuple-element.50), channel_id=1, source_target_pairs={{0,2},{1,3},{2,0},{3,1},{4,6},{5,7},{6,4},{7,5},{8,10},{9,11},{10,... | collective-permute-start | bytes 884744 | tf_op jit(solution)/shard_map/ppermute | solution.py:218
  104.4 9.7 %collective-permute-start.37 = (bf16[2,64,1152]{2,1,0:T(8,128)(2,1)S(1)}, bf16[2,64,1152]{2,1,0:T(8,128)(2,1)S(1)}, u32[]{:S(2)}, u32[]{:S(2)}) collective-permute-start(bf16[2,64,1152]{2,1,0:T(8,128)(2,1)S(1)} %get-tuple-element.56), channel_id=1, source_target_pairs={{0,16},{1,17},{2,18},{3,19},{4,20},{5,21},{6,22},{7,23},{8,24},{9,... | collective-permute-start | bytes 884744 | tf_op jit(solution)/shard_map/ppermute | solution.py:218
  111.2 12.7 %collective-permute-start.30 = (bf16[2,2,64,1152]{3,2,1,0:T(8,128)(2,1)S(1)}, bf16[2,2,64,1152]{3,2,1,0:T(8,128)(2,1)S(1)}, u32[]{:S(2)}, u32[]{:S(2)}) collective-permute-start(bf16[2,2,64,1152]{3,2,1,0:T(8,128)(2,1)S(1)} %pad_maximum_fusion.1.refs_1_), channel_id=1, source_target_pairs={{0,1},{1,0},{2,3},{3,2},{4,5},{5,4},{6,7},{7,6},{8,9},{9,8},{10,11... | collective-permute-start | bytes 1769480 | tf_op jit(solution)/shard_map/ppermute | solution.py:218
  114.2 14.9 %collective-permute-start.38 = (bf16[2,2,64,1152]{3,2,1,0:T(8,128)(2,1)S(1)}, bf16[2,2,64,1152]{3,2,1,0:T(8,128)(2,1)S(1)}, u32[]{:S(2)}, u32[]{:S(2)}) collective-permute-start(bf16[2,2,64,1152]{3,2,1,0:T(8,128)(2,1)S(1)} %maximum_bitcast_fusion.1.refs_1_), channel_id=1, source_target_pairs={{0,1},{1,0},{2,3},{3,2},{4,5},{5,4},{6,7},{7,6},{8,9},{9,8},{10,11... | collective-permute-start | bytes 1769480 | tf_op jit(solution)/shard_map/ppermute | solution.py:218
  118.7 14.9 %collective-permute-start.16 = (bf16[2,64,2048]{2,1,0:T(8,128)(2,1)S(1)}, bf16[2,64,2048]{2,1,0:T(8,128)(2,1)S(1)}, u32[]{:S(2)}, u32[]{:S(2)}) collective-permute-start(bf16[2,64,2048]{2,1,0:T(8,128)(2,1)S(1)} %get-tuple-element.14), channel_id=1, source_target_pairs={{0,1},{1,0},{2,3},{3,2},{4,5},{5,4},{6,7},{7,6},{8,9},{9,8},{10,11... | collective-permute-start | bytes 1572872 | tf_op jit(solution)/shard_map/ppermute | solution.py:218
  123.8 11.5 %collective-permute-start.23 = (bf16[2,64,2048]{2,1,0:T(8,128)(2,1)S(1)}, bf16[2,64,2048]{2,1,0:T(8,128)(2,1)S(1)}, u32[]{:S(2)}, u32[]{:S(2)}) collective-permute-start(bf16[2,64,2048]{2,1,0:T(8,128)(2,1)S(1)} %get-tuple-element.16), channel_id=1, source_target_pairs={{0,1},{1,0},{2,3},{3,2},{4,5},{5,4},{6,7},{7,6},{8,9},{9,8},{10,11... | collective-permute-start | bytes 1572872 | tf_op jit(solution)/shard_map/ppermute | solution.py:218
  136.4 12.2 %collective-permute-start.32 = (bf16[2,32,2048]{2,1,0:T(8,128)(2,1)S(1)}, bf16[2,32,2048]{2,1,0:T(8,128)(2,1)S(1)}, u32[]{:S(2)}, u32[]{:S(2)}) collective-permute-start(bf16[2,32,2048]{2,1,0:T(8,128)(2,1)S(1)} %select_bitcast_fusion), channel_id=1, source_target_pairs={{0,16},{1,17},{2,18},{3,19},{4,20},{5,21},{6,22},{7,23},{8,24},{9,... | collective-permute-start | bytes 786440 | tf_op jit(solution)/shard_map/ppermute | solution.py:218
  138.1 12.2 %collective-permute-start.40 = (bf16[2,32,2048]{2,1,0:T(8,128)(2,1)S(1)}, bf16[2,32,2048]{2,1,0:T(8,128)(2,1)S(1)}, u32[]{:S(2)}, u32[]{:S(2)}) collective-permute-start(bf16[2,32,2048]{2,1,0:T(8,128)(2,1)S(1)} %bitcast.210), channel_id=1, source_target_pairs={{0,2},{1,3},{2,0},{3,1},{4,6},{5,7},{6,4},{7,5},{8,10},{9,11},{10,... | collective-permute-start | bytes 786440 | tf_op jit(solution)/shard_map/ppermute | solution.py:218
  143.1 17.2 %collective-permute-start.18 = (bf16[32,2048]{1,0:T(8,128)(2,1)S(1)}, bf16[32,2048]{1,0:T(8,128)(2,1)S(1)}, u32[]{:S(2)}, u32[]{:S(2)}) collective-permute-start(bf16[32,2048]{1,0:T(8,128)(2,1)S(1)} %slice_bitcast_fusion.14), channel_id=1, source_target_pairs={{0,2},{1,3},{2,0},{3,1},{4,6},{5,7},{6,4},{7,5},{8,10},{9,11},{10,... | collective-permute-start | bytes 393224 | tf_op jit(solution)/shard_map/ppermute | solution.py:218
  155.2 12.8 %collective-permute-start.34 = (bf16[32,2048]{1,0:T(8,128)(2,1)S(1)}, bf16[32,2048]{1,0:T(8,128)(2,1)S(1)}, u32[]{:S(2)}, u32[]{:S(2)}) collective-permute-start(bf16[32,2048]{1,0:T(8,128)(2,1)S(1)} %fusion.33), channel_id=1, source_target_pairs={{0,8},{1,9},{2,10},{3,11},{4,12},{5,13},{6,14},{7,15},{8,0},{9,1},... | collective-permute-start | bytes 393224 | tf_op jit(solution)/shard_map/ppermute | solution.py:218
  158.2 9.8 %collective-permute-start.42 = (bf16[32,2048]{1,0:T(8,128)(2,1)S(1)}, bf16[32,2048]{1,0:T(8,128)(2,1)S(1)}, u32[]{:S(2)}, u32[]{:S(2)}) collective-permute-start(bf16[32,2048]{1,0:T(8,128)(2,1)S(1)} %fusion.32), channel_id=1, source_target_pairs={{0,12},{1,13},{2,14},{3,15},{4,8},{5,9},{6,10},{7,11},{8,4},{9,5},... | collective-permute-start | bytes 393224 | tf_op jit(solution)/shard_map/ppermute | solution.py:218
  (39 other events, 382.5 us)

commit v3 on v2

--- a/solution.py
+++ b/solution.py
@@ -218,27 +218,6 @@
     return lax.ppermute(values, ("tile", "expert"), pairs)
 
 
-def rope_tables_at(rows, columns, head_size):
-    quarter = head_size // 4
-    inverse = jnp.exp(jnp.arange(quarter).astype(jnp.float32) * (-math.log(rope_base) / quarter))
-    row_angle = rows.astype(jnp.float32)[:, None] * inverse[None, :]
-    col_angle = columns.astype(jnp.float32)[:, None] * inverse[None, :]
-    return (jnp.cos(row_angle), jnp.sin(row_angle), jnp.cos(col_angle), jnp.sin(col_angle))
-
-
-def attend_rows(query_rows, key_rows, value_rows, divisor):
-    scores = (
-        jnp.einsum("qhd,khd->hqk", query_rows, key_rows, preferred_element_type=jnp.float32)
-        / divisor
-    )
-    weights = jax.nn.softmax(scores, axis=-1).astype(jnp.bfloat16)
-    return (
-        jnp.einsum("hqk,khd->qhd", weights, value_rows, preferred_element_type=jnp.float32)
-        .astype(jnp.bfloat16)
-        .reshape(query_rows.shape[0], -1)
-    )
-
-
 def unit_pieces(units):
     cuts = list(range(0, units, 256)) + [units]
     return list(zip(cuts[:-1], cuts[1:]))
@@ -302,11 +281,11 @@
 
 
 def expert_kernel(pieces, extra, *refs):
-    place_ref, near_ref, across_ref, gain_ref, lanes_ref, gate_hbm, up_hbm, back_hbm = refs[:8]
-    extra_ref = refs[8] if extra else None
-    own_out, across_out, normed, weights, gate_rows, up_rows, back_rows, arrivals = refs[8 + extra :]
+    place_ref, near_ref, across_ref, gain_ref, lanes_ref, in_hbm, back_hbm = refs[:7]
+    extra_ref = refs[7] if extra else None
+    own_out, across_out, normed, weights, gate_rows, up_rows, back_rows, arrivals = refs[7 + extra :]
     copies = fetch_units(
-        pieces, (gate_hbm, up_hbm, back_hbm), (gate_rows, up_rows, back_rows), arrivals
+        pieces, (in_hbm.at[0], in_hbm.at[1], back_hbm), (gate_rows, up_rows, back_rows), arrivals
     )
     page_refs = [
         (ref.at[inner, 0], ref.at[inner, 1]) for ref in (near_ref, across_ref) for inner in range(2)
@@ -324,10 +303,10 @@
 
 
 def shared_kernel(pieces, *refs):
-    place_ref, mine_ref, other_ref, gain_ref, gate_hbm, up_hbm, back_hbm = refs[:7]
-    out_ref, normed, gate_rows, up_rows, back_rows, arrivals = refs[7:]
+    place_ref, mine_ref, other_ref, gain_ref, in_hbm, back_hbm = refs[:6]
+    out_ref, normed, gate_rows, up_rows, back_rows, arrivals = refs[6:]
     copies = fetch_units(
-        pieces, (gate_hbm, up_hbm, back_hbm), (gate_rows, up_rows, back_rows), arrivals
+        pieces, (in_hbm.at[0], in_hbm.at[1], back_hbm), (gate_rows, up_rows, back_rows), arrivals
     )
     norm_pages(place_ref, [(mine_ref, other_ref)], gain_ref, None, normed, None)
     out_ref[...] = expert_sums(pieces, copies, normed[...], gate_rows, up_rows, back_rows)
@@ -346,7 +325,7 @@
     )
 
 
-def run_expert(tile_place, near, across, gain, lanes, gate_rows, up_rows, back_rows, extra):
+def run_expert(tile_place, near, across, gain, lanes, in_rows, back_rows, extra):
     units, width = back_rows.shape
     page_rows = near.shape[2]
     rows = 4 * page_rows
@@ -355,7 +334,7 @@
     return pl.pallas_call(
         partial(expert_kernel, pieces, extra is not None),
         out_shape=(out, out),
-        in_specs=[smem_spec] + [vmem_spec] * 4 + [any_spec] * 3 + [vmem_spec] * (extra is not None),
+        in_specs=[smem_spec] + [vmem_spec] * 4 + [any_spec] * 2 + [vmem_spec] * (extra is not None),
         out_specs=(vmem_spec, vmem_spec),
         scratch_shapes=[
             pltpu.VMEM((rows, width), jnp.bfloat16),
@@ -365,7 +344,7 @@
             pltpu.VMEM((units, width), jnp.bfloat16),
             pltpu.SemaphoreType.DMA((len(pieces), 3)),
         ],
-        compiler_params=pltpu.CompilerParams(vmem_limit_bytes=40 * 2**20),
+        compiler_params=pltpu.CompilerParams(vmem_limit_bytes=28 * 2**20),
         cost_estimate=expert_cost(rows, units, width),
         name="expert_units",
     )(
@@ -374,21 +353,20 @@
         across,
         gain,
         lanes,
-        gate_rows,
-        up_rows,
+        in_rows,
         back_rows,
         *(() if extra is None else (extra,)),
     )
 
 
-def run_shared(tile_place, mine, other, gain, gate_rows, up_rows, back_rows):
+def run_shared(tile_place, mine, other, gain, in_rows, back_rows):
     units, width = back_rows.shape
     rows = mine.shape[0]
     pieces = unit_pieces(units)
     return pl.pallas_call(
         partial(shared_kernel, pieces),
         out_shape=jax.ShapeDtypeStruct((rows, width), jnp.float32),
-        in_specs=[smem_spec] + [vmem_spec] * 3 + [any_spec] * 3,
+        in_specs=[smem_spec] + [vmem_spec] * 3 + [any_spec] * 2,
         out_specs=vmem_spec,
         scratch_shapes=[
             pltpu.VMEM((rows, width), jnp.bfloat16),
@@ -397,10 +375,165 @@
             pltpu.VMEM((units, width), jnp.bfloat16),
             pltpu.SemaphoreType.DMA((len(pieces), 3)),
         ],
-        compiler_params=pltpu.CompilerParams(vmem_limit_bytes=40 * 2**20),
+        compiler_params=pltpu.CompilerParams(vmem_limit_bytes=28 * 2**20),
         cost_estimate=expert_cost(rows, units, width),
         name="shared_units",
-    )(tile_place, mine, other, gain, gate_rows, up_rows, back_rows)
+    )(tile_place, mine, other, gain, in_rows, back_rows)
+
+
+def project_heads(rows_ref, gain_ref, weight, bias_ref, cos_ref, sin_ref, heads):
+    normed = layer_norm(rows_ref[...].astype(jnp.float32), gain_ref[...]).astype(jnp.bfloat16)
+    quarter = HD // 4
+    outs = []
+    for which in range(3):
+        mixed = (
+            lax.dot_general(
+                weight(which),
+                normed,
+                (((1,), (1,)), ((), ())),
+                preferred_element_type=jnp.float32,
+            )
+            + bias_ref[which]
+        ).reshape(heads, HD, normed.shape[0])
+        if which < 2:
+            parts = [mixed[:, n * quarter : (n + 1) * quarter] for n in range(4)]
+            partner = jnp.concatenate([-parts[1], parts[0], -parts[3], parts[2]], axis=1)
+            mixed = mixed * cos_ref[...][None] + partner * sin_ref[...][None]
+        outs.append(mixed.astype(jnp.bfloat16))
+    return outs
+
+
+def attend_heads(query, keys, values, heads):
+    turned = (((0,), (0,)), ((), ()))
+    outs = []
+    for head in range(heads):
+        scores = lax.dot_general(
+            keys[head], query[head], turned, preferred_element_type=jnp.float32
+        ) * (1.0 / math.sqrt(HD))
+        raised = jnp.exp(scores - jnp.max(scores, axis=0, keepdims=True))
+        probs = (raised / jnp.sum(raised, axis=0, keepdims=True)).astype(jnp.bfloat16)
+        outs.append(jnp.dot(values[head], probs, preferred_element_type=jnp.float32))
+    return jnp.concatenate(outs, axis=0).astype(jnp.bfloat16)
+
+
+def own_heads_kernel(heads, *refs):
+    rows_ref, gain_ref, bias_ref, cos_ref, sin_ref, weight_hbm, out_ref, weight, arrivals = refs
+    copies = [
+        pltpu.make_async_copy(weight_hbm.at[which], weight.at[which], arrivals.at[which])
+        for which in range(3)
+    ]
+    for copy in copies:
+        copy.start()
+
+    def fetched(which):
+        copies[which].wait()
+        return weight[which]
+
+    outs = project_heads(rows_ref, gain_ref, fetched, bias_ref, cos_ref, sin_ref, heads)
+    for which, values in enumerate(outs):
+        out_ref[which] = values
+
+
+def other_rows_kernel(heads, *refs):
+    rows_ref, gain_ref, bias_ref, cos_ref, sin_ref, own_ref, weight_hbm, back_hbm = refs[:8]
+    part_ref, keys_ref, weight, back, arrivals = refs[8:]
+    copies = [
+        pltpu.make_async_copy(weight_hbm.at[which], weight.at[which], arrivals.at[which])
+        for which in range(3)
+    ] + [pltpu.make_async_copy(back_hbm, back, arrivals.at[3])]
+    for copy in copies:
+        copy.start()
+
+    def fetched(which):
+        copies[which].wait()
+        return weight[which]
+
+    query, other_keys, other_values = project_heads(
+        rows_ref, gain_ref, fetched, bias_ref, cos_ref, sin_ref, heads
+    )
+    keys = jnp.concatenate([own_ref[1], other_keys], axis=2)
+    values = jnp.concatenate([own_ref[2], other_values], axis=2)
+    keys_ref[0] = keys
+    keys_ref[1] = values
+    attended = attend_heads(query, keys, values, heads)
+    copies[3].wait()
+    part_ref[...] = lax.dot_general(
+        attended, back[...], (((0,), (0,)), ((), ())), preferred_element_type=jnp.float32
+    ).astype(jnp.bfloat16)
+
+
+def own_rows_kernel(heads, *refs):
+    rows_ref, own_ref, keys_ref, back_ref, bias_ref, out_ref = refs
+    attended = attend_heads(own_ref[0], keys_ref[0], keys_ref[1], heads)
+    out_ref[...] = (
+        rows_ref[...].astype(jnp.float32)
+        + bias_ref[...]
+        + lax.dot_general(
+            attended, back_ref[...], (((0,), (0,)), ((), ())), preferred_element_type=jnp.float32
+        )
+    )
+
+
+def merge_kernel(columns, *refs):
+    place_ref, hidden_ref, arrived_ref, gain_ref, kept_ref, given_ref, scratch = refs
+    normed = layer_norm(hidden_ref[...] + arrived_ref[...].astype(jnp.float32), gain_ref[...])
+    slabs = scratch.shape[0]
+    for slab in range(slabs):
+        scratch[slab] = normed[:, slab * 128 : (slab + 1) * 128]
+    count = columns // 2
+    for pair in range(normed.shape[0] // (2 * columns)):
+        for parity in range(2):
+            rows = [
+                scratch[slab, pl.ds((2 * pair + parity) * columns + side, count, stride=2)]
+                for side in range(2)
+                for slab in range(slabs)
+            ]
+            merged = jnp.concatenate(rows, axis=1).astype(jnp.bfloat16)
+            spot = pl.ds(pair * count, count)
+
+            @pl.when(place_ref[0] == parity)
+            def _keep(merged=merged, spot=spot):
+                kept_ref[spot] = merged
+
+            @pl.when(place_ref[0] != parity)
+            def _give(merged=merged, spot=spot):
+                given_ref[spot] = merged
+
+
+def projector_kernel(spots_ref, place_ref, mine_ref, other_ref, *refs):
+    weight_refs, out_ref, blocks = refs[:-2], refs[-2], refs[-1]
+    count, size = mine_ref.shape[0], weight_refs[0].shape[0]
+    mine_rows = pl.ds(pl.multiple_of(place_ref[0] * count, count), count)
+    other_rows = pl.ds(pl.multiple_of((1 - place_ref[0]) * count, count), count)
+    for number in range(len(weight_refs)):
+        lanes = slice(number * size, (number + 1) * size)
+        blocks[number, mine_rows] = mine_ref[:, lanes]
+        blocks[number, other_rows] = other_ref[:, lanes]
+    total = None
+    for number, weight_ref in enumerate(weight_refs):
+        part = jnp.dot(
+            blocks[spots_ref[number]], weight_ref[...], preferred_element_type=jnp.float32
+        )
+        total = part if total is None else total + part
+    out_ref[...] = total.astype(out_ref.dtype)
+
+
+def run_projector(spots, place, mine, other, weights, dtype):
+    rows, size, width = 2 * mine.shape[0], weights[0].shape[0], weights[0].shape[1]
+    return pl.pallas_call(
+        projector_kernel,
+        out_shape=jax.ShapeDtypeStruct((rows, width), dtype),
+        in_specs=[smem_spec] * 2 + [vmem_spec] * (2 + len(weights)),
+        out_specs=vmem_spec,
+        scratch_shapes=[pltpu.VMEM((len(weights), rows, size), jnp.bfloat16)],
+        compiler_params=pltpu.CompilerParams(vmem_limit_bytes=28 * 2**20),
+        cost_estimate=pl.CostEstimate(
+            flops=2 * rows * width * size * len(weights),
+            bytes_accessed=2 * width * size * len(weights),
+            transcendentals=0,
+        ),
+        name="projector",
+    )(spots, place, mine, other, *weights)
 
 
 def per_device_near(
@@ -429,33 +562,27 @@
     row_count, columns, width_vit = patches.shape[1:]
     local_rows = row_count * columns
     token_count = local_rows // 4
-    heads_here = qkv_weight.shape[2] // HD
 
     def by_place(place, mine, other):
         first = place == 0
         return jnp.where(first, mine, other), jnp.where(first, other, mine)
 
-    own_patches = (
-        patches.reshape(row_count // 2, 2, columns // 2, 2, width_vit)
-        .transpose(1, 3, 0, 2, 4)
-        .reshape(local_rows, width_vit)
-    )
+    own_patches = patches.reshape(local_rows, width_vit)
     other_patches = swap(own_patches, flips=(1, 0, 0, 0))
-
-    shard_rows = proj_weight.shape[0]
-    proj_half = jnp.zeros((outer * 2 * shard_rows, proj_weight.shape[1]), proj_weight.dtype)
+    tile_place = tile_id.astype(jnp.int32).reshape(1)
+
+    proj_blocks, proj_spots = [], []
     for low in range(outer // 2):
         for inner in range(2):
             rows = swap(proj_weight, flips=(0, low, inner, 0)) if low or inner else proj_weight
             for core, block in enumerate((rows, swap(rows, flips=(0, 0, 0, 1)))):
-                spot = (
+                proj_blocks.append(block)
+                proj_spots.append(
                     ((outer_id ^ low) % (outer // 2)) * 4
                     + (inner_id ^ inner) * 2
                     + (core_id ^ core)
                 )
-                proj_half = lax.dynamic_update_slice_in_dim(
-                    proj_half, block, spot * shard_rows, axis=0
-                )
+    proj_spots = jnp.stack(proj_spots).astype(jnp.int32)
 
     top_count = routes.shape[-1]
     page_routes = routes.reshape(2, token_count, top_count)
@@ -479,72 +606,108 @@
     expert_lanes = jnp.arange(128) % experts_count == expert_id
     expert_lanes = (expert_lanes & (jnp.arange(128) < gate_width)).astype(jnp.float32)
 
-    place = jnp.arange(local_rows)
-    pair_size = token_count
-    parity, within = place // pair_size, place % pair_size
-    patch_rows = 2 * (within // (columns // 2)) + parity // 2
-    patch_cols = 2 * (within % (columns // 2)) + parity % 2
-
-    def project_qkv(rows, tile):
-        normed = layer_norm(rows.astype(jnp.float32), norm1_gain).astype(jnp.bfloat16)
-        mixed = jnp.dot(
-            normed, qkv_weight.reshape(width_vit, -1), preferred_element_type=jnp.float32
-        ).reshape(rows.shape[0], 3, heads_here, HD) + qkv_bias.reshape(1, 3, heads_here, HD)
-        tables = rope_tables_at(tile * row_count + patch_rows, patch_cols, HD)
-        return (
-            rotate(mixed[:, 0], tables).astype(jnp.bfloat16),
-            rotate(mixed[:, 1], tables).astype(jnp.bfloat16),
-            mixed[:, 2].astype(jnp.bfloat16),
-        )
-
-    own_query, own_key, own_value = project_qkv(own_patches, tile_id)
-    other_query, other_key, other_value = project_qkv(other_patches, 1 - tile_id)
-    keys = jnp.concatenate([own_key, other_key], axis=0)
-    values = jnp.concatenate([own_value, other_value], axis=0)
-    other_part = jnp.dot(
-        attend_rows(other_query, keys, values, math.sqrt(HD)),
+    heads = qkv_weight.shape[2] // HD
+    weight_rows = qkv_weight.transpose(1, 2, 0)
+    bias_rows = qkv_bias[:, :, None]
+    quarter = HD // 4
+    feature = jnp.arange(HD)
+    inverse = jnp.exp(
+        (feature % quarter).astype(jnp.float32) * (-math.log(rope_base) / quarter)
+    )[:, None]
+    position = jnp.arange(local_rows)
+
+    def tables(tile):
+        rows = (tile * row_count + position // columns).astype(jnp.float32)[None]
+        cols = (position % columns).astype(jnp.float32)[None]
+        angles = jnp.where((feature < 2 * quarter)[:, None], rows, cols) * inverse
+        return jnp.cos(angles), jnp.sin(angles)
+
+    gain_first, gain_second = norm1_gain[None], norm2_gain[None]
+    head_rows = (heads, HD, local_rows)
+    weight_scratch = pltpu.VMEM(weight_rows.shape, jnp.bfloat16)
+    params = pltpu.CompilerParams(vmem_limit_bytes=28 * 2**20)
+    macs = local_rows * width_vit * heads * HD
+    own_heads = pl.pallas_call(
+        partial(own_heads_kernel, heads),
+        out_shape=jax.ShapeDtypeStruct((3, *head_rows), jnp.bfloat16),
+        in_specs=[vmem_spec] * 5 + [any_spec],
+        out_specs=vmem_spec,
+        scratch_shapes=[weight_scratch, pltpu.SemaphoreType.DMA((3,))],
+        compiler_params=params,
+        cost_estimate=pl.CostEstimate(
+            flops=6 * macs, bytes_accessed=2 * weight_rows.size, transcendentals=0
+        ),
+        name="own_heads",
+    )(own_patches, gain_first, bias_rows, *tables(tile_id), weight_rows)
+    other_part, keys_values = pl.pallas_call(
+        partial(other_rows_kernel, heads),
+        out_shape=(
+            jax.ShapeDtypeStruct((local_rows, width_vit), jnp.bfloat16),
+            jax.ShapeDtypeStruct((2, heads, HD, 2 * local_rows), jnp.bfloat16),
+        ),
+        in_specs=[vmem_spec] * 6 + [any_spec] * 2,
+        out_specs=(vmem_spec, vmem_spec),
+        scratch_shapes=[
+            weight_scratch,
+            pltpu.VMEM(out_weight.shape, jnp.bfloat16),
+            pltpu.SemaphoreType.DMA((4,)),
+        ],
+        compiler_params=params,
+        cost_estimate=pl.CostEstimate(
+            flops=10 * macs, bytes_accessed=2 * weight_rows.size, transcendentals=0
+        ),
+        name="other_rows",
+    )(
+        other_patches,
+        gain_first,
+        bias_rows,
+        *tables(1 - tile_id),
+        own_heads,
+        weight_rows,
         out_weight,
-        preferred_element_type=jnp.float32,
-    ).astype(jnp.bfloat16)
+    )
     arrived_part = swap(other_part, flips=(1, 0, 0, 0))
-    own_part = jnp.dot(
-        attend_rows(own_query, keys, values, math.sqrt(HD)),
-        out_weight,
-        preferred_element_type=jnp.float32,
-    )
-    hidden = (
-        own_patches.astype(jnp.float32) + own_part + arrived_part.astype(jnp.float32) + out_bias
-    )
-    normed_out = layer_norm(hidden, norm2_gain).astype(jnp.bfloat16)
+    hidden = pl.pallas_call(
+        partial(own_rows_kernel, heads),
+        out_shape=jax.ShapeDtypeStruct((local_rows, width_vit), jnp.float32),
+        in_specs=[vmem_spec] * 5,
+        out_specs=vmem_spec,
+        compiler_params=params,
+        cost_estimate=pl.CostEstimate(
+            flops=4 * macs, bytes_accessed=2 * out_weight.size, transcendentals=0
+        ),
+        name="own_rows",
+    )(own_patches, own_heads, keys_values, out_weight, out_bias[None])
+    merged_shape = jax.ShapeDtypeStruct((token_count, 2 * width_vit), jnp.bfloat16)
+    kept, given = pl.pallas_call(
+        partial(merge_kernel, columns),
+        out_shape=(merged_shape, merged_shape),
+        in_specs=[smem_spec] + [vmem_spec] * 3,
+        out_specs=(vmem_spec, vmem_spec),
+        scratch_shapes=[pltpu.VMEM((width_vit // 128, local_rows, 128), jnp.float32)],
+        compiler_params=params,
+        name="merge_windows",
+    )(
+        (outer_id // (outer // 2)).astype(jnp.int32).reshape(1),
+        hidden,
+        arrived_part,
+        gain_second,
+    )
 
     far = outer // 2
-    parity_half = local_rows // 2
-    first, second = normed_out[:parity_half], normed_out[parity_half:]
-    upper = outer_id // far
-    kept, given = by_place(upper, first, second)
     from_far = swap(given, flips=(0, far, 0, 0))
     from_both = swap(given, flips=(1, far, 0, 0))
     from_tile = swap(kept, flips=(1, 0, 0, 0))
     page_tokens = 2 * token_count
-
-    def project(mine, other):
-        features = jnp.concatenate(by_place(tile_id, mine, other), axis=0).reshape(
-            2, 2, token_count, width_vit
-        )
-        features = jnp.concatenate([features[:, 0], features[:, 1]], axis=-1)
-        return jnp.dot(
-            features.reshape(page_tokens, 2 * width_vit),
-            proj_half,
-            preferred_element_type=jnp.float32,
-        )
-
-    far_part = swap(project(from_far, from_both).astype(jnp.bfloat16), flips=(0, far, 0, 0))
-    tokens_half = (project(kept, from_tile) + far_part.astype(jnp.float32)).astype(jnp.bfloat16)
+    project = partial(run_projector, proj_spots, tile_place, weights=proj_blocks)
+    far_part = swap(project(from_far, from_both, dtype=jnp.bfloat16), flips=(0, far, 0, 0))
+    tokens_half = (
+        project(kept, from_tile, dtype=jnp.float32) + far_part.astype(jnp.float32)
+    ).astype(jnp.bfloat16)
 
     width_moe = 2 * tokens_half.shape[1]
-    expert_gate, expert_up = expert_in[0, :, 0].T, expert_in[0, :, 1].T
-    shared_gate, shared_up = shared_in[:, 0].T, shared_in[:, 1].T
-    tile_place = tile_id.astype(jnp.int32).reshape(1)
+    expert_units = expert_in[0].transpose(1, 2, 0)
+    shared_units = shared_in.transpose(1, 2, 0)
     gain_row, lane_row = moe_gain[None], expert_lanes[None]
     half_moe = tokens_half.shape[1]
     held = jnp.concatenate([tokens_half, gate_rows], axis=1)
@@ -557,7 +720,7 @@
             arrived = swap(held, flips=flip)
             if step == 0 and flip == tile_flip:
                 extra = run_shared(
-                    tile_place, held, arrived, gain_row, shared_gate, shared_up, shared_out
+                    tile_place, held, arrived, gain_row, shared_units, shared_out
                 )
                 residual = jnp.concatenate(
                     by_place(
@@ -581,8 +744,7 @@
                 swap(held, flips=core_flip),
                 gain_row,
                 lane_row,
-                expert_gate,
-                expert_up,
+                expert_units,
                 expert_out[0],
                 extra,
             )

time: 169 us -> 156 us (0.923)
  matrix products: 21.5 us -> 0 us
  Pallas kernels: 21.7 us -> 41.6 us
  local copies, waits for them, and re-layouts: 25.2 us -> 9.43 us
  waiting for transfers between devices: 49 us -> 54.5 us
  other arithmetic: 6.47 us -> 2.83 us
  starting transfers between devices: 44 us -> 46.1 us
    pallas_call x0 -> x6, Pallas kernels: none -> 19.7 us  [the longest x2 7.11 us: run_projector(): pl.pallas_call(projector_kernel, out_shape=jax.ShapeDtypeStruct((rows, wi...]
    dot_general x8 -> x0, matrix products: 18.4 us -> none  [the longest x2 7.14 us: project(): jnp.dot(features.reshape(page_tokens, 2 * width_vit), proj_half, preferre...]
    dynamic_update_slice x8 -> x0, local copies, waits for them, and re-layouts: 11.2 us -> none  [per_device_near(): lax.dynamic_update_slice_in_dim(proj_half, block, spot * shard_rows, axis=0)]
    transpose x2 -> x0, local copies, waits for them, and re-layouts: 7.23 us -> none  [the longest x1 6.25 us: per_device_near(): shared_gate, shared_up = (shared_in[:, 0].T, shared_in[:, 1].T)]
    unnamed x41, local copies, waits for them, and re-layouts: 0.09 us -> 7.09 us
    ppermute x43, waiting for transfers between devices: 49 us -> 54.5 us  [near_swap(): return lax.ppermute(values, ('tile', 'expert'), pairs)]
    sub x2 -> x0, matrix products: 3.1 us -> none  [attend_rows(): weights = jax.nn.softmax(scores, axis=-1).astype(jnp.bfloat16)]
    ppermute x43, starting transfers between devices: 44 us -> 46.1 us  [near_swap(): return lax.ppermute(values, ('tile', 'expert'), pairs)]
  transfers between devices with their start and end apart: 43 -> 43, of which waited for: 12 -> 12; matrix products, arithmetic and copies ran while one was open for 26% -> 3% of each run, Pallas kernels for 13% -> 27%
where the time goes in v3:
time: 156 us; the launch traced here: 155 us
  waiting for transfers between devices  54.5 us (35%)
  starting transfers between devices  46.1 us (30%)
  Pallas kernels  41.6 us (27%)
  local copies, waits for them, and re-layouts  9.43 us (6%)
  other arithmetic  2.83 us (2%)
    ppermute x43, waiting for transfers between devices, near_swap(): return lax.ppermute(values, ('tile', 'expert'), pairs)  54.5 us
    ppermute x43, starting transfers between devices, near_swap(): return lax.ppermute(values, ('tile', 'expert'), pairs)  46.1 us
    pallas_call x4, Pallas kernels, run_expert(): pl.pallas_call(partial(expert_kernel, pieces, extra is not None), out_sha...  18 us
    pallas_call x2, Pallas kernels, run_projector(): pl.pallas_call(projector_kernel, out_shape=jax.ShapeDtypeStruct((rows, wi...  7.11 us
    unnamed x41, local copies, waits for them, and re-layouts  7.09 us
    pallas_call x1, Pallas kernels, per_device_near(): pl.pallas_call(partial(other_rows_kernel, heads), out_shape=(jax.ShapeDty...  6 us
    pallas_call x1, Pallas kernels, run_shared(): pl.pallas_call(partial(shared_kernel, pieces), out_shape=jax.ShapeDtypeSt...  3.86 us
  transfers between devices with their start and end apart: 43, of which 12 were waited for; matrix products, arithmetic and copies ran while one was open for 3% of the time, Pallas kernels for 27%

profile of v3, /device:TPU:0, one launch (start us, length us, event | category | flops | bytes accessed | tf_op | source)
XLA Modules:
  0.0 155.2 jit_solution(5464353491820343646)
XLA Ops:
  0.0 3.0 %collective-permute-start.4 = (bf16[288,1024]{1,0:T(8,128)(2,1)}, bf16[288,1024]{1,0:T(8,128)(2,1)}, u32[]{:S(2)}, u32[]{:S(2)}) collective-permute-start(bf16[288,1024]{1,0:T(8,128)(2,1)} %refs_0_.3), channel_id=1, source_target_pairs={{0,2},{1,3},{2,0},{3,1},{4,6},{5,7},{6,4},{7,5},{8,10},{9,11},{10,... | collective-permute-start | bytes 1769480 | tf_op jit(solution)/shard_map/ppermute | solution.py:218
  11.7 2.7 %own_heads.1.refs_5_.refs_1_ = bf16[3,8,72,128]{3,2,1,0:T(8,128)(2,1)S(1)} custom-call(bf16[128,1152]{1,0:T(8,128)(2,1)S(1)} %bitcast.137, f32[1,1152]{1,0:T(1,128)S(1)} %broadcast_in_dim.81.refs_1_, f32[3,576,1]{2,1,0:T(8,128)S(1)} %copy.53.refs_2_, f32[72,128]{1,0:T(8,128)S(1)} %get-tuple-element.53.refs_3_, f32[72,128]{1,0:T(8,128)S(1)} %get-tuple-element.54.refs_4_, ...), custom_call_target="tpu_custom_call" | custom-call | flops 509607936 | bytes 3981312 | tf_op jit(solution)/shard_map/own_heads/pallas_call | solution.py:630
  14.4 6.0 %other_rows.1 = (bf16[128,1152]{1,0:T(8,128)(2,1)}, bf16[2,8,72,256]{3,2,1,0:T(8,128)(2,1)S(1)}) custom-call(bf16[128,1152]{1,0:T(8,128)(2,1)S(1)} %collective-permute-done.refs_0_, f32[1,1152]{1,0:T(1,128)S(1)} %broadcast_in_dim.81.refs_1_, f32[3,576,1]{2,1,0:T(8,128)S(1)} %copy.53.refs_2_, f32[72,128]{1,0:T(8,128)S(1)} %get-tuple-element.50.refs_3_, ...), custom_call_target="tpu_custom_call" | custom-call | flops 849346560 | bytes 3981312 | tf_op jit(solution)/shard_map/other_rows/pallas_call | solution.py:642
  23.4 7.1 %collective-permute-done.8.refs_6_ = bf16[288,1024]{1,0:T(8,128)(2,1)} collective-permute-done((bf16[288,1024]{1,0:T(8,128)(2,1)}, bf16[288,1024]{1,0:T(8,128)(2,1)}, u32[]{:S(2)}, u32[]{:S(2)}) %collective-permute-start.8) | collective-permute-done | bytes 589856 | tf_op jit(solution)/shard_map/ppermute | solution.py:218
  32.7 2.6 %own_rows.1.refs_1_ = f32[128,1152]{1,0:T(8,128)S(1)} custom-call(bf16[128,1152]{1,0:T(8,128)(2,1)S(1)} %bitcast.138, bf16[3,8,72,128]{3,2,1,0:T(8,128)(2,1)S(1)} %own_heads.1.refs_5_.refs_1_, bf16[2,8,72,256]{3,2,1,0:T(8,128)(2,1)S(1)} %copy-done.10, bf16[576,1152]{1,0:T(8,128)(2,1)S(1)} %copy-done.3, f32[1,1152]{1,0:T(1,128)S(1)} %broadcast_in_dim.87.refs_4_), custom_call_target="tpu_custom_call" | custom-call | flops 339738624 | bytes 1327104 | tf_op jit(solution)/shard_map/own_rows/pallas_call | solution.py:670
  36.7 2.8 %collective-permute-start.10 = (bf16[32,2304]{1,0:T(8,128)(2,1)S(1)}, bf16[32,2304]{1,0:T(8,128)(2,1)S(1)}, u32[]{:S(2)}, u32[]{:S(2)}) collective-permute-start(bf16[32,2304]{1,0:T(8,128)(2,1)S(1)} %get-tuple-element.20), channel_id=1, source_target_pairs={{0,8},{1,9},{2,10},{3,11},{4,12},{5,13},{6,14},{7,15},{8,0},{9,1},... | collective-permute-start | bytes 442376 | tf_op jit(solution)/shard_map/ppermute | solution.py:218
  41.0 9.6 %collective-permute-done.10.mine_ref = bf16[32,2304]{1,0:T(8,128)(2,1)S(1)} collective-permute-done((bf16[32,2304]{1,0:T(8,128)(2,1)S(1)}, bf16[32,2304]{1,0:T(8,128)(2,1)S(1)}, u32[]{:S(2)}, u32[]{:S(2)}) %collective-permute-start.10) | collective-permute-done | bytes 147488 | tf_op jit(solution)/shard_map/ppermute | solution.py:218
  55.6 3.6 %projector.3 = bf16[64,1024]{1,0:T(8,128)(2,1)S(1)} custom-call(s32[8]{0:T(128)S(1)} %stack.107.spots_ref, s32[1]{0:T(128)} %bitcast.8.place_ref.refs_0_, bf16[32,2304]{1,0:T(8,128)(2,1)S(1)} %collective-permute-done.10.mine_ref, bf16[32,2304]{1,0:T(8,128)(2,1)S(1)} %collective-permute-done.11.other_ref, bf16[288,1024]{1,0:T(8,128)(2,1)S(1)} %copy-done.5, ...), custom_call_target="tpu_custom_call" | custom-call | flops 301989888 | bytes 4718592 | tf_op jit(solution)/shard_map/projector/pallas_call | solution.py:523
  59.4 3.6 %projector.2 = f32[64,1024]{1,0:T(8,128)S(1)} custom-call(s32[8]{0:T(128)S(1)} %stack.107.spots_ref, s32[1]{0:T(128)} %bitcast.8.place_ref.refs_0_, bf16[32,2304]{1,0:T(8,128)(2,1)S(1)} %get-tuple-element.19.mine_ref, bf16[32,2304]{1,0:T(8,128)(2,1)S(1)} %collective-permute-done.2.other_ref, bf16[288,1024]{1,0:T(8,128)(2,1)S(1)} %copy-done.6, ...), custom_call_target="tpu_custom_call" | custom-call | flops 301989888 | bytes 4718592 | tf_op jit(solution)/shard_map/projector/pallas_call | solution.py:523
  63.0 5.0 %collective-permute-done.12 = bf16[64,1024]{1,0:T(8,128)(2,1)S(1)} collective-permute-done((bf16[64,1024]{1,0:T(8,128)(2,1)S(1)}, bf16[64,1024]{1,0:T(8,128)(2,1)S(1)}, u32[]{:S(2)}, u32[]{:S(2)}) %collective-permute-start.12) | collective-permute-done | bytes 131104 | tf_op jit(solution)/shard_map/ppermute | solution.py:218
  70.5 2.6 %collective-permute-start.35 = (bf16[64,1152]{1,0:T(8,128)(2,1)S(1)}, bf16[64,1152]{1,0:T(8,128)(2,1)S(1)}, u32[]{:S(2)}, u32[]{:S(2)}) collective-permute-start(bf16[64,1152]{1,0:T(8,128)(2,1)S(1)} %get-tuple-element.44.refs_1_), channel_id=1, source_target_pairs={{0,12},{1,13},{2,14},{3,15},{4,8},{5,9},{6,10},{7,11},{8,4},{9,5},... | collective-permute-start | bytes 442376 | tf_op jit(solution)/shard_map/ppermute | solution.py:218
  76.4 5.5 %collective-permute-done.27 = bf16[64,1152]{1,0:T(8,128)(2,1)S(1)} collective-permute-done((bf16[64,1152]{1,0:T(8,128)(2,1)S(1)}, bf16[64,1152]{1,0:T(8,128)(2,1)S(1)}, u32[]{:S(2)}, u32[]{:S(2)}) %collective-permute-start.27) | collective-permute-done | bytes 147488 | tf_op jit(solution)/shard_map/ppermute | solution.py:218
  84.5 3.9 %shared_units.1.refs_7_ = f32[64,2048]{1,0:T(8,128)S(1)} custom-call(s32[1]{0:T(128)} %bitcast.8.place_ref.refs_0_, bf16[64,1152]{1,0:T(8,128)(2,1)S(1)} %get-tuple-element.44.refs_1_, bf16[64,1152]{1,0:T(8,128)(2,1)S(1)} %collective-permute-done.13.refs_2_, f32[1,2048]{1,0:T(1,128)S(1)} %bitcast.139, bf16[2,704,2048]{2,1,0:T(8,128)(2,1)S(1)} %bitcast.134, ...), custom_call_target="tpu_custom_call" | custom-call | flops 553648128 | bytes 9175040 | tf_op jit(solution)/shard_map/shared_units/pallas_call | solution.py:366
  91.5 6.3 %collective-permute-done.21 = bf16[2,64,1152]{2,1,0:T(8,128)(2,1)S(1)} collective-permute-done((bf16[2,64,1152]{2,1,0:T(8,128)(2,1)S(1)}, bf16[2,64,1152]{2,1,0:T(8,128)(2,1)S(1)}, u32[]{:S(2)}, u32[]{:S(2)}) %collective-permute-start.21) | collective-permute-done | bytes 294944 | tf_op jit(solution)/shard_map/ppermute | solution.py:218
  101.1 4.5 %expert_units.4 = (bf16[2,64,2048]{2,1,0:T(8,128)(2,1)S(1)}, bf16[2,64,2048]{2,1,0:T(8,128)(2,1)S(1)}) custom-call(s32[1]{0:T(128)} %bitcast.8.place_ref.refs_0_, bf16[2,2,64,1152]{3,2,1,0:T(8,128)(2,1)S(1)} %pad_maximum_fusion.refs_1_, bf16[2,2,64,1152]{3,2,1,0:T(8,128)(2,1)S(1)} %collective-permute-done.15.refs_2_, f32[1,2048]{1,0:T(1,128)S(1)} %bitcast.140, ...), custom_call_target="tpu_custom_call" | custom-call | flops 2214592512 | bytes 10747904 | tf_op jit(solution)/shard_map/expert_units/pallas_call | solution.py:334
  106.1 4.4 %expert_units.5 = (bf16[2,64,2048]{2,1,0:T(8,128)(2,1)S(1)}, bf16[2,64,2048]{2,1,0:T(8,128)(2,1)S(1)}) custom-call(s32[1]{0:T(128)} %bitcast.8.place_ref.refs_0_, bf16[2,2,64,1152]{3,2,1,0:T(8,128)(2,1)S(1)} %copy.60.refs_1_, bf16[2,2,64,1152]{3,2,1,0:T(8,128)(2,1)S(1)} %copy.61.refs_2_, f32[1,2048]{1,0:T(1,128)S(1)} %bitcast.141, ...), custom_call_target="tpu_custom_call" | custom-call | flops 2214592512 | bytes 10747904 | tf_op jit(solution)/shard_map/expert_units/pallas_call | solution.py:334
  110.7 4.7 %expert_units.6 = (bf16[2,64,2048]{2,1,0:T(8,128)(2,1)S(1)}, bf16[2,64,2048]{2,1,0:T(8,128)(2,1)S(1)}) custom-call(s32[1]{0:T(128)} %bitcast.8.place_ref.refs_0_, bf16[2,2,64,1152]{3,2,1,0:T(8,128)(2,1)S(1)} %pad_maximum_fusion.1.refs_1_, bf16[2,2,64,1152]{3,2,1,0:T(8,128)(2,1)S(1)} %collective-permute-done.30.refs_2_, f32[1,2048]{1,0:T(1,128)S(1)} %bitcast.142, ...), custom_call_target="tpu_custom_call" | custom-call | flops 2214592512 | bytes 10747904 | tf_op jit(solution)/shard_map/expert_units/pallas_call | solution.py:334
  115.9 4.4 %expert_units.7 = (bf16[2,64,2048]{2,1,0:T(8,128)(2,1)S(1)}, bf16[2,64,2048]{2,1,0:T(8,128)(2,1)S(1)}) custom-call(s32[1]{0:T(128)} %bitcast.8.place_ref.refs_0_, bf16[2,2,64,1152]{3,2,1,0:T(8,128)(2,1)S(1)} %maximum_bitcast_fusion.1.refs_1_, bf16[2,2,64,1152]{3,2,1,0:T(8,128)(2,1)S(1)} %collective-permute-done.38.refs_2_, f32[1,2048]{1,0:T(1,128)S(1)} %bitcast.143, ...), custom_call_target="tpu_custom_call" | custom-call | flops 2214592512 | bytes 10747904 | tf_op jit(solution)/shard_map/expert_units/pallas_call | solution.py:334
  125.5 4.3 %collective-permute-done.17 = bf16[2,32,2048]{2,1,0:T(8,128)(2,1)S(1)} collective-permute-done((bf16[2,32,2048]{2,1,0:T(8,128)(2,1)S(1)}, bf16[2,32,2048]{2,1,0:T(8,128)(2,1)S(1)}, u32[]{:S(2)}, u32[]{:S(2)}) %collective-permute-start.17) | collective-permute-done | bytes 262176 | tf_op jit(solution)/shard_map/ppermute | solution.py:218
  132.3 3.1 %collective-permute-done.32 = bf16[2,32,2048]{2,1,0:T(8,128)(2,1)S(1)} collective-permute-done((bf16[2,32,2048]{2,1,0:T(8,128)(2,1)S(1)}, bf16[2,32,2048]{2,1,0:T(8,128)(2,1)S(1)}, u32[]{:S(2)}, u32[]{:S(2)}) %collective-permute-start.32) | collective-permute-done | bytes 262176 | tf_op jit(solution)/shard_map/ppermute | solution.py:218
  138.0 2.3 %collective-permute-start.26 = (bf16[32,2048]{1,0:T(8,128)(2,1)S(1)}, bf16[32,2048]{1,0:T(8,128)(2,1)S(1)}, u32[]{:S(2)}, u32[]{:S(2)}) collective-permute-start(bf16[32,2048]{1,0:T(8,128)(2,1)S(1)} %fusion.6), channel_id=1, source_target_pairs={{0,4},{1,5},{2,6},{3,7},{4,0},{5,1},{6,2},{7,3},{8,12},{9,13},{10,... | collective-permute-start | bytes 393224 | tf_op jit(solution)/shard_map/ppermute | solution.py:218
  140.9 3.5 %collective-permute-start.34 = (bf16[32,2048]{1,0:T(8,128)(2,1)S(1)}, bf16[32,2048]{1,0:T(8,128)(2,1)S(1)}, u32[]{:S(2)}, u32[]{:S(2)}) collective-permute-start(bf16[32,2048]{1,0:T(8,128)(2,1)S(1)} %fusion.5), channel_id=1, source_target_pairs={{0,8},{1,9},{2,10},{3,11},{4,12},{5,13},{6,14},{7,15},{8,0},{9,1},... | collective-permute-start | bytes 393224 | tf_op jit(solution)/shard_map/ppermute | solution.py:218
  144.5 2.6 %collective-permute-start.42 = (bf16[32,2048]{1,0:T(8,128)(2,1)S(1)}, bf16[32,2048]{1,0:T(8,128)(2,1)S(1)}, u32[]{:S(2)}, u32[]{:S(2)}) collective-permute-start(bf16[32,2048]{1,0:T(8,128)(2,1)S(1)} %fusion.4), channel_id=1, source_target_pairs={{0,12},{1,13},{2,14},{3,15},{4,8},{5,9},{6,10},{7,11},{8,4},{9,5},... | collective-permute-start | bytes 393224 | tf_op jit(solution)/shard_map/ppermute | solution.py:218
  147.2 7.2 %collective-permute-done.34 = bf16[32,2048]{1,0:T(8,128)(2,1)S(1)} collective-permute-done((bf16[32,2048]{1,0:T(8,128)(2,1)S(1)}, bf16[32,2048]{1,0:T(8,128)(2,1)S(1)}, u32[]{:S(2)}, u32[]{:S(2)}) %collective-permute-start.34) | collective-permute-done | bytes 131104 | tf_op jit(solution)/shard_map/ppermute | solution.py:218
  (170 shorter events, 49.2 us)
Async XLA Ops:
  0.0 22.9 %collective-permute-start.4 = (bf16[288,1024]{1,0:T(8,128)(2,1)}, bf16[288,1024]{1,0:T(8,128)(2,1)}, u32[]{:S(2)}, u32[]{:S(2)}) collective-permute-start(bf16[288,1024]{1,0:T(8,128)(2,1)} %refs_0_.3), channel_id=1, source_target_pairs={{0,2},{1,3},{2,0},{3,1},{4,6},{5,7},{6,4},{7,5},{8,10},{9,11},{10,... | collective-permute-start | bytes 1769480 | tf_op jit(solution)/shard_map/ppermute | solution.py:218
  3.0 20.0 %collective-permute-start.6 = (bf16[288,1024]{1,0:T(8,128)(2,1)}, bf16[288,1024]{1,0:T(8,128)(2,1)}, u32[]{:S(2)}, u32[]{:S(2)}) collective-permute-start(bf16[288,1024]{1,0:T(8,128)(2,1)} %refs_0_.3), channel_id=1, source_target_pairs={{0,4},{1,5},{2,6},{3,7},{4,0},{5,1},{6,2},{7,3},{8,12},{9,13},{10,... | collective-permute-start | bytes 1769480 | tf_op jit(solution)/shard_map/ppermute | solution.py:218
  4.5 26.0 %collective-permute-start.8 = (bf16[288,1024]{1,0:T(8,128)(2,1)}, bf16[288,1024]{1,0:T(8,128)(2,1)}, u32[]{:S(2)}, u32[]{:S(2)}) collective-permute-start(bf16[288,1024]{1,0:T(8,128)(2,1)} %refs_0_.3), channel_id=1, source_target_pairs={{0,6},{1,7},{2,4},{3,5},{4,2},{5,3},{6,0},{7,1},{8,14},{9,15},{10,... | collective-permute-start | bytes 1769480 | tf_op jit(solution)/shard_map/ppermute | solution.py:218
  4.5 35.2 %collective-permute-start.3 = (bf16[288,1024]{1,0:T(8,128)(2,1)}, bf16[288,1024]{1,0:T(8,128)(2,1)}, u32[]{:S(2)}, u32[]{:S(2)}) collective-permute-start(bf16[288,1024]{1,0:T(8,128)(2,1)} %refs_0_.3), channel_id=1, source_target_pairs={{0,1},{1,0},{2,3},{3,2},{4,5},{5,4},{6,7},{7,6},{8,9},{9,8},{10,11... | collective-permute-start | bytes 1769480 | tf_op jit(solution)/shard_map/ppermute | solution.py:218
  21.3 14.0 %collective-permute-start.1 = (bf16[128,1152]{1,0:T(8,128)(2,1)}, bf16[128,1152]{1,0:T(8,128)(2,1)}, u32[]{:S(2)}, u32[]{:S(2)}) collective-permute-start(bf16[128,1152]{1,0:T(8,128)(2,1)} %get-tuple-element.18), channel_id=1, source_target_pairs={{0,16},{1,17},{2,18},{3,19},{4,20},{5,21},{6,22},{7,23},{8,24},{9,... | collective-permute-start | bytes 884744 | tf_op jit(solution)/shard_map/ppermute | solution.py:218
  22.9 31.6 %collective-permute-start.5 = (bf16[288,1024]{1,0:T(8,128)(2,1)}, bf16[288,1024]{1,0:T(8,128)(2,1)}, u32[]{:S(2)}, u32[]{:S(2)}) collective-permute-start(bf16[288,1024]{1,0:T(8,128)(2,1)} %collective-permute-done.4.refs_2_), channel_id=1, source_target_pairs={{0,1},{1,0},{2,3},{3,2},{4,5},{5,4},{6,7},{7,6},{8,9},{9,8},{10,11... | collective-permute-start | bytes 1769480 | tf_op jit(solution)/shard_map/ppermute | solution.py:218
  22.9 31.6 %collective-permute-start.7 = (bf16[288,1024]{1,0:T(8,128)(2,1)}, bf16[288,1024]{1,0:T(8,128)(2,1)}, u32[]{:S(2)}, u32[]{:S(2)}) collective-permute-start(bf16[288,1024]{1,0:T(8,128)(2,1)} %collective-permute-done.6.refs_4_), channel_id=1, source_target_pairs={{0,1},{1,0},{2,3},{3,2},{4,5},{5,4},{6,7},{7,6},{8,9},{9,8},{10,11... | collective-permute-start | bytes 1769480 | tf_op jit(solution)/shard_map/ppermute | solution.py:218
  30.5 24.0 %collective-permute-start.9 = (bf16[288,1024]{1,0:T(8,128)(2,1)}, bf16[288,1024]{1,0:T(8,128)(2,1)}, u32[]{:S(2)}, u32[]{:S(2)}) collective-permute-start(bf16[288,1024]{1,0:T(8,128)(2,1)} %collective-permute-done.8.refs_6_), channel_id=1, source_target_pairs={{0,1},{1,0},{2,3},{3,2},{4,5},{5,4},{6,7},{7,6},{8,9},{9,8},{10,11... | collective-permute-start | bytes 1769480 | tf_op jit(solution)/shard_map/ppermute | solution.py:218
  36.7 13.9 %collective-permute-start.10 = (bf16[32,2304]{1,0:T(8,128)(2,1)S(1)}, bf16[32,2304]{1,0:T(8,128)(2,1)S(1)}, u32[]{:S(2)}, u32[]{:S(2)}) collective-permute-start(bf16[32,2304]{1,0:T(8,128)(2,1)S(1)} %get-tuple-element.20), channel_id=1, source_target_pairs={{0,8},{1,9},{2,10},{3,11},{4,12},{5,13},{6,14},{7,15},{8,0},{9,1},... | collective-permute-start | bytes 442376 | tf_op jit(solution)/shard_map/ppermute | solution.py:218
  39.7 14.8 %collective-permute-start.11 = (bf16[32,2304]{1,0:T(8,128)(2,1)S(1)}, bf16[32,2304]{1,0:T(8,128)(2,1)S(1)}, u32[]{:S(2)}, u32[]{:S(2)}) collective-permute-start(bf16[32,2304]{1,0:T(8,128)(2,1)S(1)} %get-tuple-element.20), channel_id=1, source_target_pairs={{0,24},{1,25},{2,26},{3,27},{4,28},{5,29},{6,30},{7,31},{8,16},{9,... | collective-permute-start | bytes 442376 | tf_op jit(solution)/shard_map/ppermute | solution.py:218
  68.8 13.2 %collective-permute-start.27 = (bf16[64,1152]{1,0:T(8,128)(2,1)S(1)}, bf16[64,1152]{1,0:T(8,128)(2,1)S(1)}, u32[]{:S(2)}, u32[]{:S(2)}) collective-permute-start(bf16[64,1152]{1,0:T(8,128)(2,1)S(1)} %get-tuple-element.44.refs_1_), channel_id=1, source_target_pairs={{0,8},{1,9},{2,10},{3,11},{4,12},{5,13},{6,14},{7,15},{8,0},{9,1},... | collective-permute-start | bytes 442376 | tf_op jit(solution)/shard_map/ppermute | solution.py:218
  70.5 12.5 %collective-permute-start.35 = (bf16[64,1152]{1,0:T(8,128)(2,1)S(1)}, bf16[64,1152]{1,0:T(8,128)(2,1)S(1)}, u32[]{:S(2)}, u32[]{:S(2)}) collective-permute-start(bf16[64,1152]{1,0:T(8,128)(2,1)S(1)} %get-tuple-element.44.refs_1_), channel_id=1, source_target_pairs={{0,12},{1,13},{2,14},{3,15},{4,8},{5,9},{6,10},{7,11},{8,4},{9,5},... | collective-permute-start | bytes 442376 | tf_op jit(solution)/shard_map/ppermute | solution.py:218
  74.3 14.1 %collective-permute-start.20 = (bf16[64,1152]{1,0:T(8,128)(2,1)S(1)}, bf16[64,1152]{1,0:T(8,128)(2,1)S(1)}, u32[]{:S(2)}, u32[]{:S(2)}) collective-permute-start(bf16[64,1152]{1,0:T(8,128)(2,1)S(1)} %collective-permute-done.19), channel_id=1, source_target_pairs={{0,2},{1,3},{2,0},{3,1},{4,6},{5,7},{6,4},{7,5},{8,10},{9,11},{10,... | collective-permute-start | bytes 442376 | tf_op jit(solution)/shard_map/ppermute | solution.py:218
  75.8 15.5 %collective-permute-start.14 = (bf16[2,64,1152]{2,1,0:T(8,128)(2,1)S(1)}, bf16[2,64,1152]{2,1,0:T(8,128)(2,1)S(1)}, u32[]{:S(2)}, u32[]{:S(2)}) collective-permute-start(bf16[2,64,1152]{2,1,0:T(8,128)(2,1)S(1)} %get-tuple-element.34), channel_id=1, source_target_pairs={{0,2},{1,3},{2,0},{3,1},{4,6},{5,7},{6,4},{7,5},{8,10},{9,11},{10,... | collective-permute-start | bytes 884744 | tf_op jit(solution)/shard_map/ppermute | solution.py:218
  90.2 10.7 %collective-permute-start.37 = (bf16[2,64,1152]{2,1,0:T(8,128)(2,1)S(1)}, bf16[2,64,1152]{2,1,0:T(8,128)(2,1)S(1)}, u32[]{:S(2)}, u32[]{:S(2)}) collective-permute-start(bf16[2,64,1152]{2,1,0:T(8,128)(2,1)S(1)} %get-tuple-element.40), channel_id=1, source_target_pairs={{0,16},{1,17},{2,18},{3,19},{4,20},{5,21},{6,22},{7,23},{8,24},{9,... | collective-permute-start | bytes 884744 | tf_op jit(solution)/shard_map/ppermute | solution.py:218
  98.0 12.7 %collective-permute-start.30 = (bf16[2,2,64,1152]{3,2,1,0:T(8,128)(2,1)S(1)}, bf16[2,2,64,1152]{3,2,1,0:T(8,128)(2,1)S(1)}, u32[]{:S(2)}, u32[]{:S(2)}) collective-permute-start(bf16[2,2,64,1152]{3,2,1,0:T(8,128)(2,1)S(1)} %pad_maximum_fusion.1.refs_1_), channel_id=1, source_target_pairs={{0,1},{1,0},{2,3},{3,2},{4,5},{5,4},{6,7},{7,6},{8,9},{9,8},{10,11... | collective-permute-start | bytes 1769480 | tf_op jit(solution)/shard_map/ppermute | solution.py:218
  101.0 15.0 %collective-permute-start.38 = (bf16[2,2,64,1152]{3,2,1,0:T(8,128)(2,1)S(1)}, bf16[2,2,64,1152]{3,2,1,0:T(8,128)(2,1)S(1)}, u32[]{:S(2)}, u32[]{:S(2)}) collective-permute-start(bf16[2,2,64,1152]{3,2,1,0:T(8,128)(2,1)S(1)} %maximum_bitcast_fusion.1.refs_1_), channel_id=1, source_target_pairs={{0,1},{1,0},{2,3},{3,2},{4,5},{5,4},{6,7},{7,6},{8,9},{9,8},{10,11... | collective-permute-start | bytes 1769480 | tf_op jit(solution)/shard_map/ppermute | solution.py:218
  105.5 14.9 %collective-permute-start.16 = (bf16[2,64,2048]{2,1,0:T(8,128)(2,1)S(1)}, bf16[2,64,2048]{2,1,0:T(8,128)(2,1)S(1)}, u32[]{:S(2)}, u32[]{:S(2)}) collective-permute-start(bf16[2,64,2048]{2,1,0:T(8,128)(2,1)S(1)} %get-tuple-element.22), channel_id=1, source_target_pairs={{0,1},{1,0},{2,3},{3,2},{4,5},{5,4},{6,7},{7,6},{8,9},{9,8},{10,11... | collective-permute-start | bytes 1572872 | tf_op jit(solution)/shard_map/ppermute | solution.py:218
  110.6 10.4 %collective-permute-start.23 = (bf16[2,64,2048]{2,1,0:T(8,128)(2,1)S(1)}, bf16[2,64,2048]{2,1,0:T(8,128)(2,1)S(1)}, u32[]{:S(2)}, u32[]{:S(2)}) collective-permute-start(bf16[2,64,2048]{2,1,0:T(8,128)(2,1)S(1)} %get-tuple-element.24), channel_id=1, source_target_pairs={{0,1},{1,0},{2,3},{3,2},{4,5},{5,4},{6,7},{7,6},{8,9},{9,8},{10,11... | collective-permute-start | bytes 1572872 | tf_op jit(solution)/shard_map/ppermute | solution.py:218
  122.5 12.9 %collective-permute-start.32 = (bf16[2,32,2048]{2,1,0:T(8,128)(2,1)S(1)}, bf16[2,32,2048]{2,1,0:T(8,128)(2,1)S(1)}, u32[]{:S(2)}, u32[]{:S(2)}) collective-permute-start(bf16[2,32,2048]{2,1,0:T(8,128)(2,1)S(1)} %select_bitcast_fusion), channel_id=1, source_target_pairs={{0,16},{1,17},{2,18},{3,19},{4,20},{5,21},{6,22},{7,23},{8,24},{9,... | collective-permute-start | bytes 786440 | tf_op jit(solution)/shard_map/ppermute | solution.py:218
  123.8 12.2 %collective-permute-start.40 = (bf16[2,32,2048]{2,1,0:T(8,128)(2,1)S(1)}, bf16[2,32,2048]{2,1,0:T(8,128)(2,1)S(1)}, u32[]{:S(2)}, u32[]{:S(2)}) collective-permute-start(bf16[2,32,2048]{2,1,0:T(8,128)(2,1)S(1)} %bitcast.155), channel_id=1, source_target_pairs={{0,2},{1,3},{2,0},{3,1},{4,6},{5,7},{6,4},{7,5},{8,10},{9,11},{10,... | collective-permute-start | bytes 786440 | tf_op jit(solution)/shard_map/ppermute | solution.py:218
  129.9 17.3 %collective-permute-start.18 = (bf16[32,2048]{1,0:T(8,128)(2,1)S(1)}, bf16[32,2048]{1,0:T(8,128)(2,1)S(1)}, u32[]{:S(2)}, u32[]{:S(2)}) collective-permute-start(bf16[32,2048]{1,0:T(8,128)(2,1)S(1)} %slice_bitcast_fusion.6), channel_id=1, source_target_pairs={{0,2},{1,3},{2,0},{3,1},{4,6},{5,7},{6,4},{7,5},{8,10},{9,11},{10,... | collective-permute-start | bytes 393224 | tf_op jit(solution)/shard_map/ppermute | solution.py:218
  140.9 13.5 %collective-permute-start.34 = (bf16[32,2048]{1,0:T(8,128)(2,1)S(1)}, bf16[32,2048]{1,0:T(8,128)(2,1)S(1)}, u32[]{:S(2)}, u32[]{:S(2)}) collective-permute-start(bf16[32,2048]{1,0:T(8,128)(2,1)S(1)} %fusion.5), channel_id=1, source_target_pairs={{0,8},{1,9},{2,10},{3,11},{4,12},{5,13},{6,14},{7,15},{8,0},{9,1},... | collective-permute-start | bytes 393224 | tf_op jit(solution)/shard_map/ppermute | solution.py:218
  144.5 9.9 %collective-permute-start.42 = (bf16[32,2048]{1,0:T(8,128)(2,1)S(1)}, bf16[32,2048]{1,0:T(8,128)(2,1)S(1)}, u32[]{:S(2)}, u32[]{:S(2)}) collective-permute-start(bf16[32,2048]{1,0:T(8,128)(2,1)S(1)} %fusion.4), channel_id=1, source_target_pairs={{0,12},{1,13},{2,14},{3,15},{4,8},{5,9},{6,10},{7,11},{8,4},{9,5},... | collective-permute-start | bytes 393224 | tf_op jit(solution)/shard_map/ppermute | solution.py:218
  (39 other events, 437.8 us)

commit v4 on v3

--- a/solution.py
+++ b/solution.py
@@ -204,6 +204,9 @@
     return output.astype(jnp.bfloat16).reshape(1, row_count // 2, columns // 2, width_moe)
 
 
+near_expert = ("half", "outer", "inner", "core")
+
+
 def near_swap(values, grid, flips):
     pairs = []
     for source in range(math.prod(grid)):
@@ -215,43 +218,19 @@
         for spot, size, flip in zip(reversed(place), grid, flips):
             target = target * size + (spot ^ flip)
         pairs.append((source, target))
-    return lax.ppermute(values, ("tile", "expert"), pairs)
-
-
-def unit_pieces(units):
-    cuts = list(range(0, units, 256)) + [units]
-    return list(zip(cuts[:-1], cuts[1:]))
-
-
-def fetch_units(pieces, sources, targets, arrivals):
-    copies = []
-    for number, (begin, end) in enumerate(pieces):
-        rows = pl.ds(begin, end - begin)
-        copies.append(
-            [
-                pltpu.make_async_copy(
-                    source.at[rows], target.at[rows], arrivals.at[number, which]
-                )
-                for which, (source, target) in enumerate(zip(sources, targets))
-            ]
-        )
-    for piece in copies:
-        for copy in piece:
-            copy.start()
-    return copies
-
-
-def expert_sums(pieces, copies, normed, gate_rows, up_rows, back_rows):
+    return lax.ppermute(values, ("tile", *near_expert), pairs)
+
+
+def expert_sums(normed, in_ref, back_ref):
+    units = back_ref.shape[0]
+    wide = (((1,), (1,)), ((), ()))
     total = None
-    for (begin, end), piece in zip(pieces, copies):
-        for copy in piece:
-            copy.wait()
-        rows = pl.ds(begin, end - begin)
-        wide = (((1,), (1,)), ((), ()))
-        gate = lax.dot_general(normed, gate_rows[rows], wide, preferred_element_type=jnp.float32)
-        up = lax.dot_general(normed, up_rows[rows], wide, preferred_element_type=jnp.float32)
+    for begin in range(0, units, 256):
+        rows = pl.ds(begin, min(256, units - begin))
+        gate = lax.dot_general(normed, in_ref[0, rows], wide, preferred_element_type=jnp.float32)
+        up = lax.dot_general(normed, in_ref[1, rows], wide, preferred_element_type=jnp.float32)
         hidden = (gate / (1.0 + jnp.exp(-gate)) * up).astype(jnp.bfloat16)
-        part = jnp.dot(hidden, back_rows[rows], preferred_element_type=jnp.float32)
+        part = jnp.dot(hidden, back_ref[rows], preferred_element_type=jnp.float32)
         total = part if total is None else total + part
     return total
 
@@ -280,19 +259,15 @@
             weights[rows] = jnp.sum(lanes * lanes_ref[...], axis=1, keepdims=True)
 
 
-def expert_kernel(pieces, extra, *refs):
-    place_ref, near_ref, across_ref, gain_ref, lanes_ref, in_hbm, back_hbm = refs[:7]
+def expert_kernel(extra, *refs):
+    place_ref, near_ref, across_ref, gain_ref, lanes_ref, in_ref, back_ref = refs[:7]
     extra_ref = refs[7] if extra else None
-    own_out, across_out, normed, weights, gate_rows, up_rows, back_rows, arrivals = refs[7 + extra :]
-    copies = fetch_units(
-        pieces, (in_hbm.at[0], in_hbm.at[1], back_hbm), (gate_rows, up_rows, back_rows), arrivals
-    )
+    own_out, across_out, normed, weights = refs[7 + extra :]
     page_refs = [
         (ref.at[inner, 0], ref.at[inner, 1]) for ref in (near_ref, across_ref) for inner in range(2)
     ]
     norm_pages(place_ref, page_refs, gain_ref, lanes_ref, normed, weights)
-    total = expert_sums(pieces, copies, normed[...], gate_rows, up_rows, back_rows)
-    total = total * weights[...]
+    total = expert_sums(normed[...], in_ref, back_ref) * weights[...]
     count = total.shape[0] // 4
     for page in range(4):
         rows = total[page * count : (page + 1) * count]
@@ -302,19 +277,13 @@
         target[page % 2] = rows.astype(jnp.bfloat16)
 
 
-def shared_kernel(pieces, *refs):
-    place_ref, mine_ref, other_ref, gain_ref, in_hbm, back_hbm = refs[:6]
-    out_ref, normed, gate_rows, up_rows, back_rows, arrivals = refs[6:]
-    copies = fetch_units(
-        pieces, (in_hbm.at[0], in_hbm.at[1], back_hbm), (gate_rows, up_rows, back_rows), arrivals
-    )
+def shared_kernel(place_ref, mine_ref, other_ref, gain_ref, in_ref, back_ref, out_ref, normed):
     norm_pages(place_ref, [(mine_ref, other_ref)], gain_ref, None, normed, None)
-    out_ref[...] = expert_sums(pieces, copies, normed[...], gate_rows, up_rows, back_rows)
+    out_ref[...] = expert_sums(normed[...], in_ref, back_ref)
 
 
 vmem_spec = pl.BlockSpec(memory_space=pltpu.VMEM)
 smem_spec = pl.BlockSpec(memory_space=pltpu.SMEM)
-any_spec = pl.BlockSpec(memory_space=pl.ANY)
 
 
 def expert_cost(rows, units, width):
@@ -329,22 +298,17 @@
     units, width = back_rows.shape
     page_rows = near.shape[2]
     rows = 4 * page_rows
-    pieces = unit_pieces(units)
     out = jax.ShapeDtypeStruct((2, page_rows, width), jnp.bfloat16)
     return pl.pallas_call(
-        partial(expert_kernel, pieces, extra is not None),
+        partial(expert_kernel, extra is not None),
         out_shape=(out, out),
-        in_specs=[smem_spec] + [vmem_spec] * 4 + [any_spec] * 2 + [vmem_spec] * (extra is not None),
+        in_specs=[smem_spec] + [vmem_spec] * (6 + (extra is not None)),
         out_specs=(vmem_spec, vmem_spec),
         scratch_shapes=[
             pltpu.VMEM((rows, width), jnp.bfloat16),
             pltpu.VMEM((rows, 1), jnp.float32),
-            pltpu.VMEM((units, width), jnp.bfloat16),
-            pltpu.VMEM((units, width), jnp.bfloat16),
-            pltpu.VMEM((units, width), jnp.bfloat16),
-            pltpu.SemaphoreType.DMA((len(pieces), 3)),
         ],
-        compiler_params=pltpu.CompilerParams(vmem_limit_bytes=28 * 2**20),
+        compiler_params=pltpu.CompilerParams(vmem_limit_bytes=16 * 2**20),
         cost_estimate=expert_cost(rows, units, width),
         name="expert_units",
     )(
@@ -362,33 +326,28 @@
 def run_shared(tile_place, mine, other, gain, in_rows, back_rows):
     units, width = back_rows.shape
     rows = mine.shape[0]
-    pieces = unit_pieces(units)
     return pl.pallas_call(
-        partial(shared_kernel, pieces),
+        shared_kernel,
         out_shape=jax.ShapeDtypeStruct((rows, width), jnp.float32),
-        in_specs=[smem_spec] + [vmem_spec] * 3 + [any_spec] * 2,
+        in_specs=[smem_spec] + [vmem_spec] * 5,
         out_specs=vmem_spec,
         scratch_shapes=[
             pltpu.VMEM((rows, width), jnp.bfloat16),
-            pltpu.VMEM((units, width), jnp.bfloat16),
-            pltpu.VMEM((units, width), jnp.bfloat16),
-            pltpu.VMEM((units, width), jnp.bfloat16),
-            pltpu.SemaphoreType.DMA((len(pieces), 3)),
         ],
-        compiler_params=pltpu.CompilerParams(vmem_limit_bytes=28 * 2**20),
+        compiler_params=pltpu.CompilerParams(vmem_limit_bytes=16 * 2**20),
         cost_estimate=expert_cost(rows, units, width),
         name="shared_units",
     )(tile_place, mine, other, gain, in_rows, back_rows)
 
 
-def project_heads(rows_ref, gain_ref, weight, bias_ref, cos_ref, sin_ref, heads):
+def project_heads(rows_ref, gain_ref, weight_ref, bias_ref, cos_ref, sin_ref, heads):
     normed = layer_norm(rows_ref[...].astype(jnp.float32), gain_ref[...]).astype(jnp.bfloat16)
     quarter = HD // 4
     outs = []
     for which in range(3):
         mixed = (
             lax.dot_general(
-                weight(which),
+                weight_ref[which],
                 normed,
                 (((1,), (1,)), ((), ())),
                 preferred_element_type=jnp.float32,
@@ -417,48 +376,25 @@
 
 
 def own_heads_kernel(heads, *refs):
-    rows_ref, gain_ref, bias_ref, cos_ref, sin_ref, weight_hbm, out_ref, weight, arrivals = refs
-    copies = [
-        pltpu.make_async_copy(weight_hbm.at[which], weight.at[which], arrivals.at[which])
-        for which in range(3)
-    ]
-    for copy in copies:
-        copy.start()
-
-    def fetched(which):
-        copies[which].wait()
-        return weight[which]
-
-    outs = project_heads(rows_ref, gain_ref, fetched, bias_ref, cos_ref, sin_ref, heads)
+    rows_ref, gain_ref, bias_ref, cos_ref, sin_ref, weight_ref, out_ref = refs
+    outs = project_heads(rows_ref, gain_ref, weight_ref, bias_ref, cos_ref, sin_ref, heads)
     for which, values in enumerate(outs):
         out_ref[which] = values
 
 
 def other_rows_kernel(heads, *refs):
-    rows_ref, gain_ref, bias_ref, cos_ref, sin_ref, own_ref, weight_hbm, back_hbm = refs[:8]
-    part_ref, keys_ref, weight, back, arrivals = refs[8:]
-    copies = [
-        pltpu.make_async_copy(weight_hbm.at[which], weight.at[which], arrivals.at[which])
-        for which in range(3)
-    ] + [pltpu.make_async_copy(back_hbm, back, arrivals.at[3])]
-    for copy in copies:
-        copy.start()
-
-    def fetched(which):
-        copies[which].wait()
-        return weight[which]
-
+    rows_ref, gain_ref, bias_ref, cos_ref, sin_ref, weight_ref, own_ref, back_ref = refs[:8]
+    part_ref, keys_ref = refs[8:]
     query, other_keys, other_values = project_heads(
-        rows_ref, gain_ref, fetched, bias_ref, cos_ref, sin_ref, heads
+        rows_ref, gain_ref, weight_ref, bias_ref, cos_ref, sin_ref, heads
     )
     keys = jnp.concatenate([own_ref[1], other_keys], axis=2)
     values = jnp.concatenate([own_ref[2], other_values], axis=2)
     keys_ref[0] = keys
     keys_ref[1] = values
     attended = attend_heads(query, keys, values, heads)
-    copies[3].wait()
     part_ref[...] = lax.dot_general(
-        attended, back[...], (((0,), (0,)), ((), ())), preferred_element_type=jnp.float32
+        attended, back_ref[...], (((0,), (0,)), ((), ())), preferred_element_type=jnp.float32
     ).astype(jnp.bfloat16)
 
 
@@ -474,8 +410,7 @@
     )
 
 
-def merge_kernel(columns, *refs):
-    place_ref, hidden_ref, arrived_ref, gain_ref, kept_ref, given_ref, scratch = refs
+def merge_kernel(columns, hidden_ref, arrived_ref, gain_ref, merged_ref, scratch):
     normed = layer_norm(hidden_ref[...] + arrived_ref[...].astype(jnp.float32), gain_ref[...])
     slabs = scratch.shape[0]
     for slab in range(slabs):
@@ -489,51 +424,48 @@
                 for slab in range(slabs)
             ]
             merged = jnp.concatenate(rows, axis=1).astype(jnp.bfloat16)
-            spot = pl.ds(pair * count, count)
-
-            @pl.when(place_ref[0] == parity)
-            def _keep(merged=merged, spot=spot):
-                kept_ref[spot] = merged
-
-            @pl.when(place_ref[0] != parity)
-            def _give(merged=merged, spot=spot):
-                given_ref[spot] = merged
-
-
-def projector_kernel(spots_ref, place_ref, mine_ref, other_ref, *refs):
-    weight_refs, out_ref, blocks = refs[:-2], refs[-2], refs[-1]
-    count, size = mine_ref.shape[0], weight_refs[0].shape[0]
-    mine_rows = pl.ds(pl.multiple_of(place_ref[0] * count, count), count)
-    other_rows = pl.ds(pl.multiple_of((1 - place_ref[0]) * count, count), count)
-    for number in range(len(weight_refs)):
-        lanes = slice(number * size, (number + 1) * size)
-        blocks[number, mine_rows] = mine_ref[:, lanes]
-        blocks[number, other_rows] = other_ref[:, lanes]
+            for tile in range(2):
+                merged_ref[tile, parity, pl.ds(pair * count, count)] = merged
+
+
+def projector_kernel(spots_ref, place_ref, rows_ref, *refs):
+    weight_refs, own_out, far_out, blocks = refs[:-3], refs[-3], refs[-2], refs[-1]
+    count, size = rows_ref.shape[2], weight_refs[0].shape[0]
+    for tile in range(2):
+        for half in range(2):
+            far = place_ref[0] ^ half
+            spot = pl.ds(pl.multiple_of((2 * far + tile) * count, count), count)
+            for number in range(len(weight_refs)):
+                blocks[number, spot] = rows_ref[tile, half, :, number * size : (number + 1) * size]
     total = None
     for number, weight_ref in enumerate(weight_refs):
         part = jnp.dot(
             blocks[spots_ref[number]], weight_ref[...], preferred_element_type=jnp.float32
         )
         total = part if total is None else total + part
-    out_ref[...] = total.astype(out_ref.dtype)
-
-
-def run_projector(spots, place, mine, other, weights, dtype):
-    rows, size, width = 2 * mine.shape[0], weights[0].shape[0], weights[0].shape[1]
+    own_out[...] = total[: 2 * count]
+    far_out[...] = total[2 * count :].astype(jnp.bfloat16)
+
+
+def run_projector(spots, place, rows, weights):
+    count, size, width = rows.shape[2], weights[0].shape[0], weights[0].shape[1]
     return pl.pallas_call(
         projector_kernel,
-        out_shape=jax.ShapeDtypeStruct((rows, width), dtype),
-        in_specs=[smem_spec] * 2 + [vmem_spec] * (2 + len(weights)),
-        out_specs=vmem_spec,
-        scratch_shapes=[pltpu.VMEM((len(weights), rows, size), jnp.bfloat16)],
-        compiler_params=pltpu.CompilerParams(vmem_limit_bytes=28 * 2**20),
+        out_shape=(
+            jax.ShapeDtypeStruct((2 * count, width), jnp.float32),
+            jax.ShapeDtypeStruct((2 * count, width), jnp.bfloat16),
+        ),
+        in_specs=[smem_spec] * 2 + [vmem_spec] * (1 + len(weights)),
+        out_specs=(vmem_spec, vmem_spec),
+        scratch_shapes=[pltpu.VMEM((len(weights), 4 * count, size), jnp.bfloat16)],
+        compiler_params=pltpu.CompilerParams(vmem_limit_bytes=16 * 2**20),
         cost_estimate=pl.CostEstimate(
-            flops=2 * rows * width * size * len(weights),
+            flops=8 * count * width * size * len(weights),
             bytes_accessed=2 * width * size * len(weights),
             transcendentals=0,
         ),
         name="projector",
-    )(spots, place, mine, other, *weights)
+    )(spots, place, rows, *weights)
 
 
 def per_device_near(
@@ -553,11 +485,11 @@
     routes,
     gates,
 ):
-    experts_count = lax.axis_size("expert")
+    experts_count = lax.axis_size(near_expert)
     outer = experts_count // 4
     swap = partial(near_swap, grid=(2, outer, 2, 2))
     tile_id = lax.axis_index("tile")
-    expert_id = lax.axis_index("expert")
+    expert_id = lax.axis_index(near_expert)
     outer_id, inner_id, core_id = expert_id // 4, (expert_id // 2) % 2, expert_id % 2
     row_count, columns, width_vit = patches.shape[1:]
     local_rows = row_count * columns
@@ -567,22 +499,12 @@
         first = place == 0
         return jnp.where(first, mine, other), jnp.where(first, other, mine)
 
+    def after(values, earlier):
+        return lax.optimization_barrier((values, earlier))[0]
+
     own_patches = patches.reshape(local_rows, width_vit)
     other_patches = swap(own_patches, flips=(1, 0, 0, 0))
     tile_place = tile_id.astype(jnp.int32).reshape(1)
-
-    proj_blocks, proj_spots = [], []
-    for low in range(outer // 2):
-        for inner in range(2):
-            rows = swap(proj_weight, flips=(0, low, inner, 0)) if low or inner else proj_weight
-            for core, block in enumerate((rows, swap(rows, flips=(0, 0, 0, 1)))):
-                proj_blocks.append(block)
-                proj_spots.append(
-                    ((outer_id ^ low) % (outer // 2)) * 4
-                    + (inner_id ^ inner) * 2
-                    + (core_id ^ core)
-                )
-    proj_spots = jnp.stack(proj_spots).astype(jnp.int32)
 
     top_count = routes.shape[-1]
     page_routes = routes.reshape(2, token_count, top_count)
@@ -622,36 +544,30 @@
         angles = jnp.where((feature < 2 * quarter)[:, None], rows, cols) * inverse
         return jnp.cos(angles), jnp.sin(angles)
 
+    own_tables = tables(tile_id)
     gain_first, gain_second = norm1_gain[None], norm2_gain[None]
     head_rows = (heads, HD, local_rows)
-    weight_scratch = pltpu.VMEM(weight_rows.shape, jnp.bfloat16)
-    params = pltpu.CompilerParams(vmem_limit_bytes=28 * 2**20)
+    params = pltpu.CompilerParams(vmem_limit_bytes=16 * 2**20)
     macs = local_rows * width_vit * heads * HD
     own_heads = pl.pallas_call(
         partial(own_heads_kernel, heads),
         out_shape=jax.ShapeDtypeStruct((3, *head_rows), jnp.bfloat16),
-        in_specs=[vmem_spec] * 5 + [any_spec],
+        in_specs=[vmem_spec] * 6,
         out_specs=vmem_spec,
-        scratch_shapes=[weight_scratch, pltpu.SemaphoreType.DMA((3,))],
         compiler_params=params,
         cost_estimate=pl.CostEstimate(
             flops=6 * macs, bytes_accessed=2 * weight_rows.size, transcendentals=0
         ),
         name="own_heads",
-    )(own_patches, gain_first, bias_rows, *tables(tile_id), weight_rows)
+    )(own_patches, gain_first, bias_rows, *own_tables, weight_rows)
     other_part, keys_values = pl.pallas_call(
         partial(other_rows_kernel, heads),
         out_shape=(
             jax.ShapeDtypeStruct((local_rows, width_vit), jnp.bfloat16),
             jax.ShapeDtypeStruct((2, heads, HD, 2 * local_rows), jnp.bfloat16),
         ),
-        in_specs=[vmem_spec] * 6 + [any_spec] * 2,
+        in_specs=[vmem_spec] * 8,
         out_specs=(vmem_spec, vmem_spec),
-        scratch_shapes=[
-            weight_scratch,
-            pltpu.VMEM(out_weight.shape, jnp.bfloat16),
-            pltpu.SemaphoreType.DMA((4,)),
-        ],
         compiler_params=params,
         cost_estimate=pl.CostEstimate(
             flops=10 * macs, bytes_accessed=2 * weight_rows.size, transcendentals=0
@@ -662,8 +578,8 @@
         gain_first,
         bias_rows,
         *tables(1 - tile_id),
+        weight_rows,
         own_heads,
-        weight_rows,
         out_weight,
     )
     arrived_part = swap(other_part, flips=(1, 0, 0, 0))
@@ -678,32 +594,41 @@
         ),
         name="own_rows",
     )(own_patches, own_heads, keys_values, out_weight, out_bias[None])
-    merged_shape = jax.ShapeDtypeStruct((token_count, 2 * width_vit), jnp.bfloat16)
-    kept, given = pl.pallas_call(
+    merged = pl.pallas_call(
         partial(merge_kernel, columns),
-        out_shape=(merged_shape, merged_shape),
-        in_specs=[smem_spec] + [vmem_spec] * 3,
-        out_specs=(vmem_spec, vmem_spec),
+        out_shape=jax.ShapeDtypeStruct((2, 2, token_count, 2 * width_vit), jnp.bfloat16),
+        in_specs=[vmem_spec] * 3,
+        out_specs=vmem_spec,
         scratch_shapes=[pltpu.VMEM((width_vit // 128, local_rows, 128), jnp.float32)],
         compiler_params=params,
         name="merge_windows",
-    )(
-        (outer_id // (outer // 2)).astype(jnp.int32).reshape(1),
-        hidden,
-        arrived_part,
-        gain_second,
-    )
+    )(hidden, arrived_part, gain_second)
+
+    proj_blocks, proj_spots = [], []
+    held_rows = after(proj_weight, own_tables)
+    for low in range(outer // 2):
+        for inner in range(2):
+            rows = swap(held_rows, flips=(0, low, inner, 0)) if low or inner else proj_weight
+            for core, block in enumerate(
+                (rows, swap(after(rows, merged), flips=(0, 0, 0, 1)))
+            ):
+                proj_blocks.append(block)
+                proj_spots.append(
+                    ((outer_id ^ low) % (outer // 2)) * 4
+                    + (inner_id ^ inner) * 2
+                    + (core_id ^ core)
+                )
+    proj_spots = jnp.stack(proj_spots).astype(jnp.int32)
 
     far = outer // 2
-    from_far = swap(given, flips=(0, far, 0, 0))
-    from_both = swap(given, flips=(1, far, 0, 0))
-    from_tile = swap(kept, flips=(1, 0, 0, 0))
+    merged = lax.all_to_all(
+        merged.reshape(4, token_count, -1), ("tile", "half"), split_axis=0, concat_axis=0, tiled=True
+    ).reshape(merged.shape)
     page_tokens = 2 * token_count
-    project = partial(run_projector, proj_spots, tile_place, weights=proj_blocks)
-    far_part = swap(project(from_far, from_both, dtype=jnp.bfloat16), flips=(0, far, 0, 0))
-    tokens_half = (
-        project(kept, from_tile, dtype=jnp.float32) + far_part.astype(jnp.float32)
-    ).astype(jnp.bfloat16)
+    half_place = (outer_id // far).astype(jnp.int32).reshape(1)
+    own_tokens, far_tokens = run_projector(proj_spots, half_place, merged, proj_blocks)
+    far_part = swap(far_tokens, flips=(0, far, 0, 0))
+    tokens_half = (own_tokens + far_part.astype(jnp.float32)).astype(jnp.bfloat16)
 
     width_moe = 2 * tokens_half.shape[1]
     expert_units = expert_in[0].transpose(1, 2, 0)
@@ -713,94 +638,99 @@
     held = jnp.concatenate([tokens_half, gate_rows], axis=1)
     held_by_step = [held] + [swap(held, flips=(0, step, 0, 0)) for step in range(1, outer)]
     tile_flip, inner_flip, core_flip = (1, 0, 0, 0), (0, 0, 1, 0), (0, 0, 0, 1)
-    contributions = []
-    for step, held in enumerate(held_by_step):
-        extra = None
-        for flip in (inner_flip, tile_flip) if step % 2 else (tile_flip, inner_flip):
-            arrived = swap(held, flips=flip)
-            if step == 0 and flip == tile_flip:
-                extra = run_shared(
-                    tile_place, held, arrived, gain_row, shared_units, shared_out
-                )
-                residual = jnp.concatenate(
-                    by_place(
-                        tile_id,
-                        *(
-                            lax.dynamic_slice_in_dim(
-                                rows[:, :half_moe], tile_id * token_count, token_count, 0
-                            )
-                            for rows in (held, arrived)
-                        ),
-                    ),
-                    axis=1,
-                )
-            held = jnp.stack([held, arrived])
-        if step % 2:
-            held = held.transpose(1, 0, 2, 3)
-        contributions.append(
-            run_expert(
-                tile_place,
-                held,
-                swap(held, flips=core_flip),
-                gain_row,
-                lane_row,
-                expert_units,
-                expert_out[0],
-                extra,
-            )
-        )
-
     def add(mine, other):
         return (mine.astype(jnp.float32) + other.astype(jnp.float32)).astype(jnp.bfloat16)
 
-    total = residual.astype(jnp.float32)
-    for step, (own_sums, across_sums) in enumerate(contributions):
+    flips_of = [
+        (inner_flip, tile_flip) if step % 2 else (tile_flip, inner_flip) for step in range(outer)
+    ]
+    near_blocks, first_sums, kept_sums = [], [], []
+    for step, held in enumerate(held_by_step):
+        arrived = swap(held, flips=flips_of[step][0])
+        if step == 0:
+            own_held, tile_held = held, arrived
+        held = jnp.stack([held, arrived])
+        held = jnp.stack([held, swap(held, flips=flips_of[step][1])])
+        near_blocks.append(held.transpose(1, 0, 2, 3) if step % 2 else held)
+    residual = jnp.concatenate(
+        by_place(
+            tile_id,
+            *(
+                lax.dynamic_slice_in_dim(
+                    rows[:, :half_moe], tile_id * token_count, token_count, 0
+                )
+                for rows in (own_held, tile_held)
+            ),
+        ),
+        axis=1,
+    )
+    shared_sums = run_shared(
+        tile_place, after(own_held, near_blocks[0]), tile_held, gain_row, shared_units, shared_out
+    )
+    across_blocks = [swap(near, flips=core_flip) for near in near_blocks]
+    for step, (near, across) in enumerate(zip(near_blocks, across_blocks)):
+        if step > 1:
+            near = after(near, first_sums[step - 2])
+        own_sums, across_sums = run_expert(
+            tile_place,
+            near,
+            across,
+            gain_row,
+            lane_row,
+            expert_units,
+            expert_out[0],
+            None if step else shared_sums,
+        )
         summed = add(own_sums, swap(across_sums, flips=core_flip)).reshape(
             2, 2, token_count, width_moe
         )
         if step % 2:
-            summed = add(summed[0], swap(summed[1], flips=inner_flip))
-            stays, leaves = by_place(tile_id, summed[0], summed[1])
-            summed = add(stays, swap(leaves, flips=tile_flip))
+            stays, leaves = summed[0], summed[1]
         else:
             stays, leaves = by_place(tile_id, summed[:, 0], summed[:, 1])
-            summed = add(stays, swap(leaves, flips=tile_flip))
-            summed = add(summed[0], swap(summed[1], flips=inner_flip))
+        first_sums.append(leaves)
+        kept_sums.append(stays)
+    total = residual.astype(jnp.float32)
+    for step, (stays, leaves) in enumerate(zip(kept_sums, first_sums)):
+        summed = add(stays, swap(leaves, flips=flips_of[step][0]))
+        if step % 2:
+            stays, leaves = by_place(tile_id, summed[0], summed[1])
+        else:
+            stays, leaves = summed[0], summed[1]
+        summed = add(stays, swap(leaves, flips=flips_of[step][1]))
         if step:
             summed = swap(summed, flips=(0, step, 0, 0))
         total = total + summed.astype(jnp.float32)
     return total.astype(jnp.bfloat16).reshape(1, row_count // 2, columns // 2, width_moe)
 
 
-def per_device(*arguments):
-    experts_count = lax.axis_size("expert")
-    if lax.axis_size("tile") == 2 and experts_count % 4 == 0 and experts_count == 16:
-        return per_device_near(*arguments)
-    return per_device_slots(*arguments)
-
-
 def solution(mesh):
+    expert = "expert"
+    near = mesh.shape["tile"] == 2 and mesh.shape["expert"] == 16
+    if near:
+        mesh = jax.sharding.Mesh(mesh.devices.reshape(2, 2, 2, 2, 2), ("tile", *near_expert))
+        expert = near_expert
     placed = (
-        P("expert", "tile", None, None),
+        P(expert, "tile", None, None),
         P(),
         P(None, None, "tile"),
         P(None, "tile"),
         P("tile", None),
         P(),
         P(),
-        P("expert", "tile"),
+        P(expert, "tile"),
         P(),
-        P("expert", None, None, "tile"),
-        P("expert", "tile", None),
+        P(expert, None, None, "tile"),
+        P(expert, "tile", None),
         P(None, None, "tile"),
         P("tile", None),
-        P("expert", None, None, None),
-        P("expert", "tile", None, None),
+        P(expert, None, None, None),
+        P(expert, "tile", None, None),
     )
     return jax.shard_map(
-        per_device,
+        per_device_near if near else per_device_slots,
         mesh=mesh,
         in_specs=placed,
-        out_specs=P("expert", "tile", None, None),
+        out_specs=P(expert, "tile", None, None),
         check_vma=False,
     )

time: 156 us -> 139 us (0.89)
  Pallas kernels: 41.6 us -> 28.8 us
  waiting for transfers between devices: 54.5 us -> 51 us
  starting transfers between devices: 46.1 us -> 42.8 us
  local copies, waits for them, and re-layouts: 9.43 us -> 11.8 us
    ppermute x43 -> x40, waiting for transfers between devices: 54.5 us -> 41.9 us  [near_swap(): return lax.ppermute(values, ('tile', *near_expert), pairs)]
    pallas_call x8 -> x7, Pallas kernels: 30.3 us -> 20.9 us  [the longest x4 13.5 us: run_expert(): pl.pallas_call(partial(expert_kernel, extra is not None), out_shape=(out,...]
    all_to_all x0 -> x1, waiting for transfers between devices: none -> 9.11 us  [per_device_near(): lax.all_to_all(merged.reshape(4, token_count, -1), ('tile', 'half'), spli...]
    ppermute x43 -> x40, starting transfers between devices: 46.1 us -> 39 us  [near_swap(): return lax.ppermute(values, ('tile', *near_expert), pairs)]
    all_to_all x0 -> x1, starting transfers between devices: none -> 3.86 us  [per_device_near(): lax.all_to_all(merged.reshape(4, token_count, -1), ('tile', 'half'), spli...]
    pallas_call x1, Pallas kernels: 6 us -> 3.88 us  [per_device_near(): pl.pallas_call(partial(other_rows_kernel, heads), out_shape=(jax.ShapeDty...]
    unnamed x41 -> x37, local copies, waits for them, and re-layouts: 7.09 us -> 7.52 us
  transfers between devices with their start and end apart: 43 -> 41, of which waited for: 12 -> 15; matrix products, arithmetic and copies ran while one was open for 3% -> 5% of each run, Pallas kernels for 27% -> 18%
where the time goes in v4:
time: 139 us
  waiting for transfers between devices  51 us (37%)
  starting transfers between devices  42.8 us (31%)
  Pallas kernels  28.8 us (21%)
  local copies, waits for them, and re-layouts  11.8 us (8%)
  other arithmetic  3.78 us (3%)
    ppermute x40, waiting for transfers between devices, near_swap(): return lax.ppermute(values, ('tile', *near_expert), pairs)  41.9 us
    ppermute x40, starting transfers between devices, near_swap(): return lax.ppermute(values, ('tile', *near_expert), pairs)  39 us
    pallas_call x4, Pallas kernels, run_expert(): pl.pallas_call(partial(expert_kernel, extra is not None), out_shape=(out,...  13.5 us
    all_to_all x1, waiting for transfers between devices, per_device_near(): lax.all_to_all(merged.reshape(4, token_count, -1), ('tile', 'half'), spli...  9.11 us
    unnamed x37, local copies, waits for them, and re-layouts  7.52 us
    pallas_call x1, Pallas kernels, per_device_near(): pl.pallas_call(partial(other_rows_kernel, heads), out_shape=(jax.ShapeDty...  3.88 us
    all_to_all x1, starting transfers between devices, per_device_near(): lax.all_to_all(merged.reshape(4, token_count, -1), ('tile', 'half'), spli...  3.86 us
    pallas_call x1, Pallas kernels, run_projector(): pl.pallas_call(projector_kernel, out_shape=(jax.ShapeDtypeStruct((2 * cou...  3.6 us
  transfers between devices with their start and end apart: 41, of which 15 were waited for; matrix products, arithmetic and copies ran while one was open for 5% of the time, Pallas kernels for 18%

profile of v4, /device:TPU:0, one launch (start us, length us, event | category | flops | bytes accessed | tf_op | source)
XLA Modules:
  0.0 138.8 jit_solution(4734059000560516616)
XLA Ops:
  0.0 2.9 %collective-permute-start = (bf16[128,1152]{1,0:T(8,128)(2,1)}, bf16[128,1152]{1,0:T(8,128)(2,1)S(1)}, u32[]{:S(2)}, u32[]{:S(2)}) collective-permute-start(bf16[128,1152]{1,0:T(8,128)(2,1)} %bitcast.137), channel_id=1, source_target_pairs={{0,16},{1,17},{2,18},{3,19},{4,20},{5,21},{6,22},{7,23},{8,24},{9,... | collective-permute-start | bytes 884744 | tf_op jit(solution)/shard_map/ppermute | solution.py:221
  14.2 3.9 %other_rows.1 = (bf16[128,1152]{1,0:T(8,128)(2,1)S(1)}, bf16[2,8,72,256]{3,2,1,0:T(8,128)(2,1)S(1)}) custom-call(bf16[128,1152]{1,0:T(8,128)(2,1)S(1)} %collective-permute-done.refs_0_, f32[1,1152]{1,0:T(1,128)S(1)} %broadcast_in_dim.81.refs_1_, f32[3,576,1]{2,1,0:T(8,128)S(1)} %copy.53.refs_2_, f32[72,128]{1,0:T(8,128)S(1)} %get-tuple-element.66.refs_3_, ...), custom_call_target="tpu_custom_call" | custom-call | flops 849346560 | bytes 3981312 | tf_op jit(solution)/shard_map/other_rows/pallas_call | solution.py:563
  18.4 2.6 %own_rows.1.hidden_ref = f32[128,1152]{1,0:T(8,128)S(1)} custom-call(bf16[128,1152]{1,0:T(8,128)(2,1)S(1)} %bitcast.139, bf16[3,8,72,128]{3,2,1,0:T(8,128)(2,1)S(1)} %own_heads.1.refs_6_.refs_1_, bf16[2,8,72,256]{3,2,1,0:T(8,128)(2,1)S(1)} %get-tuple-element.25.refs_2_, bf16[576,1152]{1,0:T(8,128)(2,1)S(1)} %copy-done.4, f32[1,1152]{1,0:T(1,128)S(1)} %broadcast_in_dim.87.refs_4_), custom_call_target="tpu_custom_call" | custom-call | flops 339738624 | bytes 1327104 | tf_op jit(solution)/shard_map/own_rows/pallas_call | solution.py:586
  21.0 4.9 %collective-permute-done.1.arrived_ref = bf16[128,1152]{1,0:T(8,128)(2,1)S(1)} collective-permute-done((bf16[128,1152]{1,0:T(8,128)(2,1)S(1)}, bf16[128,1152]{1,0:T(8,128)(2,1)S(1)}, u32[]{:S(2)}, u32[]{:S(2)}) %collective-permute-start.1) | collective-permute-done | bytes 294944 | tf_op jit(solution)/shard_map/ppermute | solution.py:221
  27.0 3.9 %all-to-all-start = ((bf16[4,32,2304]{2,1,0:T(8,128)(2,1)}), bf16[4,32,2304]{2,1,0:T(8,128)(2,1)S(1)}, u32[]{:S(2)}, u32[]{:S(2)}) async-start(bf16[4,32,2304]{2,1,0:T(8,128)(2,1)} %bitcast.12), calls=%async_computation | async-start | bytes 1179648 | tf_op jit(solution)/shard_map/all_to_all | solution.py:624
  35.6 9.1 %all-to-all-done = bf16[4,32,2304]{2,1,0:T(8,128)(2,1)S(1)} async-done(((bf16[4,32,2304]{2,1,0:T(8,128)(2,1)}), bf16[4,32,2304]{2,1,0:T(8,128)(2,1)S(1)}, u32[]{:S(2)}, u32[]{:S(2)}) %all-to-all-start) | async-done | bytes 589856 | tf_op jit(solution)/shard_map/all_to_all | solution.py:624
  44.8 3.6 %projector.1 = (f32[64,1024]{1,0:T(8,128)S(1)}, bf16[64,1024]{1,0:T(8,128)(2,1)}) custom-call(s32[8]{0:T(128)S(1)} %stack.107.spots_ref, s32[1]{0:T(128)} %bitcast.8.place_ref, bf16[2,2,32,2304]{3,2,1,0:T(8,128)(2,1)S(1)} %bitcast.135, bf16[288,1024]{1,0:T(8,128)(2,1)S(1)} %copy-done.8, bf16[288,1024]{1,0:T(8,128)(2,1)S(1)} %collective-permute-done.2.refs_1_, ...), custom_call_target="tpu_custom_call" | custom-call | flops 603979776 | bytes 4718592 | tf_op jit(solution)/shard_map/projector/pallas_call | solution.py:452
  49.2 7.0 %collective-permute-done.9 = bf16[64,1024]{1,0:T(8,128)(2,1)S(1)} collective-permute-done((bf16[64,1024]{1,0:T(8,128)(2,1)}, bf16[64,1024]{1,0:T(8,128)(2,1)S(1)}, u32[]{:S(2)}, u32[]{:S(2)}) %collective-permute-start.9) | collective-permute-done | bytes 131104 | tf_op jit(solution)/shard_map/ppermute | solution.py:221
  67.1 2.2 %collective-permute-start.33 = (bf16[64,1152]{1,0:T(8,128)(2,1)S(1)}, bf16[64,1152]{1,0:T(8,128)(2,1)S(1)}, u32[]{:S(2)}, u32[]{:S(2)}) collective-permute-start(bf16[64,1152]{1,0:T(8,128)(2,1)S(1)} %collective-permute-done.32), channel_id=1, source_target_pairs={{0,2},{1,3},{2,0},{3,1},{4,6},{5,7},{6,4},{7,5},{8,10},{9,11},{10,... | collective-permute-start | bytes 442376 | tf_op jit(solution)/shard_map/ppermute | solution.py:221
  69.3 4.1 %collective-permute-done.24 = bf16[64,1152]{1,0:T(8,128)(2,1)S(1)} collective-permute-done((bf16[64,1152]{1,0:T(8,128)(2,1)S(1)}, bf16[64,1152]{1,0:T(8,128)(2,1)S(1)}, u32[]{:S(2)}, u32[]{:S(2)}) %collective-permute-start.24) | collective-permute-done | bytes 147488 | tf_op jit(solution)/shard_map/ppermute | solution.py:221
  76.5 2.8 %collective-permute-start.34 = (bf16[2,64,1152]{2,1,0:T(8,128)(2,1)S(1)}, bf16[2,64,1152]{2,1,0:T(8,128)(2,1)S(1)}, u32[]{:S(2)}, u32[]{:S(2)}) collective-permute-start(bf16[2,64,1152]{2,1,0:T(8,128)(2,1)S(1)} %get-tuple-element.56), channel_id=1, source_target_pairs={{0,16},{1,17},{2,18},{3,19},{4,20},{5,21},{6,22},{7,23},{8,24},{9,... | collective-permute-start | bytes 884744 | tf_op jit(solution)/shard_map/ppermute | solution.py:221
  80.2 3.4 %collective-permute-start.26 = (bf16[2,64,1152]{2,1,0:T(8,128)(2,1)S(1)}, bf16[2,64,1152]{2,1,0:T(8,128)(2,1)S(1)}, u32[]{:S(2)}, u32[]{:S(2)}) collective-permute-start(bf16[2,64,1152]{2,1,0:T(8,128)(2,1)S(1)} %get-tuple-element.52), channel_id=1, source_target_pairs={{0,2},{1,3},{2,0},{3,1},{4,6},{5,7},{6,4},{7,5},{8,10},{9,11},{10,... | collective-permute-start | bytes 884744 | tf_op jit(solution)/shard_map/ppermute | solution.py:221
  83.7 2.6 %copy-done.3 = bf16[2048,2,704]{0,2,1:T(8,128)(2,1)S(1)} copy-done((bf16[2048,2,704]{0,2,1:T(8,128)(2,1)S(1)}, bf16[2048,2,704]{0,2,1:T(8,128)(2,1)}, u32[]{:S(2)}) %copy-start.3) | copy-done | bytes 5767192
  86.3 2.7 %shared_units.1.refs_7_ = f32[64,2048]{1,0:T(8,128)S(1)} custom-call(s32[1]{0:T(128)} %bitcast.14.place_ref.refs_0_, bf16[64,1152]{1,0:T(8,128)(2,1)S(1)} %get-tuple-element.34.mine_ref, bf16[64,1152]{1,0:T(8,128)(2,1)S(1)} %collective-permute-done.10.other_ref, f32[1,2048]{1,0:T(1,128)S(1)} %bitcast.140, bf16[2,704,2048]{2,1,0:T(8,128)(2,1)S(1)} %bitcast.134, ...), custom_call_target="tpu_custom_call" | custom-call | flops 553648128 | bytes 9175040 | tf_op jit(solution)/shard_map/shared_units/pallas_call | solution.py:329
  89.2 3.3 %expert_units.4 = (bf16[2,64,2048]{2,1,0:T(8,128)(2,1)S(1)}, bf16[2,64,2048]{2,1,0:T(8,128)(2,1)S(1)}) custom-call(s32[1]{0:T(128)} %bitcast.14.place_ref.refs_0_, bf16[2,2,64,1152]{3,2,1,0:T(8,128)(2,1)S(1)} %pad_maximum_fusion.refs_1_, bf16[2,2,64,1152]{3,2,1,0:T(8,128)(2,1)S(1)} %collective-permute-done.12.refs_2_, f32[1,2048]{1,0:T(1,128)S(1)} %bitcast.141, ...), custom_call_target="tpu_custom_call" | custom-call | flops 2214592512 | bytes 10747904 | tf_op jit(solution)/shard_map/expert_units/pallas_call | solution.py:302
  94.0 3.3 %expert_units.5 = (bf16[2,64,2048]{2,1,0:T(8,128)(2,1)S(1)}, bf16[2,64,2048]{2,1,0:T(8,128)(2,1)S(1)}) custom-call(s32[1]{0:T(128)} %bitcast.14.place_ref.refs_0_, bf16[2,2,64,1152]{3,2,1,0:T(8,128)(2,1)S(1)} %copy.60.refs_1_, bf16[2,2,64,1152]{3,2,1,0:T(8,128)(2,1)S(1)} %copy.61.refs_2_, f32[1,2048]{1,0:T(1,128)S(1)} %bitcast.142, ...), custom_call_target="tpu_custom_call" | custom-call | flops 2214592512 | bytes 10747904 | tf_op jit(solution)/shard_map/expert_units/pallas_call | solution.py:302
  97.8 3.5 %expert_units.6 = (bf16[2,64,2048]{2,1,0:T(8,128)(2,1)S(1)}, bf16[2,64,2048]{2,1,0:T(8,128)(2,1)S(1)}) custom-call(s32[1]{0:T(128)} %bitcast.14.place_ref.refs_0_, bf16[2,2,64,1152]{3,2,1,0:T(8,128)(2,1)S(1)} %pad_maximum_fusion.1.refs_1_, bf16[2,2,64,1152]{3,2,1,0:T(8,128)(2,1)S(1)} %collective-permute-done.27.refs_2_, f32[1,2048]{1,0:T(1,128)S(1)} %bitcast.143, ...), custom_call_target="tpu_custom_call" | custom-call | flops 2214592512 | bytes 10747904 | tf_op jit(solution)/shard_map/expert_units/pallas_call | solution.py:302
  103.0 3.3 %expert_units.7 = (bf16[2,64,2048]{2,1,0:T(8,128)(2,1)S(1)}, bf16[2,64,2048]{2,1,0:T(8,128)(2,1)S(1)}) custom-call(s32[1]{0:T(128)} %bitcast.14.place_ref.refs_0_, bf16[2,2,64,1152]{3,2,1,0:T(8,128)(2,1)S(1)} %maximum_bitcast_fusion.1.refs_1_, bf16[2,2,64,1152]{3,2,1,0:T(8,128)(2,1)S(1)} %collective-permute-done.35.refs_2_, f32[1,2048]{1,0:T(1,128)S(1)} %bitcast.144, ...), custom_call_target="tpu_custom_call" | custom-call | flops 2214592512 | bytes 10747904 | tf_op jit(solution)/shard_map/expert_units/pallas_call | solution.py:302
  107.6 3.4 %collective-permute-done.21 = bf16[2,32,2048]{2,1,0:T(8,128)(2,1)S(1)} collective-permute-done((bf16[2,32,2048]{2,1,0:T(8,128)(2,1)S(1)}, bf16[2,32,2048]{2,1,0:T(8,128)(2,1)S(1)}, u32[]{:S(2)}, u32[]{:S(2)}) %collective-permute-start.21) | collective-permute-done | bytes 262176 | tf_op jit(solution)/shard_map/ppermute | solution.py:221
  113.4 4.1 %collective-permute-done.22 = bf16[32,2048]{1,0:T(8,128)(2,1)S(1)} collective-permute-done((bf16[32,2048]{1,0:T(8,128)(2,1)S(1)}, bf16[32,2048]{1,0:T(8,128)(2,1)S(1)}, u32[]{:S(2)}, u32[]{:S(2)}) %collective-permute-start.22) | collective-permute-done | bytes 131104 | tf_op jit(solution)/shard_map/ppermute | solution.py:221
  119.0 2.5 %collective-permute-done.29 = bf16[2,32,2048]{2,1,0:T(8,128)(2,1)S(1)} collective-permute-done((bf16[2,32,2048]{2,1,0:T(8,128)(2,1)S(1)}, bf16[2,32,2048]{2,1,0:T(8,128)(2,1)S(1)}, u32[]{:S(2)}, u32[]{:S(2)}) %collective-permute-start.29) | collective-permute-done | bytes 262176 | tf_op jit(solution)/shard_map/ppermute | solution.py:221
  122.6 3.1 %collective-permute-done.37 = bf16[2,32,2048]{2,1,0:T(8,128)(2,1)S(1)} collective-permute-done((bf16[2,32,2048]{2,1,0:T(8,128)(2,1)S(1)}, bf16[2,32,2048]{2,1,0:T(8,128)(2,1)S(1)}, u32[]{:S(2)}, u32[]{:S(2)}) %collective-permute-start.37) | collective-permute-done | bytes 262176 | tf_op jit(solution)/shard_map/ppermute | solution.py:221
  130.9 2.8 %collective-permute-start.39 = (bf16[32,2048]{1,0:T(8,128)(2,1)S(1)}, bf16[32,2048]{1,0:T(8,128)(2,1)S(1)}, u32[]{:S(2)}, u32[]{:S(2)}) collective-permute-start(bf16[32,2048]{1,0:T(8,128)(2,1)S(1)} %fusion.4), channel_id=1, source_target_pairs={{0,12},{1,13},{2,14},{3,15},{4,8},{5,9},{6,10},{7,11},{8,4},{9,5},... | collective-permute-start | bytes 393224 | tf_op jit(solution)/shard_map/ppermute | solution.py:221
  133.7 4.3 %collective-permute-done.31 = bf16[32,2048]{1,0:T(8,128)(2,1)S(1)} collective-permute-done((bf16[32,2048]{1,0:T(8,128)(2,1)S(1)}, bf16[32,2048]{1,0:T(8,128)(2,1)S(1)}, u32[]{:S(2)}, u32[]{:S(2)}) %collective-permute-start.31) | collective-permute-done | bytes 131104 | tf_op jit(solution)/shard_map/ppermute | solution.py:221
  (160 shorter events, 48.9 us)
Async XLA Ops:
  0.0 13.2 %collective-permute-start = (bf16[128,1152]{1,0:T(8,128)(2,1)}, bf16[128,1152]{1,0:T(8,128)(2,1)S(1)}, u32[]{:S(2)}, u32[]{:S(2)}) collective-permute-start(bf16[128,1152]{1,0:T(8,128)(2,1)} %bitcast.137), channel_id=1, source_target_pairs={{0,16},{1,17},{2,18},{3,19},{4,20},{5,21},{6,22},{7,23},{8,24},{9,... | collective-permute-start | bytes 884744 | tf_op jit(solution)/shard_map/ppermute | solution.py:221
  3.3 27.5 %collective-permute-start.3 = (bf16[288,1024]{1,0:T(8,128)(2,1)}, bf16[288,1024]{1,0:T(8,128)(2,1)S(1)}, u32[]{:S(2)}, u32[]{:S(2)}) collective-permute-start(bf16[288,1024]{1,0:T(8,128)(2,1)} %refs_0_.1), channel_id=1, source_target_pairs={{0,2},{1,3},{2,0},{3,1},{4,6},{5,7},{6,4},{7,5},{8,10},{9,11},{10,... | collective-permute-start | bytes 1769480 | tf_op jit(solution)/shard_map/ppermute | solution.py:221
  4.9 26.4 %collective-permute-start.5 = (bf16[288,1024]{1,0:T(8,128)(2,1)}, bf16[288,1024]{1,0:T(8,128)(2,1)S(1)}, u32[]{:S(2)}, u32[]{:S(2)}) collective-permute-start(bf16[288,1024]{1,0:T(8,128)(2,1)} %refs_0_.1), channel_id=1, source_target_pairs={{0,4},{1,5},{2,6},{3,7},{4,0},{5,1},{6,2},{7,3},{8,12},{9,13},{10,... | collective-permute-start | bytes 1769480 | tf_op jit(solution)/shard_map/ppermute | solution.py:221
  6.5 26.7 %collective-permute-start.7 = (bf16[288,1024]{1,0:T(8,128)(2,1)}, bf16[288,1024]{1,0:T(8,128)(2,1)S(1)}, u32[]{:S(2)}, u32[]{:S(2)}) collective-permute-start(bf16[288,1024]{1,0:T(8,128)(2,1)} %refs_0_.1), channel_id=1, source_target_pairs={{0,6},{1,7},{2,4},{3,5},{4,2},{5,3},{6,0},{7,1},{8,14},{9,15},{10,... | collective-permute-start | bytes 1769480 | tf_op jit(solution)/shard_map/ppermute | solution.py:221
  27.0 17.8 %all-to-all-start = ((bf16[4,32,2304]{2,1,0:T(8,128)(2,1)}), bf16[4,32,2304]{2,1,0:T(8,128)(2,1)S(1)}, u32[]{:S(2)}, u32[]{:S(2)}) async-start(bf16[4,32,2304]{2,1,0:T(8,128)(2,1)} %bitcast.12), calls=%async_computation | async-start | bytes 1179648 | tf_op jit(solution)/shard_map/all_to_all | solution.py:624
  58.2 8.9 %collective-permute-start.32 = (bf16[64,1152]{1,0:T(8,128)(2,1)S(1)}, bf16[64,1152]{1,0:T(8,128)(2,1)S(1)}, u32[]{:S(2)}, u32[]{:S(2)}) collective-permute-start(bf16[64,1152]{1,0:T(8,128)(2,1)S(1)} %get-tuple-element.34.mine_ref), channel_id=1, source_target_pairs={{0,12},{1,13},{2,14},{3,15},{4,8},{5,9},{6,10},{7,11},{8,4},{9,5},... | collective-permute-start | bytes 442376 | tf_op jit(solution)/shard_map/ppermute | solution.py:221
  60.2 13.2 %collective-permute-start.24 = (bf16[64,1152]{1,0:T(8,128)(2,1)S(1)}, bf16[64,1152]{1,0:T(8,128)(2,1)S(1)}, u32[]{:S(2)}, u32[]{:S(2)}) collective-permute-start(bf16[64,1152]{1,0:T(8,128)(2,1)S(1)} %get-tuple-element.34.mine_ref), channel_id=1, source_target_pairs={{0,8},{1,9},{2,10},{3,11},{4,12},{5,13},{6,14},{7,15},{8,0},{9,1},... | collective-permute-start | bytes 442376 | tf_op jit(solution)/shard_map/ppermute | solution.py:221
  63.6 10.6 %collective-permute-start.17 = (bf16[64,1152]{1,0:T(8,128)(2,1)S(1)}, bf16[64,1152]{1,0:T(8,128)(2,1)S(1)}, u32[]{:S(2)}, u32[]{:S(2)}) collective-permute-start(bf16[64,1152]{1,0:T(8,128)(2,1)S(1)} %collective-permute-done.16), channel_id=1, source_target_pairs={{0,2},{1,3},{2,0},{3,1},{4,6},{5,7},{6,4},{7,5},{8,10},{9,11},{10,... | collective-permute-start | bytes 442376 | tf_op jit(solution)/shard_map/ppermute | solution.py:221
  64.9 10.7 %collective-permute-start.11 = (bf16[2,64,1152]{2,1,0:T(8,128)(2,1)S(1)}, bf16[2,64,1152]{2,1,0:T(8,128)(2,1)S(1)}, u32[]{:S(2)}, u32[]{:S(2)}) collective-permute-start(bf16[2,64,1152]{2,1,0:T(8,128)(2,1)S(1)} %get-tuple-element.50), channel_id=1, source_target_pairs={{0,2},{1,3},{2,0},{3,1},{4,6},{5,7},{6,4},{7,5},{8,10},{9,11},{10,... | collective-permute-start | bytes 884744 | tf_op jit(solution)/shard_map/ppermute | solution.py:221
  67.1 9.4 %collective-permute-start.33 = (bf16[64,1152]{1,0:T(8,128)(2,1)S(1)}, bf16[64,1152]{1,0:T(8,128)(2,1)S(1)}, u32[]{:S(2)}, u32[]{:S(2)}) collective-permute-start(bf16[64,1152]{1,0:T(8,128)(2,1)S(1)} %collective-permute-done.32), channel_id=1, source_target_pairs={{0,2},{1,3},{2,0},{3,1},{4,6},{5,7},{6,4},{7,5},{8,10},{9,11},{10,... | collective-permute-start | bytes 442376 | tf_op jit(solution)/shard_map/ppermute | solution.py:221
  74.3 14.7 %collective-permute-start.18 = (bf16[2,64,1152]{2,1,0:T(8,128)(2,1)S(1)}, bf16[2,64,1152]{2,1,0:T(8,128)(2,1)S(1)}, u32[]{:S(2)}, u32[]{:S(2)}) collective-permute-start(bf16[2,64,1152]{2,1,0:T(8,128)(2,1)S(1)} %get-tuple-element.54), channel_id=1, source_target_pairs={{0,16},{1,17},{2,18},{3,19},{4,20},{5,21},{6,22},{7,23},{8,24},{9,... | collective-permute-start | bytes 884744 | tf_op jit(solution)/shard_map/ppermute | solution.py:221
  75.6 13.6 %collective-permute-start.12 = (bf16[2,2,64,1152]{3,2,1,0:T(8,128)(2,1)S(1)}, bf16[2,2,64,1152]{3,2,1,0:T(8,128)(2,1)S(1)}, u32[]{:S(2)}, u32[]{:S(2)}) collective-permute-start(bf16[2,2,64,1152]{3,2,1,0:T(8,128)(2,1)S(1)} %pad_maximum_fusion.refs_1_), channel_id=1, source_target_pairs={{0,1},{1,0},{2,3},{3,2},{4,5},{5,4},{6,7},{7,6},{8,9},{9,8},{10,11... | collective-permute-start | bytes 1769480 | tf_op jit(solution)/shard_map/ppermute | solution.py:221
  76.5 16.5 %collective-permute-start.34 = (bf16[2,64,1152]{2,1,0:T(8,128)(2,1)S(1)}, bf16[2,64,1152]{2,1,0:T(8,128)(2,1)S(1)}, u32[]{:S(2)}, u32[]{:S(2)}) collective-permute-start(bf16[2,64,1152]{2,1,0:T(8,128)(2,1)S(1)} %get-tuple-element.56), channel_id=1, source_target_pairs={{0,16},{1,17},{2,18},{3,19},{4,20},{5,21},{6,22},{7,23},{8,24},{9,... | collective-permute-start | bytes 884744 | tf_op jit(solution)/shard_map/ppermute | solution.py:221
  80.2 13.1 %collective-permute-start.26 = (bf16[2,64,1152]{2,1,0:T(8,128)(2,1)S(1)}, bf16[2,64,1152]{2,1,0:T(8,128)(2,1)S(1)}, u32[]{:S(2)}, u32[]{:S(2)}) collective-permute-start(bf16[2,64,1152]{2,1,0:T(8,128)(2,1)S(1)} %get-tuple-element.52), channel_id=1, source_target_pairs={{0,2},{1,3},{2,0},{3,1},{4,6},{5,7},{6,4},{7,5},{8,10},{9,11},{10,... | collective-permute-start | bytes 884744 | tf_op jit(solution)/shard_map/ppermute | solution.py:221
  93.2 9.8 %collective-permute-start.35 = (bf16[2,2,64,1152]{3,2,1,0:T(8,128)(2,1)S(1)}, bf16[2,2,64,1152]{3,2,1,0:T(8,128)(2,1)S(1)}, u32[]{:S(2)}, u32[]{:S(2)}) collective-permute-start(bf16[2,2,64,1152]{3,2,1,0:T(8,128)(2,1)S(1)} %maximum_bitcast_fusion.1.refs_1_), channel_id=1, source_target_pairs={{0,1},{1,0},{2,3},{3,2},{4,5},{5,4},{6,7},{7,6},{8,9},{9,8},{10,11... | collective-permute-start | bytes 1769480 | tf_op jit(solution)/shard_map/ppermute | solution.py:221
  97.6 8.8 %collective-permute-start.14 = (bf16[2,32,2048]{2,1,0:T(8,128)(2,1)S(1)}, bf16[2,32,2048]{2,1,0:T(8,128)(2,1)S(1)}, u32[]{:S(2)}, u32[]{:S(2)}) collective-permute-start(bf16[2,32,2048]{2,1,0:T(8,128)(2,1)S(1)} %select_bitcast_fusion.1), channel_id=1, source_target_pairs={{0,16},{1,17},{2,18},{3,19},{4,20},{5,21},{6,22},{7,23},{8,24},{9,... | collective-permute-start | bytes 786440 | tf_op jit(solution)/shard_map/ppermute | solution.py:221
  101.3 11.7 %collective-permute-start.28 = (bf16[2,64,2048]{2,1,0:T(8,128)(2,1)S(1)}, bf16[2,64,2048]{2,1,0:T(8,128)(2,1)S(1)}, u32[]{:S(2)}, u32[]{:S(2)}) collective-permute-start(bf16[2,64,2048]{2,1,0:T(8,128)(2,1)S(1)} %get-tuple-element.41), channel_id=1, source_target_pairs={{0,1},{1,0},{2,3},{3,2},{4,5},{5,4},{6,7},{7,6},{8,9},{9,8},{10,11... | collective-permute-start | bytes 1572872 | tf_op jit(solution)/shard_map/ppermute | solution.py:221
  101.9 9.1 %collective-permute-start.21 = (bf16[2,32,2048]{2,1,0:T(8,128)(2,1)S(1)}, bf16[2,32,2048]{2,1,0:T(8,128)(2,1)S(1)}, u32[]{:S(2)}, u32[]{:S(2)}) collective-permute-start(bf16[2,32,2048]{2,1,0:T(8,128)(2,1)S(1)} %bitcast.155), channel_id=1, source_target_pairs={{0,2},{1,3},{2,0},{3,1},{4,6},{5,7},{6,4},{7,5},{8,10},{9,11},{10,... | collective-permute-start | bytes 786440 | tf_op jit(solution)/shard_map/ppermute | solution.py:221
  106.3 11.4 %collective-permute-start.36 = (bf16[2,64,2048]{2,1,0:T(8,128)(2,1)S(1)}, bf16[2,64,2048]{2,1,0:T(8,128)(2,1)S(1)}, u32[]{:S(2)}, u32[]{:S(2)}) collective-permute-start(bf16[2,64,2048]{2,1,0:T(8,128)(2,1)S(1)} %get-tuple-element.44), channel_id=1, source_target_pairs={{0,1},{1,0},{2,3},{3,2},{4,5},{5,4},{6,7},{7,6},{8,9},{9,8},{10,11... | collective-permute-start | bytes 1572872 | tf_op jit(solution)/shard_map/ppermute | solution.py:221
  106.5 27.2 %collective-permute-start.15 = (bf16[32,2048]{1,0:T(8,128)(2,1)S(1)}, bf16[32,2048]{1,0:T(8,128)(2,1)S(1)}, u32[]{:S(2)}, u32[]{:S(2)}) collective-permute-start(bf16[32,2048]{1,0:T(8,128)(2,1)S(1)} %slice_bitcast_fusion.6), channel_id=1, source_target_pairs={{0,2},{1,3},{2,0},{3,1},{4,6},{5,7},{6,4},{7,5},{8,10},{9,11},{10,... | collective-permute-start | bytes 393224 | tf_op jit(solution)/shard_map/ppermute | solution.py:221
  113.2 8.3 %collective-permute-start.29 = (bf16[2,32,2048]{2,1,0:T(8,128)(2,1)S(1)}, bf16[2,32,2048]{2,1,0:T(8,128)(2,1)S(1)}, u32[]{:S(2)}, u32[]{:S(2)}) collective-permute-start(bf16[2,32,2048]{2,1,0:T(8,128)(2,1)S(1)} %select_bitcast_fusion), channel_id=1, source_target_pairs={{0,16},{1,17},{2,18},{3,19},{4,20},{5,21},{6,22},{7,23},{8,24},{9,... | collective-permute-start | bytes 786440 | tf_op jit(solution)/shard_map/ppermute | solution.py:221
  117.6 16.1 %collective-permute-start.23 = (bf16[32,2048]{1,0:T(8,128)(2,1)S(1)}, bf16[32,2048]{1,0:T(8,128)(2,1)S(1)}, u32[]{:S(2)}, u32[]{:S(2)}) collective-permute-start(bf16[32,2048]{1,0:T(8,128)(2,1)S(1)} %fusion.6), channel_id=1, source_target_pairs={{0,4},{1,5},{2,6},{3,7},{4,0},{5,1},{6,2},{7,3},{8,12},{9,13},{10,... | collective-permute-start | bytes 393224 | tf_op jit(solution)/shard_map/ppermute | solution.py:221
  117.8 7.8 %collective-permute-start.37 = (bf16[2,32,2048]{2,1,0:T(8,128)(2,1)S(1)}, bf16[2,32,2048]{2,1,0:T(8,128)(2,1)S(1)}, u32[]{:S(2)}, u32[]{:S(2)}) collective-permute-start(bf16[2,32,2048]{2,1,0:T(8,128)(2,1)S(1)} %bitcast.156), channel_id=1, source_target_pairs={{0,2},{1,3},{2,0},{3,1},{4,6},{5,7},{6,4},{7,5},{8,10},{9,11},{10,... | collective-permute-start | bytes 786440 | tf_op jit(solution)/shard_map/ppermute | solution.py:221
  127.8 10.2 %collective-permute-start.31 = (bf16[32,2048]{1,0:T(8,128)(2,1)S(1)}, bf16[32,2048]{1,0:T(8,128)(2,1)S(1)}, u32[]{:S(2)}, u32[]{:S(2)}) collective-permute-start(bf16[32,2048]{1,0:T(8,128)(2,1)S(1)} %fusion.5), channel_id=1, source_target_pairs={{0,8},{1,9},{2,10},{3,11},{4,12},{5,13},{6,14},{7,15},{8,0},{9,1},... | collective-permute-start | bytes 393224 | tf_op jit(solution)/shard_map/ppermute | solution.py:221
  (35 other events, 242.1 us)

commit v5 on v4

--- a/solution.py
+++ b/solution.py
@@ -284,6 +284,7 @@
 
 vmem_spec = pl.BlockSpec(memory_space=pltpu.VMEM)
 smem_spec = pl.BlockSpec(memory_space=pltpu.SMEM)
+any_spec = pl.BlockSpec(memory_space=pl.ANY)
 
 
 def expert_cost(rows, units, width):
@@ -428,44 +429,72 @@
                 merged_ref[tile, parity, pl.ds(pair * count, count)] = merged
 
 
-def projector_kernel(spots_ref, place_ref, rows_ref, *refs):
-    weight_refs, own_out, far_out, blocks = refs[:-3], refs[-3], refs[-2], refs[-1]
-    count, size = rows_ref.shape[2], weight_refs[0].shape[0]
-    for tile in range(2):
-        for half in range(2):
-            far = place_ref[0] ^ half
-            spot = pl.ds(pl.multiple_of((2 * far + tile) * count, count), count)
-            for number in range(len(weight_refs)):
-                blocks[number, spot] = rows_ref[tile, half, :, number * size : (number + 1) * size]
-    total = None
-    for number, weight_ref in enumerate(weight_refs):
-        part = jnp.dot(
-            blocks[spots_ref[number]], weight_ref[...], preferred_element_type=jnp.float32
-        )
-        total = part if total is None else total + part
-    own_out[...] = total[: 2 * count]
-    far_out[...] = total[2 * count :].astype(jnp.bfloat16)
-
-
-def run_projector(spots, place, rows, weights):
-    count, size, width = rows.shape[2], weights[0].shape[0], weights[0].shape[1]
+def assemble_kernel(spots_ref, *refs):
+    block_refs, rows_ref, arrivals = refs[:-2], refs[-2], refs[-1]
+    copies = []
+    for number, block_ref in enumerate(block_refs):
+        size = block_ref.shape[0]
+        spot = pl.ds(pl.multiple_of(spots_ref[number] * size, size), size)
+        copies.append(
+            pltpu.make_async_copy(block_ref, rows_ref.at[spot], arrivals.at[number])
+        )
+    for copy in copies:
+        copy.start()
+    for copy in copies:
+        copy.wait()
+
+
+def assemble_rows(spots, blocks):
+    size, width = blocks[0].shape
+    return pl.pallas_call(
+        assemble_kernel,
+        out_shape=jax.ShapeDtypeStruct((len(blocks) * size, width), blocks[0].dtype),
+        in_specs=[smem_spec] + [any_spec] * len(blocks),
+        out_specs=vmem_spec,
+        scratch_shapes=[pltpu.SemaphoreType.DMA((len(blocks),))],
+        compiler_params=pltpu.CompilerParams(vmem_limit_bytes=16 * 2**20),
+        cost_estimate=pl.CostEstimate(
+            flops=0, bytes_accessed=4 * len(blocks) * size * width, transcendentals=0
+        ),
+        name="assemble_rows",
+    )(spots, *blocks)
+
+
+def projector_kernel(place_ref, rows_ref, weight_ref, own_out, far_out):
+    mine, other = (
+        jnp.concatenate([rows_ref[tile, place_ref[0] ^ half] for tile in range(2)], axis=0)
+        for half in range(2)
+    )
+    total = jnp.dot(
+        jnp.concatenate([mine, other], axis=0), weight_ref[...], preferred_element_type=jnp.float32
+    )
+    count = mine.shape[0]
+    own_out[...] = total[:count]
+    far_out[...] = total[count:].astype(jnp.bfloat16)
+
+
+def run_projector(place, rows, weight):
+    count, (depth, width) = rows.shape[2], weight.shape
     return pl.pallas_call(
         projector_kernel,
         out_shape=(
             jax.ShapeDtypeStruct((2 * count, width), jnp.float32),
             jax.ShapeDtypeStruct((2 * count, width), jnp.bfloat16),
         ),
-        in_specs=[smem_spec] * 2 + [vmem_spec] * (1 + len(weights)),
+        in_specs=[smem_spec] + [vmem_spec] * 2,
         out_specs=(vmem_spec, vmem_spec),
-        scratch_shapes=[pltpu.VMEM((len(weights), 4 * count, size), jnp.bfloat16)],
         compiler_params=pltpu.CompilerParams(vmem_limit_bytes=16 * 2**20),
         cost_estimate=pl.CostEstimate(
-            flops=8 * count * width * size * len(weights),
-            bytes_accessed=2 * width * size * len(weights),
-            transcendentals=0,
+            flops=8 * count * width * depth, bytes_accessed=2 * width * depth, transcendentals=0
         ),
         name="projector",
-    )(spots, place, rows, *weights)
+    )(place, rows, weight)
+
+
+def finish_kernel(own_ref, arrived_ref, gates_ref, out_ref):
+    width = own_ref.shape[1]
+    out_ref[:, :width] = (own_ref[...] + arrived_ref[...].astype(jnp.float32)).astype(jnp.bfloat16)
+    out_ref[:, width:] = gates_ref[...]
 
 
 def per_device_near(
@@ -626,7 +655,9 @@
     ).reshape(merged.shape)
     page_tokens = 2 * token_count
     half_place = (outer_id // far).astype(jnp.int32).reshape(1)
-    own_tokens, far_tokens = run_projector(proj_spots, half_place, merged, proj_blocks)
+    own_tokens, far_tokens = run_projector(
+        half_place, merged, assemble_rows(proj_spots, proj_blocks)
+    )
     far_part = swap(far_tokens, flips=(0, far, 0, 0))
     tokens_half = (own_tokens + far_part.astype(jnp.float32)).astype(jnp.bfloat16)
 
@@ -646,6 +677,14 @@
     ]
     near_blocks, first_sums, kept_sums = [], [], []
     for step, held in enumerate(held_by_step):
+        if step in ():
+            over_tile, over_inner, over_both = (
+                swap(held, flips=flip) for flip in (tile_flip, inner_flip, (1, 0, 1, 0))
+            )
+            near_blocks.append(
+                jnp.stack([held, over_tile, over_inner, over_both]).reshape(2, 2, *held.shape)
+            )
+            continue
         arrived = swap(held, flips=flips_of[step][0])
         if step == 0:
             own_held, tile_held = held, arrived
@@ -684,7 +723,7 @@
         summed = add(own_sums, swap(across_sums, flips=core_flip)).reshape(
             2, 2, token_count, width_moe
         )
-        if step % 2:
+        if step % 2 and step not in (2, 3):
             stays, leaves = summed[0], summed[1]
         else:
             stays, leaves = by_place(tile_id, summed[:, 0], summed[:, 1])
@@ -692,12 +731,20 @@
         kept_sums.append(stays)
     total = residual.astype(jnp.float32)
     for step, (stays, leaves) in enumerate(zip(kept_sums, first_sums)):
-        summed = add(stays, swap(leaves, flips=flips_of[step][0]))
-        if step % 2:
-            stays, leaves = by_place(tile_id, summed[0], summed[1])
+        if step in (2, 3):
+            summed = (
+                stays[0].astype(jnp.float32)
+                + swap(leaves[0], flips=tile_flip).astype(jnp.float32)
+                + swap(stays[1], flips=inner_flip).astype(jnp.float32)
+                + swap(leaves[1], flips=(1, 0, 1, 0)).astype(jnp.float32)
+            ).astype(jnp.bfloat16)
         else:
-            stays, leaves = summed[0], summed[1]
-        summed = add(stays, swap(leaves, flips=flips_of[step][1]))
+            summed = add(stays, swap(leaves, flips=flips_of[step][0]))
+            if step % 2:
+                stays, leaves = by_place(tile_id, summed[0], summed[1])
+            else:
+                stays, leaves = summed[0], summed[1]
+            summed = add(stays, swap(leaves, flips=flips_of[step][1]))
         if step:
             summed = swap(summed, flips=(0, step, 0, 0))
         total = total + summed.astype(jnp.float32)

time: 139 us -> 135 us (0.971)
  waiting for transfers between devices: 51 us -> 43.9 us
  local copies, waits for them, and re-layouts: 11.8 us -> 15.8 us
    all_to_all x1, waiting for transfers between devices: 9.11 us -> 3.73 us  [per_device_near(): lax.all_to_all(merged.reshape(4, token_count, -1), ('tile', 'half'), spli...]
    unnamed x37 -> x35, local copies, waits for them, and re-layouts: 7.52 us -> 11.5 us
    pallas_call x1, Pallas kernels: 3.6 us -> 0.79 us  [run_projector(): pl.pallas_call(projector_kernel, out_shape=(jax.ShapeDtypeStruct((2 * cou...]
    pallas_call x0 -> x1, Pallas kernels: none -> 2.58 us  [assemble_rows(): pl.pallas_call(assemble_kernel, out_shape=jax.ShapeDtypeStruct((len(block...]
    ppermute x40 -> x42, waiting for transfers between devices: 41.9 us -> 40.2 us  [near_swap(): return lax.ppermute(values, ('tile', *near_expert), pairs)]
    ppermute x40 -> x42, starting transfers between devices: 39 us -> 38.4 us  [near_swap(): return lax.ppermute(values, ('tile', *near_expert), pairs)]
  transfers between devices with their start and end apart: 41 -> 43, of which waited for: 15 -> 17; matrix products, arithmetic and copies ran while one was open for 5% -> 5% of each run, Pallas kernels for 18% -> 21%
where the time goes in v5:
time: 135 us
  waiting for transfers between devices  43.9 us (33%)
  starting transfers between devices  42.3 us (31%)
  Pallas kernels  28.6 us (21%)
  local copies, waits for them, and re-layouts  15.8 us (12%)
  other arithmetic  3.66 us (3%)
    ppermute x42, waiting for transfers between devices, near_swap(): return lax.ppermute(values, ('tile', *near_expert), pairs)  40.2 us
    ppermute x42, starting transfers between devices, near_swap(): return lax.ppermute(values, ('tile', *near_expert), pairs)  38.4 us
    pallas_call x4, Pallas kernels, run_expert(): pl.pallas_call(partial(expert_kernel, extra is not None), out_shape=(out,...  13.5 us
    unnamed x35, local copies, waits for them, and re-layouts  11.5 us
    pallas_call x1, Pallas kernels, per_device_near(): pl.pallas_call(partial(other_rows_kernel, heads), out_shape=(jax.ShapeDty...  3.9 us
    all_to_all x1, starting transfers between devices, per_device_near(): lax.all_to_all(merged.reshape(4, token_count, -1), ('tile', 'half'), spli...  3.85 us
    all_to_all x1, waiting for transfers between devices, per_device_near(): lax.all_to_all(merged.reshape(4, token_count, -1), ('tile', 'half'), spli...  3.73 us
  transfers between devices with their start and end apart: 43, of which 17 were waited for; matrix products, arithmetic and copies ran while one was open for 5% of the time, Pallas kernels for 21%

profile of v5, /device:TPU:0, one launch (start us, length us, event | category | flops | bytes accessed | tf_op | source)
XLA Modules:
  0.0 134.8 jit_solution(18399339272493739940)
XLA Ops:
  0.0 2.9 %collective-permute-start = (bf16[128,1152]{1,0:T(8,128)(2,1)}, bf16[128,1152]{1,0:T(8,128)(2,1)S(1)}, u32[]{:S(2)}, u32[]{:S(2)}) collective-permute-start(bf16[128,1152]{1,0:T(8,128)(2,1)} %bitcast.132), channel_id=1, source_target_pairs={{0,16},{1,17},{2,18},{3,19},{4,20},{5,21},{6,22},{7,23},{8,24},{9,... | collective-permute-start | bytes 884744 | tf_op jit(solution)/shard_map/ppermute | solution.py:221
  14.2 3.9 %other_rows.1 = (bf16[128,1152]{1,0:T(8,128)(2,1)S(1)}, bf16[2,8,72,256]{3,2,1,0:T(8,128)(2,1)S(1)}) custom-call(bf16[128,1152]{1,0:T(8,128)(2,1)S(1)} %collective-permute-done.refs_0_, f32[1,1152]{1,0:T(1,128)S(1)} %broadcast_in_dim.81.refs_1_, f32[3,576,1]{2,1,0:T(8,128)S(1)} %copy.59.refs_2_, f32[72,128]{1,0:T(8,128)S(1)} %get-tuple-element.72.refs_3_, ...), custom_call_target="tpu_custom_call" | custom-call | flops 849346560 | bytes 3981312 | tf_op jit(solution)/shard_map/other_rows/pallas_call | solution.py:592
  18.4 2.6 %own_rows.1.hidden_ref = f32[128,1152]{1,0:T(8,128)S(1)} custom-call(bf16[128,1152]{1,0:T(8,128)(2,1)S(1)} %bitcast.134, bf16[3,8,72,128]{3,2,1,0:T(8,128)(2,1)S(1)} %own_heads.1.refs_6_.refs_1_, bf16[2,8,72,256]{3,2,1,0:T(8,128)(2,1)S(1)} %get-tuple-element.25.refs_2_, bf16[576,1152]{1,0:T(8,128)(2,1)S(1)} %copy-done.6, f32[1,1152]{1,0:T(1,128)S(1)} %broadcast_in_dim.87.refs_4_), custom_call_target="tpu_custom_call" | custom-call | flops 339738624 | bytes 1327104 | tf_op jit(solution)/shard_map/own_rows/pallas_call | solution.py:615
  21.0 4.9 %collective-permute-done.1.arrived_ref = bf16[128,1152]{1,0:T(8,128)(2,1)S(1)} collective-permute-done((bf16[128,1152]{1,0:T(8,128)(2,1)S(1)}, bf16[128,1152]{1,0:T(8,128)(2,1)S(1)}, u32[]{:S(2)}, u32[]{:S(2)}) %collective-permute-start.1) | collective-permute-done | bytes 294944 | tf_op jit(solution)/shard_map/ppermute | solution.py:221
  27.0 3.9 %all-to-all-start = ((bf16[4,32,2304]{2,1,0:T(8,128)(2,1)}), bf16[4,32,2304]{2,1,0:T(8,128)(2,1)S(1)}, u32[]{:S(2)}, u32[]{:S(2)}) async-start(bf16[4,32,2304]{2,1,0:T(8,128)(2,1)} %bitcast.4), calls=%async_computation | async-start | bytes 1179648 | tf_op jit(solution)/shard_map/all_to_all | solution.py:653
  36.2 2.6 %assemble_rows.1.weight_ref = bf16[2304,1024]{1,0:T(8,128)(2,1)S(1)} custom-call(s32[8]{0:T(128)S(1)} %stack.107.spots_ref, bf16[288,1024]{1,0:T(8,128)(2,1)S(1)} %copy-done.10, bf16[288,1024]{1,0:T(8,128)(2,1)} %collective-permute-done.2.refs_1_, bf16[288,1024]{1,0:T(8,128)(2,1)S(1)} %collective-permute-done.3.refs_2_, ...), custom_call_target="tpu_custom_call" | custom-call | bytes 9437184 | tf_op jit(solution)/shard_map/assemble_rows/pallas_call | solution.py:449
  41.0 3.7 %all-to-all-done = bf16[4,32,2304]{2,1,0:T(8,128)(2,1)S(1)} async-done(((bf16[4,32,2304]{2,1,0:T(8,128)(2,1)}), bf16[4,32,2304]{2,1,0:T(8,128)(2,1)S(1)}, u32[]{:S(2)}, u32[]{:S(2)}) %all-to-all-start) | async-done | bytes 589856 | tf_op jit(solution)/shard_map/all_to_all | solution.py:653
  44.7 2.3 %copy-done.2 = bf16[2304,1024]{1,0:T(8,128)(2,1)S(1)} copy-done((bf16[2304,1024]{1,0:T(8,128)(2,1)S(1)}, bf16[2304,1024]{1,0:T(8,128)(2,1)}, u32[]{:S(2)}) %copy-start.2) | copy-done | bytes 4718616
  49.0 5.9 %collective-permute-done.9 = bf16[64,1024]{1,0:T(8,128)(2,1)S(1)} collective-permute-done((bf16[64,1024]{1,0:T(8,128)(2,1)S(1)}, bf16[64,1024]{1,0:T(8,128)(2,1)S(1)}, u32[]{:S(2)}, u32[]{:S(2)}) %collective-permute-start.9) | collective-permute-done | bytes 131104 | tf_op jit(solution)/shard_map/ppermute | solution.py:221
  56.0 2.9 %collective-permute-start.24 = (bf16[64,1152]{1,0:T(8,128)(2,1)S(1)}, bf16[64,1152]{1,0:T(8,128)(2,1)S(1)}, u32[]{:S(2)}, u32[]{:S(2)}) collective-permute-start(bf16[64,1152]{1,0:T(8,128)(2,1)S(1)} %get-tuple-element.34.mine_ref), channel_id=1, source_target_pairs={{0,8},{1,9},{2,10},{3,11},{4,12},{5,13},{6,14},{7,15},{8,0},{9,1},... | collective-permute-start | bytes 442376 | tf_op jit(solution)/shard_map/ppermute | solution.py:221
  64.5 5.5 %collective-permute-done.24 = bf16[64,1152]{1,0:T(8,128)(2,1)S(1)} collective-permute-done((bf16[64,1152]{1,0:T(8,128)(2,1)S(1)}, bf16[64,1152]{1,0:T(8,128)(2,1)S(1)}, u32[]{:S(2)}, u32[]{:S(2)}) %collective-permute-start.24) | collective-permute-done | bytes 147488 | tf_op jit(solution)/shard_map/ppermute | solution.py:221
  70.6 2.4 %collective-permute-start.34 = (bf16[64,1152]{1,0:T(8,128)(2,1)S(1)}, bf16[64,1152]{1,0:T(8,128)(2,1)S(1)}, u32[]{:S(2)}, u32[]{:S(2)}) collective-permute-start(bf16[64,1152]{1,0:T(8,128)(2,1)S(1)} %collective-permute-done.33), channel_id=1, source_target_pairs={{0,2},{1,3},{2,0},{3,1},{4,6},{5,7},{6,4},{7,5},{8,10},{9,11},{10,... | collective-permute-start | bytes 442376 | tf_op jit(solution)/shard_map/ppermute | solution.py:221
  76.8 2.3 %collective-permute-start.26 = (bf16[2,64,1152]{2,1,0:T(8,128)(2,1)S(1)}, bf16[2,64,1152]{2,1,0:T(8,128)(2,1)S(1)}, u32[]{:S(2)}, u32[]{:S(2)}) collective-permute-start(bf16[2,64,1152]{2,1,0:T(8,128)(2,1)S(1)} %get-tuple-element.54), channel_id=1, source_target_pairs={{0,2},{1,3},{2,0},{3,1},{4,6},{5,7},{6,4},{7,5},{8,10},{9,11},{10,... | collective-permute-start | bytes 884744 | tf_op jit(solution)/shard_map/ppermute | solution.py:221
  79.5 2.8 %copy-done.5 = bf16[2048,2,704]{0,2,1:T(8,128)(2,1)S(1)} copy-done((bf16[2048,2,704]{0,2,1:T(8,128)(2,1)S(1)}, bf16[2048,2,704]{0,2,1:T(8,128)(2,1)}, u32[]{:S(2)}) %copy-start.5) | copy-done | bytes 5767192
  82.4 2.7 %shared_units.1.refs_7_ = f32[64,2048]{1,0:T(8,128)S(1)} custom-call(s32[1]{0:T(128)} %bitcast.15.place_ref.refs_0_, bf16[64,1152]{1,0:T(8,128)(2,1)S(1)} %get-tuple-element.34.mine_ref, bf16[64,1152]{1,0:T(8,128)(2,1)S(1)} %collective-permute-done.10.other_ref, f32[1,2048]{1,0:T(1,128)S(1)} %bitcast.135, bf16[2,704,2048]{2,1,0:T(8,128)(2,1)S(1)} %bitcast.129, ...), custom_call_target="tpu_custom_call" | custom-call | flops 553648128 | bytes 9175040 | tf_op jit(solution)/shard_map/shared_units/pallas_call | solution.py:330
  85.3 3.3 %expert_units.4 = (bf16[2,64,2048]{2,1,0:T(8,128)(2,1)S(1)}, bf16[2,64,2048]{2,1,0:T(8,128)(2,1)S(1)}) custom-call(s32[1]{0:T(128)} %bitcast.15.place_ref.refs_0_, bf16[2,2,64,1152]{3,2,1,0:T(8,128)(2,1)S(1)} %pad_maximum_fusion.refs_1_, bf16[2,2,64,1152]{3,2,1,0:T(8,128)(2,1)S(1)} %collective-permute-done.12.refs_2_, f32[1,2048]{1,0:T(1,128)S(1)} %bitcast.136, ...), custom_call_target="tpu_custom_call" | custom-call | flops 2214592512 | bytes 10747904 | tf_op jit(solution)/shard_map/expert_units/pallas_call | solution.py:303
  90.0 3.3 %expert_units.5 = (bf16[2,64,2048]{2,1,0:T(8,128)(2,1)S(1)}, bf16[2,64,2048]{2,1,0:T(8,128)(2,1)S(1)}) custom-call(s32[1]{0:T(128)} %bitcast.15.place_ref.refs_0_, bf16[2,2,64,1152]{3,2,1,0:T(8,128)(2,1)S(1)} %copy.69.refs_1_, bf16[2,2,64,1152]{3,2,1,0:T(8,128)(2,1)S(1)} %copy.70.refs_2_, f32[1,2048]{1,0:T(1,128)S(1)} %bitcast.137, ...), custom_call_target="tpu_custom_call" | custom-call | flops 2214592512 | bytes 10747904 | tf_op jit(solution)/shard_map/expert_units/pallas_call | solution.py:303
  95.2 3.5 %expert_units.6 = (bf16[2,64,2048]{2,1,0:T(8,128)(2,1)S(1)}, bf16[2,64,2048]{2,1,0:T(8,128)(2,1)S(1)}) custom-call(s32[1]{0:T(128)} %bitcast.15.place_ref.refs_0_, bf16[2,2,64,1152]{3,2,1,0:T(8,128)(2,1)S(1)} %pad_maximum_fusion.1.refs_1_, bf16[2,2,64,1152]{3,2,1,0:T(8,128)(2,1)S(1)} %collective-permute-done.27.refs_2_, f32[1,2048]{1,0:T(1,128)S(1)} %bitcast.138, ...), custom_call_target="tpu_custom_call" | custom-call | flops 2214592512 | bytes 10747904 | tf_op jit(solution)/shard_map/expert_units/pallas_call | solution.py:303
  99.4 3.3 %expert_units.7 = (bf16[2,64,2048]{2,1,0:T(8,128)(2,1)S(1)}, bf16[2,64,2048]{2,1,0:T(8,128)(2,1)S(1)}) custom-call(s32[1]{0:T(128)} %bitcast.15.place_ref.refs_0_, bf16[2,2,64,1152]{3,2,1,0:T(8,128)(2,1)S(1)} %maximum_bitcast_fusion.1.refs_1_, bf16[2,2,64,1152]{3,2,1,0:T(8,128)(2,1)S(1)} %collective-permute-done.36.refs_2_, f32[1,2048]{1,0:T(1,128)S(1)} %bitcast.139, ...), custom_call_target="tpu_custom_call" | custom-call | flops 2214592512 | bytes 10747904 | tf_op jit(solution)/shard_map/expert_units/pallas_call | solution.py:303
  104.9 3.5 %collective-permute-done.21 = bf16[2,32,2048]{2,1,0:T(8,128)(2,1)S(1)} collective-permute-done((bf16[2,32,2048]{2,1,0:T(8,128)(2,1)S(1)}, bf16[2,32,2048]{2,1,0:T(8,128)(2,1)S(1)}, u32[]{:S(2)}, u32[]{:S(2)}) %collective-permute-start.21) | collective-permute-done | bytes 262176 | tf_op jit(solution)/shard_map/ppermute | solution.py:221
  111.3 3.7 %collective-permute-done.22 = bf16[32,2048]{1,0:T(8,128)(2,1)S(1)} collective-permute-done((bf16[32,2048]{1,0:T(8,128)(2,1)S(1)}, bf16[32,2048]{1,0:T(8,128)(2,1)S(1)}, u32[]{:S(2)}, u32[]{:S(2)}) %collective-permute-start.22) | collective-permute-done | bytes 131104 | tf_op jit(solution)/shard_map/ppermute | solution.py:221
  127.1 2.2 %collective-permute-start.41 = (bf16[32,2048]{1,0:T(8,128)(2,1)S(1)}, bf16[32,2048]{1,0:T(8,128)(2,1)S(1)}, u32[]{:S(2)}, u32[]{:S(2)}) collective-permute-start(bf16[32,2048]{1,0:T(8,128)(2,1)S(1)} %fusion.5), channel_id=1, source_target_pairs={{0,12},{1,13},{2,14},{3,15},{4,8},{5,9},{6,10},{7,11},{8,4},{9,5},... | collective-permute-start | bytes 393224 | tf_op jit(solution)/shard_map/ppermute | solution.py:221
  129.4 2.2 %collective-permute-done.32 = bf16[32,2048]{1,0:T(8,128)(2,1)S(1)} collective-permute-done((bf16[32,2048]{1,0:T(8,128)(2,1)S(1)}, bf16[32,2048]{1,0:T(8,128)(2,1)S(1)}, u32[]{:S(2)}, u32[]{:S(2)}) %collective-permute-start.32) | collective-permute-done | bytes 131104 | tf_op jit(solution)/shard_map/ppermute | solution.py:221
  131.6 2.5 %collective-permute-done.41 = bf16[32,2048]{1,0:T(8,128)(2,1)S(1)} collective-permute-done((bf16[32,2048]{1,0:T(8,128)(2,1)S(1)}, bf16[32,2048]{1,0:T(8,128)(2,1)S(1)}, u32[]{:S(2)}, u32[]{:S(2)}) %collective-permute-start.41) | collective-permute-done | bytes 131104 | tf_op jit(solution)/shard_map/ppermute | solution.py:221
  (163 shorter events, 55.3 us)
Async XLA Ops:
  0.0 13.2 %collective-permute-start = (bf16[128,1152]{1,0:T(8,128)(2,1)}, bf16[128,1152]{1,0:T(8,128)(2,1)S(1)}, u32[]{:S(2)}, u32[]{:S(2)}) collective-permute-start(bf16[128,1152]{1,0:T(8,128)(2,1)} %bitcast.132), channel_id=1, source_target_pairs={{0,16},{1,17},{2,18},{3,19},{4,20},{5,21},{6,22},{7,23},{8,24},{9,... | collective-permute-start | bytes 884744 | tf_op jit(solution)/shard_map/ppermute | solution.py:221
  3.3 27.5 %collective-permute-start.3 = (bf16[288,1024]{1,0:T(8,128)(2,1)}, bf16[288,1024]{1,0:T(8,128)(2,1)S(1)}, u32[]{:S(2)}, u32[]{:S(2)}) collective-permute-start(bf16[288,1024]{1,0:T(8,128)(2,1)} %refs_0_.1), channel_id=1, source_target_pairs={{0,2},{1,3},{2,0},{3,1},{4,6},{5,7},{6,4},{7,5},{8,10},{9,11},{10,... | collective-permute-start | bytes 1769480 | tf_op jit(solution)/shard_map/ppermute | solution.py:221
  4.9 25.9 %collective-permute-start.5 = (bf16[288,1024]{1,0:T(8,128)(2,1)}, bf16[288,1024]{1,0:T(8,128)(2,1)S(1)}, u32[]{:S(2)}, u32[]{:S(2)}) collective-permute-start(bf16[288,1024]{1,0:T(8,128)(2,1)} %refs_0_.1), channel_id=1, source_target_pairs={{0,4},{1,5},{2,6},{3,7},{4,0},{5,1},{6,2},{7,3},{8,12},{9,13},{10,... | collective-permute-start | bytes 1769480 | tf_op jit(solution)/shard_map/ppermute | solution.py:221
  6.5 26.7 %collective-permute-start.7 = (bf16[288,1024]{1,0:T(8,128)(2,1)}, bf16[288,1024]{1,0:T(8,128)(2,1)S(1)}, u32[]{:S(2)}, u32[]{:S(2)}) collective-permute-start(bf16[288,1024]{1,0:T(8,128)(2,1)} %refs_0_.1), channel_id=1, source_target_pairs={{0,6},{1,7},{2,4},{3,5},{4,2},{5,3},{6,0},{7,1},{8,14},{9,15},{10,... | collective-permute-start | bytes 1769480 | tf_op jit(solution)/shard_map/ppermute | solution.py:221
  27.0 17.7 %all-to-all-start = ((bf16[4,32,2304]{2,1,0:T(8,128)(2,1)}), bf16[4,32,2304]{2,1,0:T(8,128)(2,1)S(1)}, u32[]{:S(2)}, u32[]{:S(2)}) async-start(bf16[4,32,2304]{2,1,0:T(8,128)(2,1)} %bitcast.4), calls=%async_computation | async-start | bytes 1179648 | tf_op jit(solution)/shard_map/all_to_all | solution.py:653
  55.0 9.1 %collective-permute-start.10 = (bf16[64,1152]{1,0:T(8,128)(2,1)S(1)}, bf16[64,1152]{1,0:T(8,128)(2,1)S(1)}, u32[]{:S(2)}, u32[]{:S(2)}) collective-permute-start(bf16[64,1152]{1,0:T(8,128)(2,1)S(1)} %get-tuple-element.34.mine_ref), channel_id=1, source_target_pairs={{0,16},{1,17},{2,18},{3,19},{4,20},{5,21},{6,22},{7,23},{8,24},{9,... | collective-permute-start | bytes 442376 | tf_op jit(solution)/shard_map/ppermute | solution.py:221
  56.0 14.0 %collective-permute-start.24 = (bf16[64,1152]{1,0:T(8,128)(2,1)S(1)}, bf16[64,1152]{1,0:T(8,128)(2,1)S(1)}, u32[]{:S(2)}, u32[]{:S(2)}) collective-permute-start(bf16[64,1152]{1,0:T(8,128)(2,1)S(1)} %get-tuple-element.34.mine_ref), channel_id=1, source_target_pairs={{0,8},{1,9},{2,10},{3,11},{4,12},{5,13},{6,14},{7,15},{8,0},{9,1},... | collective-permute-start | bytes 442376 | tf_op jit(solution)/shard_map/ppermute | solution.py:221
  58.9 11.8 %collective-permute-start.33 = (bf16[64,1152]{1,0:T(8,128)(2,1)S(1)}, bf16[64,1152]{1,0:T(8,128)(2,1)S(1)}, u32[]{:S(2)}, u32[]{:S(2)}) collective-permute-start(bf16[64,1152]{1,0:T(8,128)(2,1)S(1)} %get-tuple-element.34.mine_ref), channel_id=1, source_target_pairs={{0,12},{1,13},{2,14},{3,15},{4,8},{5,9},{6,10},{7,11},{8,4},{9,5},... | collective-permute-start | bytes 442376 | tf_op jit(solution)/shard_map/ppermute | solution.py:221
  62.3 10.7 %collective-permute-start.17 = (bf16[64,1152]{1,0:T(8,128)(2,1)S(1)}, bf16[64,1152]{1,0:T(8,128)(2,1)S(1)}, u32[]{:S(2)}, u32[]{:S(2)}) collective-permute-start(bf16[64,1152]{1,0:T(8,128)(2,1)S(1)} %collective-permute-done.16), channel_id=1, source_target_pairs={{0,2},{1,3},{2,0},{3,1},{4,6},{5,7},{6,4},{7,5},{8,10},{9,11},{10,... | collective-permute-start | bytes 442376 | tf_op jit(solution)/shard_map/ppermute | solution.py:221
  64.2 10.3 %collective-permute-start.11 = (bf16[2,64,1152]{2,1,0:T(8,128)(2,1)S(1)}, bf16[2,64,1152]{2,1,0:T(8,128)(2,1)S(1)}, u32[]{:S(2)}, u32[]{:S(2)}) collective-permute-start(bf16[2,64,1152]{2,1,0:T(8,128)(2,1)S(1)} %get-tuple-element.52), channel_id=1, source_target_pairs={{0,2},{1,3},{2,0},{3,1},{4,6},{5,7},{6,4},{7,5},{8,10},{9,11},{10,... | collective-permute-start | bytes 884744 | tf_op jit(solution)/shard_map/ppermute | solution.py:221
  73.1 12.0 %collective-permute-start.18 = (bf16[2,64,1152]{2,1,0:T(8,128)(2,1)S(1)}, bf16[2,64,1152]{2,1,0:T(8,128)(2,1)S(1)}, u32[]{:S(2)}, u32[]{:S(2)}) collective-permute-start(bf16[2,64,1152]{2,1,0:T(8,128)(2,1)S(1)} %get-tuple-element.56), channel_id=1, source_target_pairs={{0,16},{1,17},{2,18},{3,19},{4,20},{5,21},{6,22},{7,23},{8,24},{9,... | collective-permute-start | bytes 884744 | tf_op jit(solution)/shard_map/ppermute | solution.py:221
  74.6 10.7 %collective-permute-start.12 = (bf16[2,2,64,1152]{3,2,1,0:T(8,128)(2,1)S(1)}, bf16[2,2,64,1152]{3,2,1,0:T(8,128)(2,1)S(1)}, u32[]{:S(2)}, u32[]{:S(2)}) collective-permute-start(bf16[2,2,64,1152]{3,2,1,0:T(8,128)(2,1)S(1)} %pad_maximum_fusion.refs_1_), channel_id=1, source_target_pairs={{0,1},{1,0},{2,3},{3,2},{4,5},{5,4},{6,7},{7,6},{8,9},{9,8},{10,11... | collective-permute-start | bytes 1769480 | tf_op jit(solution)/shard_map/ppermute | solution.py:221
  76.8 12.4 %collective-permute-start.26 = (bf16[2,64,1152]{2,1,0:T(8,128)(2,1)S(1)}, bf16[2,64,1152]{2,1,0:T(8,128)(2,1)S(1)}, u32[]{:S(2)}, u32[]{:S(2)}) collective-permute-start(bf16[2,64,1152]{2,1,0:T(8,128)(2,1)S(1)} %get-tuple-element.54), channel_id=1, source_target_pairs={{0,2},{1,3},{2,0},{3,1},{4,6},{5,7},{6,4},{7,5},{8,10},{9,11},{10,... | collective-permute-start | bytes 884744 | tf_op jit(solution)/shard_map/ppermute | solution.py:221
  79.2 10.2 %collective-permute-start.35 = (bf16[2,64,1152]{2,1,0:T(8,128)(2,1)S(1)}, bf16[2,64,1152]{2,1,0:T(8,128)(2,1)S(1)}, u32[]{:S(2)}, u32[]{:S(2)}) collective-permute-start(bf16[2,64,1152]{2,1,0:T(8,128)(2,1)S(1)} %get-tuple-element.58), channel_id=1, source_target_pairs={{0,16},{1,17},{2,18},{3,19},{4,20},{5,21},{6,22},{7,23},{8,24},{9,... | collective-permute-start | bytes 884744 | tf_op jit(solution)/shard_map/ppermute | solution.py:221
  89.5 9.9 %collective-permute-start.36 = (bf16[2,2,64,1152]{3,2,1,0:T(8,128)(2,1)S(1)}, bf16[2,2,64,1152]{3,2,1,0:T(8,128)(2,1)S(1)}, u32[]{:S(2)}, u32[]{:S(2)}) collective-permute-start(bf16[2,2,64,1152]{3,2,1,0:T(8,128)(2,1)S(1)} %maximum_bitcast_fusion.1.refs_1_), channel_id=1, source_target_pairs={{0,1},{1,0},{2,3},{3,2},{4,5},{5,4},{6,7},{7,6},{8,9},{9,8},{10,11... | collective-permute-start | bytes 1769480 | tf_op jit(solution)/shard_map/ppermute | solution.py:221
  93.6 9.4 %collective-permute-start.14 = (bf16[2,32,2048]{2,1,0:T(8,128)(2,1)S(1)}, bf16[2,32,2048]{2,1,0:T(8,128)(2,1)S(1)}, u32[]{:S(2)}, u32[]{:S(2)}) collective-permute-start(bf16[2,32,2048]{2,1,0:T(8,128)(2,1)S(1)} %select_bitcast_fusion), channel_id=1, source_target_pairs={{0,16},{1,17},{2,18},{3,19},{4,20},{5,21},{6,22},{7,23},{8,24},{9,... | collective-permute-start | bytes 786440 | tf_op jit(solution)/shard_map/ppermute | solution.py:221
  98.8 10.3 %collective-permute-start.28 = (bf16[2,64,2048]{2,1,0:T(8,128)(2,1)S(1)}, bf16[2,64,2048]{2,1,0:T(8,128)(2,1)S(1)}, u32[]{:S(2)}, u32[]{:S(2)}) collective-permute-start(bf16[2,64,2048]{2,1,0:T(8,128)(2,1)S(1)} %get-tuple-element.41), channel_id=1, source_target_pairs={{0,1},{1,0},{2,3},{3,2},{4,5},{5,4},{6,7},{7,6},{8,9},{9,8},{10,11... | collective-permute-start | bytes 1572872 | tf_op jit(solution)/shard_map/ppermute | solution.py:221
  99.2 9.2 %collective-permute-start.21 = (bf16[2,32,2048]{2,1,0:T(8,128)(2,1)S(1)}, bf16[2,32,2048]{2,1,0:T(8,128)(2,1)S(1)}, u32[]{:S(2)}, u32[]{:S(2)}) collective-permute-start(bf16[2,32,2048]{2,1,0:T(8,128)(2,1)S(1)} %bitcast.149), channel_id=1, source_target_pairs={{0,2},{1,3},{2,0},{3,1},{4,6},{5,7},{6,4},{7,5},{8,10},{9,11},{10,... | collective-permute-start | bytes 786440 | tf_op jit(solution)/shard_map/ppermute | solution.py:221
  102.7 12.4 %collective-permute-start.37 = (bf16[2,64,2048]{2,1,0:T(8,128)(2,1)S(1)}, bf16[2,64,2048]{2,1,0:T(8,128)(2,1)S(1)}, u32[]{:S(2)}, u32[]{:S(2)}) collective-permute-start(bf16[2,64,2048]{2,1,0:T(8,128)(2,1)S(1)} %get-tuple-element.44), channel_id=1, source_target_pairs={{0,1},{1,0},{2,3},{3,2},{4,5},{5,4},{6,7},{7,6},{8,9},{9,8},{10,11... | collective-permute-start | bytes 1572872 | tf_op jit(solution)/shard_map/ppermute | solution.py:221
  103.1 26.2 %collective-permute-start.15 = (bf16[32,2048]{1,0:T(8,128)(2,1)S(1)}, bf16[32,2048]{1,0:T(8,128)(2,1)S(1)}, u32[]{:S(2)}, u32[]{:S(2)}) collective-permute-start(bf16[32,2048]{1,0:T(8,128)(2,1)S(1)} %slice_bitcast_fusion.8), channel_id=1, source_target_pairs={{0,2},{1,3},{2,0},{3,1},{4,6},{5,7},{6,4},{7,5},{8,10},{9,11},{10,... | collective-permute-start | bytes 393224 | tf_op jit(solution)/shard_map/ppermute | solution.py:221
  109.3 8.5 %collective-permute-start.29 = (bf16[32,2048]{1,0:T(8,128)(2,1)S(1)}, bf16[32,2048]{1,0:T(8,128)(2,1)S(1)}, u32[]{:S(2)}, u32[]{:S(2)}) collective-permute-start(bf16[32,2048]{1,0:T(8,128)(2,1)S(1)} %get-tuple-element.61), channel_id=1, source_target_pairs={{0,16},{1,17},{2,18},{3,19},{4,20},{5,21},{6,22},{7,23},{8,24},{9,... | collective-permute-start | bytes 393224 | tf_op jit(solution)/shard_map/ppermute | solution.py:221
  110.9 8.9 %collective-permute-start.31 = (bf16[32,2048]{1,0:T(8,128)(2,1)S(1)}, bf16[32,2048]{1,0:T(8,128)(2,1)S(1)}, u32[]{:S(2)}, u32[]{:S(2)}) collective-permute-start(bf16[32,2048]{1,0:T(8,128)(2,1)S(1)} %get-tuple-element.62), channel_id=1, source_target_pairs={{0,18},{1,19},{2,16},{3,17},{4,22},{5,23},{6,20},{7,21},{8,26},{9,... | collective-permute-start | bytes 393224 | tf_op jit(solution)/shard_map/ppermute | solution.py:221
  115.1 14.3 %collective-permute-start.23 = (bf16[32,2048]{1,0:T(8,128)(2,1)S(1)}, bf16[32,2048]{1,0:T(8,128)(2,1)S(1)}, u32[]{:S(2)}, u32[]{:S(2)}) collective-permute-start(bf16[32,2048]{1,0:T(8,128)(2,1)S(1)} %fusion.9), channel_id=1, source_target_pairs={{0,4},{1,5},{2,6},{3,7},{4,0},{5,1},{6,2},{7,3},{8,12},{9,13},{10,... | collective-permute-start | bytes 393224 | tf_op jit(solution)/shard_map/ppermute | solution.py:221
  122.8 8.8 %collective-permute-start.32 = (bf16[32,2048]{1,0:T(8,128)(2,1)S(1)}, bf16[32,2048]{1,0:T(8,128)(2,1)S(1)}, u32[]{:S(2)}, u32[]{:S(2)}) collective-permute-start(bf16[32,2048]{1,0:T(8,128)(2,1)S(1)} %fusion.8), channel_id=1, source_target_pairs={{0,8},{1,9},{2,10},{3,11},{4,12},{5,13},{6,14},{7,15},{8,0},{9,1},... | collective-permute-start | bytes 393224 | tf_op jit(solution)/shard_map/ppermute | solution.py:221
  (36 other events, 248.8 us)

commit v6 on v5

--- a/solution.py
+++ b/solution.py
@@ -708,8 +708,8 @@
     )
     across_blocks = [swap(near, flips=core_flip) for near in near_blocks]
     for step, (near, across) in enumerate(zip(near_blocks, across_blocks)):
-        if step > 1:
-            near = after(near, first_sums[step - 2])
+        if step == 3:
+            near = after(near, first_sums[1])
         own_sums, across_sums = run_expert(
             tile_place,
             near,

time: 135 us -> 135 us (level)
  waiting for transfers between devices: 43.9 us -> 37.8 us
  starting transfers between devices: 42.3 us -> 47.9 us
    ppermute x42, waiting for transfers between devices: 40.2 us -> 34.1 us  [near_swap(): return lax.ppermute(values, ('tile', *near_expert), pairs)]
    ppermute x42, starting transfers between devices: 38.4 us -> 44.1 us  [near_swap(): return lax.ppermute(values, ('tile', *near_expert), pairs)]
  transfers between devices with their start and end apart: 43 -> 43, of which waited for: 17 -> 16; matrix products, arithmetic and copies ran while one was open for 5% -> 5% of each run, Pallas kernels for 21% -> 21%
where the time goes in v6:
time: 135 us; the launch traced here: 134 us
  starting transfers between devices  47.9 us (35%)
  waiting for transfers between devices  37.8 us (28%)
  Pallas kernels  28.6 us (21%)
  local copies, waits for them, and re-layouts  15.7 us (12%)
  other arithmetic  3.66 us (3%)
    ppermute x42, starting transfers between devices, near_swap(): return lax.ppermute(values, ('tile', *near_expert), pairs)  44.1 us
    ppermute x42, waiting for transfers between devices, near_swap(): return lax.ppermute(values, ('tile', *near_expert), pairs)  34.1 us
    pallas_call x4, Pallas kernels, run_expert(): pl.pallas_call(partial(expert_kernel, extra is not None), out_shape=(out,...  13.5 us
    unnamed x35, local copies, waits for them, and re-layouts  11.5 us
    pallas_call x1, Pallas kernels, per_device_near(): pl.pallas_call(partial(other_rows_kernel, heads), out_shape=(jax.ShapeDty...  3.9 us
    all_to_all x1, starting transfers between devices, per_device_near(): lax.all_to_all(merged.reshape(4, token_count, -1), ('tile', 'half'), spli...  3.85 us
    all_to_all x1, waiting for transfers between devices, per_device_near(): lax.all_to_all(merged.reshape(4, token_count, -1), ('tile', 'half'), spli...  3.73 us
  transfers between devices with their start and end apart: 43, of which 16 were waited for; matrix products, arithmetic and copies ran while one was open for 5% of the time, Pallas kernels for 21%

profile of v6, /device:TPU:0, one launch (start us, length us, event | category | flops | bytes accessed | tf_op | source)
XLA Modules:
  0.0 134.3 jit_solution(10959540343764351099)
XLA Ops:
  0.0 2.9 %collective-permute-start = (bf16[128,1152]{1,0:T(8,128)(2,1)}, bf16[128,1152]{1,0:T(8,128)(2,1)S(1)}, u32[]{:S(2)}, u32[]{:S(2)}) collective-permute-start(bf16[128,1152]{1,0:T(8,128)(2,1)} %bitcast.132), channel_id=1, source_target_pairs={{0,16},{1,17},{2,18},{3,19},{4,20},{5,21},{6,22},{7,23},{8,24},{9,... | collective-permute-start | bytes 884744 | tf_op jit(solution)/shard_map/ppermute | solution.py:221
  14.2 3.9 %other_rows.1 = (bf16[128,1152]{1,0:T(8,128)(2,1)S(1)}, bf16[2,8,72,256]{3,2,1,0:T(8,128)(2,1)S(1)}) custom-call(bf16[128,1152]{1,0:T(8,128)(2,1)S(1)} %collective-permute-done.refs_0_, f32[1,1152]{1,0:T(1,128)S(1)} %broadcast_in_dim.81.refs_1_, f32[3,576,1]{2,1,0:T(8,128)S(1)} %copy.59.refs_2_, f32[72,128]{1,0:T(8,128)S(1)} %get-tuple-element.70.refs_3_, ...), custom_call_target="tpu_custom_call" | custom-call | flops 849346560 | bytes 3981312 | tf_op jit(solution)/shard_map/other_rows/pallas_call | solution.py:592
  18.4 2.6 %own_rows.1.hidden_ref = f32[128,1152]{1,0:T(8,128)S(1)} custom-call(bf16[128,1152]{1,0:T(8,128)(2,1)S(1)} %bitcast.134, bf16[3,8,72,128]{3,2,1,0:T(8,128)(2,1)S(1)} %own_heads.1.refs_6_.refs_1_, bf16[2,8,72,256]{3,2,1,0:T(8,128)(2,1)S(1)} %get-tuple-element.24.refs_2_, bf16[576,1152]{1,0:T(8,128)(2,1)S(1)} %copy-done.6, f32[1,1152]{1,0:T(1,128)S(1)} %broadcast_in_dim.87.refs_4_), custom_call_target="tpu_custom_call" | custom-call | flops 339738624 | bytes 1327104 | tf_op jit(solution)/shard_map/own_rows/pallas_call | solution.py:615
  21.0 4.9 %collective-permute-done.1.arrived_ref = bf16[128,1152]{1,0:T(8,128)(2,1)S(1)} collective-permute-done((bf16[128,1152]{1,0:T(8,128)(2,1)S(1)}, bf16[128,1152]{1,0:T(8,128)(2,1)S(1)}, u32[]{:S(2)}, u32[]{:S(2)}) %collective-permute-start.1) | collective-permute-done | bytes 294944 | tf_op jit(solution)/shard_map/ppermute | solution.py:221
  27.0 3.9 %all-to-all-start = ((bf16[4,32,2304]{2,1,0:T(8,128)(2,1)}), bf16[4,32,2304]{2,1,0:T(8,128)(2,1)S(1)}, u32[]{:S(2)}, u32[]{:S(2)}) async-start(bf16[4,32,2304]{2,1,0:T(8,128)(2,1)} %bitcast.4), calls=%async_computation | async-start | bytes 1179648 | tf_op jit(solution)/shard_map/all_to_all | solution.py:653
  36.2 2.6 %assemble_rows.1.weight_ref = bf16[2304,1024]{1,0:T(8,128)(2,1)S(1)} custom-call(s32[8]{0:T(128)S(1)} %stack.107.spots_ref, bf16[288,1024]{1,0:T(8,128)(2,1)S(1)} %copy-done.10, bf16[288,1024]{1,0:T(8,128)(2,1)} %collective-permute-done.2.refs_1_, bf16[288,1024]{1,0:T(8,128)(2,1)S(1)} %collective-permute-done.3.refs_2_, ...), custom_call_target="tpu_custom_call" | custom-call | bytes 9437184 | tf_op jit(solution)/shard_map/assemble_rows/pallas_call | solution.py:449
  41.0 3.7 %all-to-all-done = bf16[4,32,2304]{2,1,0:T(8,128)(2,1)S(1)} async-done(((bf16[4,32,2304]{2,1,0:T(8,128)(2,1)}), bf16[4,32,2304]{2,1,0:T(8,128)(2,1)S(1)}, u32[]{:S(2)}, u32[]{:S(2)}) %all-to-all-start) | async-done | bytes 589856 | tf_op jit(solution)/shard_map/all_to_all | solution.py:653
  44.7 2.3 %copy-done.2 = bf16[2304,1024]{1,0:T(8,128)(2,1)S(1)} copy-done((bf16[2304,1024]{1,0:T(8,128)(2,1)S(1)}, bf16[2304,1024]{1,0:T(8,128)(2,1)}, u32[]{:S(2)}) %copy-start.2) | copy-done | bytes 4718616
  49.0 5.9 %collective-permute-done.9 = bf16[64,1024]{1,0:T(8,128)(2,1)S(1)} collective-permute-done((bf16[64,1024]{1,0:T(8,128)(2,1)S(1)}, bf16[64,1024]{1,0:T(8,128)(2,1)S(1)}, u32[]{:S(2)}, u32[]{:S(2)}) %collective-permute-start.9) | collective-permute-done | bytes 131104 | tf_op jit(solution)/shard_map/ppermute | solution.py:221
  56.0 2.9 %collective-permute-start.24 = (bf16[64,1152]{1,0:T(8,128)(2,1)S(1)}, bf16[64,1152]{1,0:T(8,128)(2,1)S(1)}, u32[]{:S(2)}, u32[]{:S(2)}) collective-permute-start(bf16[64,1152]{1,0:T(8,128)(2,1)S(1)} %get-tuple-element.33.mine_ref), channel_id=1, source_target_pairs={{0,8},{1,9},{2,10},{3,11},{4,12},{5,13},{6,14},{7,15},{8,0},{9,1},... | collective-permute-start | bytes 442376 | tf_op jit(solution)/shard_map/ppermute | solution.py:221
  64.5 5.6 %collective-permute-done.24 = bf16[64,1152]{1,0:T(8,128)(2,1)S(1)} collective-permute-done((bf16[64,1152]{1,0:T(8,128)(2,1)S(1)}, bf16[64,1152]{1,0:T(8,128)(2,1)S(1)}, u32[]{:S(2)}, u32[]{:S(2)}) %collective-permute-start.24) | collective-permute-done | bytes 147488 | tf_op jit(solution)/shard_map/ppermute | solution.py:221
  70.6 2.5 %collective-permute-start.34 = (bf16[64,1152]{1,0:T(8,128)(2,1)S(1)}, bf16[64,1152]{1,0:T(8,128)(2,1)S(1)}, u32[]{:S(2)}, u32[]{:S(2)}) collective-permute-start(bf16[64,1152]{1,0:T(8,128)(2,1)S(1)} %collective-permute-done.33), channel_id=1, source_target_pairs={{0,2},{1,3},{2,0},{3,1},{4,6},{5,7},{6,4},{7,5},{8,10},{9,11},{10,... | collective-permute-start | bytes 442376 | tf_op jit(solution)/shard_map/ppermute | solution.py:221
  74.5 2.3 %collective-permute-done.25 = bf16[64,1152]{1,0:T(8,128)(2,1)S(1)} collective-permute-done((bf16[64,1152]{1,0:T(8,128)(2,1)S(1)}, bf16[64,1152]{1,0:T(8,128)(2,1)S(1)}, u32[]{:S(2)}, u32[]{:S(2)}) %collective-permute-start.25) | collective-permute-done | bytes 147488 | tf_op jit(solution)/shard_map/ppermute | solution.py:221
  76.8 2.3 %collective-permute-start.26 = (bf16[2,64,1152]{2,1,0:T(8,128)(2,1)S(1)}, bf16[2,64,1152]{2,1,0:T(8,128)(2,1)S(1)}, u32[]{:S(2)}, u32[]{:S(2)}) collective-permute-start(bf16[2,64,1152]{2,1,0:T(8,128)(2,1)S(1)} %get-tuple-element.52), channel_id=1, source_target_pairs={{0,2},{1,3},{2,0},{3,1},{4,6},{5,7},{6,4},{7,5},{8,10},{9,11},{10,... | collective-permute-start | bytes 884744 | tf_op jit(solution)/shard_map/ppermute | solution.py:221
  80.3 2.8 %copy-done.5 = bf16[2048,2,704]{0,2,1:T(8,128)(2,1)S(1)} copy-done((bf16[2048,2,704]{0,2,1:T(8,128)(2,1)S(1)}, bf16[2048,2,704]{0,2,1:T(8,128)(2,1)}, u32[]{:S(2)}) %copy-start.5) | copy-done | bytes 5767192
  83.1 2.7 %shared_units.1.refs_7_ = f32[64,2048]{1,0:T(8,128)S(1)} custom-call(s32[1]{0:T(128)} %bitcast.15.place_ref.refs_0_, bf16[64,1152]{1,0:T(8,128)(2,1)S(1)} %get-tuple-element.33.mine_ref, bf16[64,1152]{1,0:T(8,128)(2,1)S(1)} %collective-permute-done.10.other_ref, f32[1,2048]{1,0:T(1,128)S(1)} %bitcast.135, bf16[2,704,2048]{2,1,0:T(8,128)(2,1)S(1)} %bitcast.129, ...), custom_call_target="tpu_custom_call" | custom-call | flops 553648128 | bytes 9175040 | tf_op jit(solution)/shard_map/shared_units/pallas_call | solution.py:330
  86.6 3.3 %expert_units.4 = (bf16[2,64,2048]{2,1,0:T(8,128)(2,1)S(1)}, bf16[2,64,2048]{2,1,0:T(8,128)(2,1)S(1)}) custom-call(s32[1]{0:T(128)} %bitcast.15.place_ref.refs_0_, bf16[2,2,64,1152]{3,2,1,0:T(8,128)(2,1)S(1)} %pad_maximum_fusion.refs_1_, bf16[2,2,64,1152]{3,2,1,0:T(8,128)(2,1)S(1)} %collective-permute-done.12.refs_2_, f32[1,2048]{1,0:T(1,128)S(1)} %bitcast.136, ...), custom_call_target="tpu_custom_call" | custom-call | flops 2214592512 | bytes 10747904 | tf_op jit(solution)/shard_map/expert_units/pallas_call | solution.py:303
  90.7 3.3 %expert_units.5 = (bf16[2,64,2048]{2,1,0:T(8,128)(2,1)S(1)}, bf16[2,64,2048]{2,1,0:T(8,128)(2,1)S(1)}) custom-call(s32[1]{0:T(128)} %bitcast.15.place_ref.refs_0_, bf16[2,2,64,1152]{3,2,1,0:T(8,128)(2,1)S(1)} %copy.69.refs_1_, bf16[2,2,64,1152]{3,2,1,0:T(8,128)(2,1)S(1)} %copy.70.refs_2_, f32[1,2048]{1,0:T(1,128)S(1)} %bitcast.137, ...), custom_call_target="tpu_custom_call" | custom-call | flops 2214592512 | bytes 10747904 | tf_op jit(solution)/shard_map/expert_units/pallas_call | solution.py:303
  94.1 3.5 %expert_units.6 = (bf16[2,64,2048]{2,1,0:T(8,128)(2,1)S(1)}, bf16[2,64,2048]{2,1,0:T(8,128)(2,1)S(1)}) custom-call(s32[1]{0:T(128)} %bitcast.15.place_ref.refs_0_, bf16[2,2,64,1152]{3,2,1,0:T(8,128)(2,1)S(1)} %pad_maximum_fusion.1.refs_1_, bf16[2,2,64,1152]{3,2,1,0:T(8,128)(2,1)S(1)} %collective-permute-done.27.refs_2_, f32[1,2048]{1,0:T(1,128)S(1)} %bitcast.138, ...), custom_call_target="tpu_custom_call" | custom-call | flops 2214592512 | bytes 10747904 | tf_op jit(solution)/shard_map/expert_units/pallas_call | solution.py:303
  105.0 3.3 %expert_units.7 = (bf16[2,64,2048]{2,1,0:T(8,128)(2,1)S(1)}, bf16[2,64,2048]{2,1,0:T(8,128)(2,1)S(1)}) custom-call(s32[1]{0:T(128)} %bitcast.15.place_ref.refs_0_, bf16[2,2,64,1152]{3,2,1,0:T(8,128)(2,1)S(1)} %maximum_bitcast_fusion.1.refs_1_, bf16[2,2,64,1152]{3,2,1,0:T(8,128)(2,1)S(1)} %collective-permute-done.36.refs_2_, f32[1,2048]{1,0:T(1,128)S(1)} %bitcast.139, ...), custom_call_target="tpu_custom_call" | custom-call | flops 2214592512 | bytes 10747904 | tf_op jit(solution)/shard_map/expert_units/pallas_call | solution.py:303
  110.4 2.3 %collective-permute-start.15 = (bf16[32,2048]{1,0:T(8,128)(2,1)S(1)}, bf16[32,2048]{1,0:T(8,128)(2,1)S(1)}, u32[]{:S(2)}, u32[]{:S(2)}) collective-permute-start(bf16[32,2048]{1,0:T(8,128)(2,1)S(1)} %slice_bitcast_fusion.8), channel_id=1, source_target_pairs={{0,2},{1,3},{2,0},{3,1},{4,6},{5,7},{6,4},{7,5},{8,10},{9,11},{10,... | collective-permute-start | bytes 393224 | tf_op jit(solution)/shard_map/ppermute | solution.py:221
  117.4 3.1 %collective-permute-start.40 = (bf16[32,2048]{1,0:T(8,128)(2,1)S(1)}, bf16[32,2048]{1,0:T(8,128)(2,1)S(1)}, u32[]{:S(2)}, u32[]{:S(2)}) collective-permute-start(bf16[32,2048]{1,0:T(8,128)(2,1)S(1)} %get-tuple-element.62), channel_id=1, source_target_pairs={{0,18},{1,19},{2,16},{3,17},{4,22},{5,23},{6,20},{7,21},{8,26},{9,... | collective-permute-start | bytes 393224 | tf_op jit(solution)/shard_map/ppermute | solution.py:221
  126.6 2.5 %collective-permute-start.41 = (bf16[32,2048]{1,0:T(8,128)(2,1)S(1)}, bf16[32,2048]{1,0:T(8,128)(2,1)S(1)}, u32[]{:S(2)}, u32[]{:S(2)}) collective-permute-start(bf16[32,2048]{1,0:T(8,128)(2,1)S(1)} %fusion.5), channel_id=1, source_target_pairs={{0,12},{1,13},{2,14},{3,15},{4,8},{5,9},{6,10},{7,11},{8,4},{9,5},... | collective-permute-start | bytes 393224 | tf_op jit(solution)/shard_map/ppermute | solution.py:221
  129.8 3.7 %collective-permute-done.41 = bf16[32,2048]{1,0:T(8,128)(2,1)S(1)} collective-permute-done((bf16[32,2048]{1,0:T(8,128)(2,1)S(1)}, bf16[32,2048]{1,0:T(8,128)(2,1)S(1)}, u32[]{:S(2)}, u32[]{:S(2)}) %collective-permute-start.41) | collective-permute-done | bytes 131104 | tf_op jit(solution)/shard_map/ppermute | solution.py:221
  (163 shorter events, 54.9 us)
Async XLA Ops:
  0.0 13.2 %collective-permute-start = (bf16[128,1152]{1,0:T(8,128)(2,1)}, bf16[128,1152]{1,0:T(8,128)(2,1)S(1)}, u32[]{:S(2)}, u32[]{:S(2)}) collective-permute-start(bf16[128,1152]{1,0:T(8,128)(2,1)} %bitcast.132), channel_id=1, source_target_pairs={{0,16},{1,17},{2,18},{3,19},{4,20},{5,21},{6,22},{7,23},{8,24},{9,... | collective-permute-start | bytes 884744 | tf_op jit(solution)/shard_map/ppermute | solution.py:221
  3.3 27.5 %collective-permute-start.3 = (bf16[288,1024]{1,0:T(8,128)(2,1)}, bf16[288,1024]{1,0:T(8,128)(2,1)S(1)}, u32[]{:S(2)}, u32[]{:S(2)}) collective-permute-start(bf16[288,1024]{1,0:T(8,128)(2,1)} %refs_0_.1), channel_id=1, source_target_pairs={{0,2},{1,3},{2,0},{3,1},{4,6},{5,7},{6,4},{7,5},{8,10},{9,11},{10,... | collective-permute-start | bytes 1769480 | tf_op jit(solution)/shard_map/ppermute | solution.py:221
  4.9 25.9 %collective-permute-start.5 = (bf16[288,1024]{1,0:T(8,128)(2,1)}, bf16[288,1024]{1,0:T(8,128)(2,1)S(1)}, u32[]{:S(2)}, u32[]{:S(2)}) collective-permute-start(bf16[288,1024]{1,0:T(8,128)(2,1)} %refs_0_.1), channel_id=1, source_target_pairs={{0,4},{1,5},{2,6},{3,7},{4,0},{5,1},{6,2},{7,3},{8,12},{9,13},{10,... | collective-permute-start | bytes 1769480 | tf_op jit(solution)/shard_map/ppermute | solution.py:221
  6.5 26.7 %collective-permute-start.7 = (bf16[288,1024]{1,0:T(8,128)(2,1)}, bf16[288,1024]{1,0:T(8,128)(2,1)S(1)}, u32[]{:S(2)}, u32[]{:S(2)}) collective-permute-start(bf16[288,1024]{1,0:T(8,128)(2,1)} %refs_0_.1), channel_id=1, source_target_pairs={{0,6},{1,7},{2,4},{3,5},{4,2},{5,3},{6,0},{7,1},{8,14},{9,15},{10,... | collective-permute-start | bytes 1769480 | tf_op jit(solution)/shard_map/ppermute | solution.py:221
  27.0 17.7 %all-to-all-start = ((bf16[4,32,2304]{2,1,0:T(8,128)(2,1)}), bf16[4,32,2304]{2,1,0:T(8,128)(2,1)S(1)}, u32[]{:S(2)}, u32[]{:S(2)}) async-start(bf16[4,32,2304]{2,1,0:T(8,128)(2,1)} %bitcast.4), calls=%async_computation | async-start | bytes 1179648 | tf_op jit(solution)/shard_map/all_to_all | solution.py:653
  55.0 9.1 %collective-permute-start.10 = (bf16[64,1152]{1,0:T(8,128)(2,1)S(1)}, bf16[64,1152]{1,0:T(8,128)(2,1)S(1)}, u32[]{:S(2)}, u32[]{:S(2)}) collective-permute-start(bf16[64,1152]{1,0:T(8,128)(2,1)S(1)} %get-tuple-element.33.mine_ref), channel_id=1, source_target_pairs={{0,16},{1,17},{2,18},{3,19},{4,20},{5,21},{6,22},{7,23},{8,24},{9,... | collective-permute-start | bytes 442376 | tf_op jit(solution)/shard_map/ppermute | solution.py:221
  56.0 14.0 %collective-permute-start.24 = (bf16[64,1152]{1,0:T(8,128)(2,1)S(1)}, bf16[64,1152]{1,0:T(8,128)(2,1)S(1)}, u32[]{:S(2)}, u32[]{:S(2)}) collective-permute-start(bf16[64,1152]{1,0:T(8,128)(2,1)S(1)} %get-tuple-element.33.mine_ref), channel_id=1, source_target_pairs={{0,8},{1,9},{2,10},{3,11},{4,12},{5,13},{6,14},{7,15},{8,0},{9,1},... | collective-permute-start | bytes 442376 | tf_op jit(solution)/shard_map/ppermute | solution.py:221
  58.9 11.8 %collective-permute-start.33 = (bf16[64,1152]{1,0:T(8,128)(2,1)S(1)}, bf16[64,1152]{1,0:T(8,128)(2,1)S(1)}, u32[]{:S(2)}, u32[]{:S(2)}) collective-permute-start(bf16[64,1152]{1,0:T(8,128)(2,1)S(1)} %get-tuple-element.33.mine_ref), channel_id=1, source_target_pairs={{0,12},{1,13},{2,14},{3,15},{4,8},{5,9},{6,10},{7,11},{8,4},{9,5},... | collective-permute-start | bytes 442376 | tf_op jit(solution)/shard_map/ppermute | solution.py:221
  62.3 10.8 %collective-permute-start.17 = (bf16[64,1152]{1,0:T(8,128)(2,1)S(1)}, bf16[64,1152]{1,0:T(8,128)(2,1)S(1)}, u32[]{:S(2)}, u32[]{:S(2)}) collective-permute-start(bf16[64,1152]{1,0:T(8,128)(2,1)S(1)} %collective-permute-done.16), channel_id=1, source_target_pairs={{0,2},{1,3},{2,0},{3,1},{4,6},{5,7},{6,4},{7,5},{8,10},{9,11},{10,... | collective-permute-start | bytes 442376 | tf_op jit(solution)/shard_map/ppermute | solution.py:221
  64.2 14.9 %collective-permute-start.11 = (bf16[2,64,1152]{2,1,0:T(8,128)(2,1)S(1)}, bf16[2,64,1152]{2,1,0:T(8,128)(2,1)S(1)}, u32[]{:S(2)}, u32[]{:S(2)}) collective-permute-start(bf16[2,64,1152]{2,1,0:T(8,128)(2,1)S(1)} %get-tuple-element.50), channel_id=1, source_target_pairs={{0,2},{1,3},{2,0},{3,1},{4,6},{5,7},{6,4},{7,5},{8,10},{9,11},{10,... | collective-permute-start | bytes 884744 | tf_op jit(solution)/shard_map/ppermute | solution.py:221
  70.6 8.6 %collective-permute-start.34 = (bf16[64,1152]{1,0:T(8,128)(2,1)S(1)}, bf16[64,1152]{1,0:T(8,128)(2,1)S(1)}, u32[]{:S(2)}, u32[]{:S(2)}) collective-permute-start(bf16[64,1152]{1,0:T(8,128)(2,1)S(1)} %collective-permute-done.33), channel_id=1, source_target_pairs={{0,2},{1,3},{2,0},{3,1},{4,6},{5,7},{6,4},{7,5},{8,10},{9,11},{10,... | collective-permute-start | bytes 442376 | tf_op jit(solution)/shard_map/ppermute | solution.py:221
  73.2 12.6 %collective-permute-start.18 = (bf16[2,64,1152]{2,1,0:T(8,128)(2,1)S(1)}, bf16[2,64,1152]{2,1,0:T(8,128)(2,1)S(1)}, u32[]{:S(2)}, u32[]{:S(2)}) collective-permute-start(bf16[2,64,1152]{2,1,0:T(8,128)(2,1)S(1)} %get-tuple-element.54), channel_id=1, source_target_pairs={{0,16},{1,17},{2,18},{3,19},{4,20},{5,21},{6,22},{7,23},{8,24},{9,... | collective-permute-start | bytes 884744 | tf_op jit(solution)/shard_map/ppermute | solution.py:221
  76.8 9.1 %collective-permute-start.26 = (bf16[2,64,1152]{2,1,0:T(8,128)(2,1)S(1)}, bf16[2,64,1152]{2,1,0:T(8,128)(2,1)S(1)}, u32[]{:S(2)}, u32[]{:S(2)}) collective-permute-start(bf16[2,64,1152]{2,1,0:T(8,128)(2,1)S(1)} %get-tuple-element.52), channel_id=1, source_target_pairs={{0,2},{1,3},{2,0},{3,1},{4,6},{5,7},{6,4},{7,5},{8,10},{9,11},{10,... | collective-permute-start | bytes 884744 | tf_op jit(solution)/shard_map/ppermute | solution.py:221
  79.3 10.7 %collective-permute-start.35 = (bf16[2,64,1152]{2,1,0:T(8,128)(2,1)S(1)}, bf16[2,64,1152]{2,1,0:T(8,128)(2,1)S(1)}, u32[]{:S(2)}, u32[]{:S(2)}) collective-permute-start(bf16[2,64,1152]{2,1,0:T(8,128)(2,1)S(1)} %get-tuple-element.56), channel_id=1, source_target_pairs={{0,16},{1,17},{2,18},{3,19},{4,20},{5,21},{6,22},{7,23},{8,24},{9,... | collective-permute-start | bytes 884744 | tf_op jit(solution)/shard_map/ppermute | solution.py:221
  89.9 8.3 %collective-permute-start.13 = (bf16[2,64,2048]{2,1,0:T(8,128)(2,1)S(1)}, bf16[2,64,2048]{2,1,0:T(8,128)(2,1)S(1)}, u32[]{:S(2)}, u32[]{:S(2)}) collective-permute-start(bf16[2,64,2048]{2,1,0:T(8,128)(2,1)S(1)} %get-tuple-element.35), channel_id=1, source_target_pairs={{0,1},{1,0},{2,3},{3,2},{4,5},{5,4},{6,7},{7,6},{8,9},{9,8},{10,11... | collective-permute-start | bytes 1572872 | tf_op jit(solution)/shard_map/ppermute | solution.py:221
  90.1 13.7 %collective-permute-start.36 = (bf16[2,2,64,1152]{3,2,1,0:T(8,128)(2,1)S(1)}, bf16[2,2,64,1152]{3,2,1,0:T(8,128)(2,1)S(1)}, u32[]{:S(2)}, u32[]{:S(2)}) collective-permute-start(bf16[2,2,64,1152]{3,2,1,0:T(8,128)(2,1)S(1)} %maximum_bitcast_fusion.1.refs_1_), channel_id=1, source_target_pairs={{0,1},{1,0},{2,3},{3,2},{4,5},{5,4},{6,7},{7,6},{8,9},{9,8},{10,11... | collective-permute-start | bytes 1769480 | tf_op jit(solution)/shard_map/ppermute | solution.py:221
  98.4 9.9 %collective-permute-start.14 = (bf16[2,32,2048]{2,1,0:T(8,128)(2,1)S(1)}, bf16[2,32,2048]{2,1,0:T(8,128)(2,1)S(1)}, u32[]{:S(2)}, u32[]{:S(2)}) collective-permute-start(bf16[2,32,2048]{2,1,0:T(8,128)(2,1)S(1)} %select_bitcast_fusion), channel_id=1, source_target_pairs={{0,16},{1,17},{2,18},{3,19},{4,20},{5,21},{6,22},{7,23},{8,24},{9,... | collective-permute-start | bytes 786440 | tf_op jit(solution)/shard_map/ppermute | solution.py:221
  99.8 15.1 %collective-permute-start.21 = (bf16[2,32,2048]{2,1,0:T(8,128)(2,1)S(1)}, bf16[2,32,2048]{2,1,0:T(8,128)(2,1)S(1)}, u32[]{:S(2)}, u32[]{:S(2)}) collective-permute-start(bf16[2,32,2048]{2,1,0:T(8,128)(2,1)S(1)} %bitcast.149), channel_id=1, source_target_pairs={{0,2},{1,3},{2,0},{3,1},{4,6},{5,7},{6,4},{7,5},{8,10},{9,11},{10,... | collective-permute-start | bytes 786440 | tf_op jit(solution)/shard_map/ppermute | solution.py:221
  101.3 9.2 %collective-permute-start.29 = (bf16[32,2048]{1,0:T(8,128)(2,1)S(1)}, bf16[32,2048]{1,0:T(8,128)(2,1)S(1)}, u32[]{:S(2)}, u32[]{:S(2)}) collective-permute-start(bf16[32,2048]{1,0:T(8,128)(2,1)S(1)} %get-tuple-element.59), channel_id=1, source_target_pairs={{0,16},{1,17},{2,18},{3,19},{4,20},{5,21},{6,22},{7,23},{8,24},{9,... | collective-permute-start | bytes 393224 | tf_op jit(solution)/shard_map/ppermute | solution.py:221
  103.3 10.8 %collective-permute-start.31 = (bf16[32,2048]{1,0:T(8,128)(2,1)S(1)}, bf16[32,2048]{1,0:T(8,128)(2,1)S(1)}, u32[]{:S(2)}, u32[]{:S(2)}) collective-permute-start(bf16[32,2048]{1,0:T(8,128)(2,1)S(1)} %get-tuple-element.60), channel_id=1, source_target_pairs={{0,18},{1,19},{2,16},{3,17},{4,22},{5,23},{6,20},{7,21},{8,26},{9,... | collective-permute-start | bytes 393224 | tf_op jit(solution)/shard_map/ppermute | solution.py:221
  103.8 10.3 %collective-permute-start.30 = (bf16[32,2048]{1,0:T(8,128)(2,1)S(1)}, bf16[32,2048]{1,0:T(8,128)(2,1)S(1)}, u32[]{:S(2)}, u32[]{:S(2)}) collective-permute-start(bf16[32,2048]{1,0:T(8,128)(2,1)S(1)} %slice_bitcast_fusion.5), channel_id=1, source_target_pairs={{0,2},{1,3},{2,0},{3,1},{4,6},{5,7},{6,4},{7,5},{8,10},{9,11},{10,... | collective-permute-start | bytes 393224 | tf_op jit(solution)/shard_map/ppermute | solution.py:221
  108.3 8.4 %collective-permute-start.37 = (bf16[2,64,2048]{2,1,0:T(8,128)(2,1)S(1)}, bf16[2,64,2048]{2,1,0:T(8,128)(2,1)S(1)}, u32[]{:S(2)}, u32[]{:S(2)}) collective-permute-start(bf16[2,64,2048]{2,1,0:T(8,128)(2,1)S(1)} %get-tuple-element.42), channel_id=1, source_target_pairs={{0,1},{1,0},{2,3},{3,2},{4,5},{5,4},{6,7},{7,6},{8,9},{9,8},{10,11... | collective-permute-start | bytes 1572872 | tf_op jit(solution)/shard_map/ppermute | solution.py:221
  110.4 18.7 %collective-permute-start.15 = (bf16[32,2048]{1,0:T(8,128)(2,1)S(1)}, bf16[32,2048]{1,0:T(8,128)(2,1)S(1)}, u32[]{:S(2)}, u32[]{:S(2)}) collective-permute-start(bf16[32,2048]{1,0:T(8,128)(2,1)S(1)} %slice_bitcast_fusion.8), channel_id=1, source_target_pairs={{0,2},{1,3},{2,0},{3,1},{4,6},{5,7},{6,4},{7,5},{8,10},{9,11},{10,... | collective-permute-start | bytes 393224 | tf_op jit(solution)/shard_map/ppermute | solution.py:221
  114.2 14.9 %collective-permute-start.32 = (bf16[32,2048]{1,0:T(8,128)(2,1)S(1)}, bf16[32,2048]{1,0:T(8,128)(2,1)S(1)}, u32[]{:S(2)}, u32[]{:S(2)}) collective-permute-start(bf16[32,2048]{1,0:T(8,128)(2,1)S(1)} %fusion.8), channel_id=1, source_target_pairs={{0,8},{1,9},{2,10},{3,11},{4,12},{5,13},{6,14},{7,15},{8,0},{9,1},... | collective-permute-start | bytes 393224 | tf_op jit(solution)/shard_map/ppermute | solution.py:221
  (36 other events, 254.0 us)

commit v7 on v6

--- a/solution.py
+++ b/solution.py
@@ -353,7 +353,7 @@
                 (((1,), (1,)), ((), ())),
                 preferred_element_type=jnp.float32,
             )
-            + bias_ref[which]
+            + jnp.broadcast_to(bias_ref[which : which + 1], (normed.shape[0], heads * HD)).T
         ).reshape(heads, HD, normed.shape[0])
         if which < 2:
             parts = [mixed[:, n * quarter : (n + 1) * quarter] for n in range(4)]
@@ -559,7 +559,7 @@
 
     heads = qkv_weight.shape[2] // HD
     weight_rows = qkv_weight.transpose(1, 2, 0)
-    bias_rows = qkv_bias[:, :, None]
+    bias_rows = qkv_bias
     quarter = HD // 4
     feature = jnp.arange(HD)
     inverse = jnp.exp(

time: 135 us -> 135 us (level)
    unnamed x35 -> x37, local copies, waits for them, and re-layouts: 11.5 us -> 13.1 us
where the time goes in v7:
time: 135 us
  starting transfers between devices  47 us (35%)
  waiting for transfers between devices  38.8 us (29%)
  Pallas kernels  28.6 us (21%)
  local copies, waits for them, and re-layouts  16.3 us (12%)
  other arithmetic  3.66 us (3%)
    ppermute x42, starting transfers between devices, near_swap(): return lax.ppermute(values, ('tile', *near_expert), pairs)  43.1 us
    ppermute x42, waiting for transfers between devices, near_swap(): return lax.ppermute(values, ('tile', *near_expert), pairs)  34.5 us
    pallas_call x4, Pallas kernels, run_expert(): pl.pallas_call(partial(expert_kernel, extra is not None), out_shape=(out,...  13.5 us
    unnamed x37, local copies, waits for them, and re-layouts  13.1 us
    all_to_all x1, waiting for transfers between devices, per_device_near(): lax.all_to_all(merged.reshape(4, token_count, -1), ('tile', 'half'), spli...  4.31 us
    pallas_call x1, Pallas kernels, per_device_near(): pl.pallas_call(partial(other_rows_kernel, heads), out_shape=(jax.ShapeDty...  3.89 us
    all_to_all x1, starting transfers between devices, per_device_near(): lax.all_to_all(merged.reshape(4, token_count, -1), ('tile', 'half'), spli...  3.86 us
  transfers between devices with their start and end apart: 43, of which 16 were waited for; matrix products, arithmetic and copies ran while one was open for 5% of the time, Pallas kernels for 21%

profile of v7, /device:TPU:0, one launch (start us, length us, event | category | flops | bytes accessed | tf_op | source)
XLA Modules:
  0.0 134.9 jit_solution(14517274146484086672)
XLA Ops:
  0.0 2.9 %collective-permute-start = (bf16[128,1152]{1,0:T(8,128)(2,1)}, bf16[128,1152]{1,0:T(8,128)(2,1)S(1)}, u32[]{:S(2)}, u32[]{:S(2)}) collective-permute-start(bf16[128,1152]{1,0:T(8,128)(2,1)} %bitcast.131), channel_id=1, source_target_pairs={{0,16},{1,17},{2,18},{3,19},{4,20},{5,21},{6,22},{7,23},{8,24},{9,... | collective-permute-start | bytes 884744 | tf_op jit(solution)/shard_map/ppermute | solution.py:221
  7.6 2.1 %copy-done.3 = bf16[1152,3,576]{0,2,1:T(8,128)(2,1)S(1)} copy-done((bf16[1152,3,576]{0,2,1:T(8,128)(2,1)S(1)}, bf16[1152,3,576]{0,2,1:T(8,128)(2,1)}, u32[]{:S(2)}) %copy-start.3) | copy-done | bytes 3981336
  14.8 3.9 %other_rows.1 = (bf16[128,1152]{1,0:T(8,128)(2,1)S(1)}, bf16[2,8,72,256]{3,2,1,0:T(8,128)(2,1)S(1)}) custom-call(bf16[128,1152]{1,0:T(8,128)(2,1)S(1)} %collective-permute-done.refs_0_, f32[1,1152]{1,0:T(1,128)S(1)} %broadcast_in_dim.78.refs_1_, f32[3,576]{1,0:T(4,128)S(1)} %copy-done.12, f32[72,128]{1,0:T(8,128)S(1)} %get-tuple-element.70.refs_3_, ...), custom_call_target="tpu_custom_call" | custom-call | flops 849346560 | bytes 3981312 | tf_op jit(solution)/shard_map/other_rows/pallas_call | solution.py:592
  19.0 2.6 %own_rows.1.hidden_ref = f32[128,1152]{1,0:T(8,128)S(1)} custom-call(bf16[128,1152]{1,0:T(8,128)(2,1)S(1)} %bitcast.133, bf16[3,8,72,128]{3,2,1,0:T(8,128)(2,1)S(1)} %own_heads.1.refs_6_.refs_1_, bf16[2,8,72,256]{3,2,1,0:T(8,128)(2,1)S(1)} %get-tuple-element.24.refs_2_, bf16[576,1152]{1,0:T(8,128)(2,1)S(1)} %copy-done.6, f32[1,1152]{1,0:T(1,128)S(1)} %broadcast_in_dim.83.refs_4_), custom_call_target="tpu_custom_call" | custom-call | flops 339738624 | bytes 1327104 | tf_op jit(solution)/shard_map/own_rows/pallas_call | solution.py:615
  21.6 4.9 %collective-permute-done.1.arrived_ref = bf16[128,1152]{1,0:T(8,128)(2,1)S(1)} collective-permute-done((bf16[128,1152]{1,0:T(8,128)(2,1)S(1)}, bf16[128,1152]{1,0:T(8,128)(2,1)S(1)}, u32[]{:S(2)}, u32[]{:S(2)}) %collective-permute-start.1) | collective-permute-done | bytes 294944 | tf_op jit(solution)/shard_map/ppermute | solution.py:221
  27.6 3.9 %all-to-all-start = ((bf16[4,32,2304]{2,1,0:T(8,128)(2,1)}), bf16[4,32,2304]{2,1,0:T(8,128)(2,1)S(1)}, u32[]{:S(2)}, u32[]{:S(2)}) async-start(bf16[4,32,2304]{2,1,0:T(8,128)(2,1)} %bitcast.3), calls=%async_computation | async-start | bytes 1179648 | tf_op jit(solution)/shard_map/all_to_all | solution.py:653
  36.2 2.6 %assemble_rows.1.weight_ref = bf16[2304,1024]{1,0:T(8,128)(2,1)S(1)} custom-call(s32[8]{0:T(128)S(1)} %stack.107.spots_ref, bf16[288,1024]{1,0:T(8,128)(2,1)S(1)} %copy-done.10, bf16[288,1024]{1,0:T(8,128)(2,1)} %collective-permute-done.2.refs_1_, bf16[288,1024]{1,0:T(8,128)(2,1)S(1)} %collective-permute-done.3.refs_2_, ...), custom_call_target="tpu_custom_call" | custom-call | bytes 9437184 | tf_op jit(solution)/shard_map/assemble_rows/pallas_call | solution.py:449
  38.8 2.2 %copy-done.1 = bf16[2304,1024]{1,0:T(8,128)(2,1)} copy-done((bf16[2304,1024]{1,0:T(8,128)(2,1)}, bf16[2304,1024]{1,0:T(8,128)(2,1)S(1)}, u32[]{:S(2)}) %copy-start.1) | copy-done | bytes 4718616
  41.0 4.3 %all-to-all-done = bf16[4,32,2304]{2,1,0:T(8,128)(2,1)S(1)} async-done(((bf16[4,32,2304]{2,1,0:T(8,128)(2,1)}), bf16[4,32,2304]{2,1,0:T(8,128)(2,1)S(1)}, u32[]{:S(2)}, u32[]{:S(2)}) %all-to-all-start) | async-done | bytes 589856 | tf_op jit(solution)/shard_map/all_to_all | solution.py:653
  45.3 2.3 %copy-done.2 = bf16[2304,1024]{1,0:T(8,128)(2,1)S(1)} copy-done((bf16[2304,1024]{1,0:T(8,128)(2,1)S(1)}, bf16[2304,1024]{1,0:T(8,128)(2,1)}, u32[]{:S(2)}) %copy-start.2) | copy-done | bytes 4718616
  49.5 6.4 %collective-permute-done.9 = bf16[64,1024]{1,0:T(8,128)(2,1)S(1)} collective-permute-done((bf16[64,1024]{1,0:T(8,128)(2,1)S(1)}, bf16[64,1024]{1,0:T(8,128)(2,1)S(1)}, u32[]{:S(2)}, u32[]{:S(2)}) %collective-permute-start.9) | collective-permute-done | bytes 131104 | tf_op jit(solution)/shard_map/ppermute | solution.py:221
  57.0 2.4 %collective-permute-start.24 = (bf16[64,1152]{1,0:T(8,128)(2,1)S(1)}, bf16[64,1152]{1,0:T(8,128)(2,1)S(1)}, u32[]{:S(2)}, u32[]{:S(2)}) collective-permute-start(bf16[64,1152]{1,0:T(8,128)(2,1)S(1)} %get-tuple-element.33.mine_ref), channel_id=1, source_target_pairs={{0,8},{1,9},{2,10},{3,11},{4,12},{5,13},{6,14},{7,15},{8,0},{9,1},... | collective-permute-start | bytes 442376 | tf_op jit(solution)/shard_map/ppermute | solution.py:221
  65.3 5.6 %collective-permute-done.24 = bf16[64,1152]{1,0:T(8,128)(2,1)S(1)} collective-permute-done((bf16[64,1152]{1,0:T(8,128)(2,1)S(1)}, bf16[64,1152]{1,0:T(8,128)(2,1)S(1)}, u32[]{:S(2)}, u32[]{:S(2)}) %collective-permute-start.24) | collective-permute-done | bytes 147488 | tf_op jit(solution)/shard_map/ppermute | solution.py:221
  71.6 2.3 %collective-permute-start.34 = (bf16[64,1152]{1,0:T(8,128)(2,1)S(1)}, bf16[64,1152]{1,0:T(8,128)(2,1)S(1)}, u32[]{:S(2)}, u32[]{:S(2)}) collective-permute-start(bf16[64,1152]{1,0:T(8,128)(2,1)S(1)} %collective-permute-done.33), channel_id=1, source_target_pairs={{0,2},{1,3},{2,0},{3,1},{4,6},{5,7},{6,4},{7,5},{8,10},{9,11},{10,... | collective-permute-start | bytes 442376 | tf_op jit(solution)/shard_map/ppermute | solution.py:221
  74.9 2.7 %collective-permute-done.25 = bf16[64,1152]{1,0:T(8,128)(2,1)S(1)} collective-permute-done((bf16[64,1152]{1,0:T(8,128)(2,1)S(1)}, bf16[64,1152]{1,0:T(8,128)(2,1)S(1)}, u32[]{:S(2)}, u32[]{:S(2)}) %collective-permute-start.25) | collective-permute-done | bytes 147488 | tf_op jit(solution)/shard_map/ppermute | solution.py:221
  80.4 2.8 %copy-done.5 = bf16[2048,2,704]{0,2,1:T(8,128)(2,1)S(1)} copy-done((bf16[2048,2,704]{0,2,1:T(8,128)(2,1)S(1)}, bf16[2048,2,704]{0,2,1:T(8,128)(2,1)}, u32[]{:S(2)}) %copy-start.5) | copy-done | bytes 5767192
  83.2 2.7 %shared_units.1.refs_7_ = f32[64,2048]{1,0:T(8,128)S(1)} custom-call(s32[1]{0:T(128)} %bitcast.14.place_ref.refs_0_, bf16[64,1152]{1,0:T(8,128)(2,1)S(1)} %get-tuple-element.33.mine_ref, bf16[64,1152]{1,0:T(8,128)(2,1)S(1)} %collective-permute-done.10.other_ref, f32[1,2048]{1,0:T(1,128)S(1)} %bitcast.134, bf16[2,704,2048]{2,1,0:T(8,128)(2,1)S(1)} %bitcast.128, ...), custom_call_target="tpu_custom_call" | custom-call | flops 553648128 | bytes 9175040 | tf_op jit(solution)/shard_map/shared_units/pallas_call | solution.py:330
  86.7 3.3 %expert_units.4 = (bf16[2,64,2048]{2,1,0:T(8,128)(2,1)S(1)}, bf16[2,64,2048]{2,1,0:T(8,128)(2,1)S(1)}) custom-call(s32[1]{0:T(128)} %bitcast.14.place_ref.refs_0_, bf16[2,2,64,1152]{3,2,1,0:T(8,128)(2,1)S(1)} %pad_maximum_fusion.refs_1_, bf16[2,2,64,1152]{3,2,1,0:T(8,128)(2,1)S(1)} %collective-permute-done.12.refs_2_, f32[1,2048]{1,0:T(1,128)S(1)} %bitcast.135, ...), custom_call_target="tpu_custom_call" | custom-call | flops 2214592512 | bytes 10747904 | tf_op jit(solution)/shard_map/expert_units/pallas_call | solution.py:303
  90.9 3.3 %expert_units.5 = (bf16[2,64,2048]{2,1,0:T(8,128)(2,1)S(1)}, bf16[2,64,2048]{2,1,0:T(8,128)(2,1)S(1)}) custom-call(s32[1]{0:T(128)} %bitcast.14.place_ref.refs_0_, bf16[2,2,64,1152]{3,2,1,0:T(8,128)(2,1)S(1)} %copy.61.refs_1_, bf16[2,2,64,1152]{3,2,1,0:T(8,128)(2,1)S(1)} %copy.62.refs_2_, f32[1,2048]{1,0:T(1,128)S(1)} %bitcast.136, ...), custom_call_target="tpu_custom_call" | custom-call | flops 2214592512 | bytes 10747904 | tf_op jit(solution)/shard_map/expert_units/pallas_call | solution.py:303
  94.3 3.5 %expert_units.6 = (bf16[2,64,2048]{2,1,0:T(8,128)(2,1)S(1)}, bf16[2,64,2048]{2,1,0:T(8,128)(2,1)S(1)}) custom-call(s32[1]{0:T(128)} %bitcast.14.place_ref.refs_0_, bf16[2,2,64,1152]{3,2,1,0:T(8,128)(2,1)S(1)} %pad_maximum_fusion.1.refs_1_, bf16[2,2,64,1152]{3,2,1,0:T(8,128)(2,1)S(1)} %collective-permute-done.27.refs_2_, f32[1,2048]{1,0:T(1,128)S(1)} %bitcast.137, ...), custom_call_target="tpu_custom_call" | custom-call | flops 2214592512 | bytes 10747904 | tf_op jit(solution)/shard_map/expert_units/pallas_call | solution.py:303
  105.1 3.3 %expert_units.7 = (bf16[2,64,2048]{2,1,0:T(8,128)(2,1)S(1)}, bf16[2,64,2048]{2,1,0:T(8,128)(2,1)S(1)}) custom-call(s32[1]{0:T(128)} %bitcast.14.place_ref.refs_0_, bf16[2,2,64,1152]{3,2,1,0:T(8,128)(2,1)S(1)} %maximum_bitcast_fusion.1.refs_1_, bf16[2,2,64,1152]{3,2,1,0:T(8,128)(2,1)S(1)} %collective-permute-done.36.refs_2_, f32[1,2048]{1,0:T(1,128)S(1)} %bitcast.138, ...), custom_call_target="tpu_custom_call" | custom-call | flops 2214592512 | bytes 10747904 | tf_op jit(solution)/shard_map/expert_units/pallas_call | solution.py:303
  118.0 3.1 %collective-permute-start.40 = (bf16[32,2048]{1,0:T(8,128)(2,1)S(1)}, bf16[32,2048]{1,0:T(8,128)(2,1)S(1)}, u32[]{:S(2)}, u32[]{:S(2)}) collective-permute-start(bf16[32,2048]{1,0:T(8,128)(2,1)S(1)} %get-tuple-element.62), channel_id=1, source_target_pairs={{0,18},{1,19},{2,16},{3,17},{4,22},{5,23},{6,20},{7,21},{8,26},{9,... | collective-permute-start | bytes 393224 | tf_op jit(solution)/shard_map/ppermute | solution.py:221
  127.2 2.2 %collective-permute-start.41 = (bf16[32,2048]{1,0:T(8,128)(2,1)S(1)}, bf16[32,2048]{1,0:T(8,128)(2,1)S(1)}, u32[]{:S(2)}, u32[]{:S(2)}) collective-permute-start(bf16[32,2048]{1,0:T(8,128)(2,1)S(1)} %fusion.5), channel_id=1, source_target_pairs={{0,12},{1,13},{2,14},{3,15},{4,8},{5,9},{6,10},{7,11},{8,4},{9,5},... | collective-permute-start | bytes 393224 | tf_op jit(solution)/shard_map/ppermute | solution.py:221
  130.5 3.7 %collective-permute-done.41 = bf16[32,2048]{1,0:T(8,128)(2,1)S(1)} collective-permute-done((bf16[32,2048]{1,0:T(8,128)(2,1)S(1)}, bf16[32,2048]{1,0:T(8,128)(2,1)S(1)}, u32[]{:S(2)}, u32[]{:S(2)}) %collective-permute-start.41) | collective-permute-done | bytes 131104 | tf_op jit(solution)/shard_map/ppermute | solution.py:221
  (164 shorter events, 55.2 us)
Async XLA Ops:
  0.0 12.9 %collective-permute-start = (bf16[128,1152]{1,0:T(8,128)(2,1)}, bf16[128,1152]{1,0:T(8,128)(2,1)S(1)}, u32[]{:S(2)}, u32[]{:S(2)}) collective-permute-start(bf16[128,1152]{1,0:T(8,128)(2,1)} %bitcast.131), channel_id=1, source_target_pairs={{0,16},{1,17},{2,18},{3,19},{4,20},{5,21},{6,22},{7,23},{8,24},{9,... | collective-permute-start | bytes 884744 | tf_op jit(solution)/shard_map/ppermute | solution.py:221
  3.3 28.1 %collective-permute-start.3 = (bf16[288,1024]{1,0:T(8,128)(2,1)}, bf16[288,1024]{1,0:T(8,128)(2,1)S(1)}, u32[]{:S(2)}, u32[]{:S(2)}) collective-permute-start(bf16[288,1024]{1,0:T(8,128)(2,1)} %refs_0_.1), channel_id=1, source_target_pairs={{0,2},{1,3},{2,0},{3,1},{4,6},{5,7},{6,4},{7,5},{8,10},{9,11},{10,... | collective-permute-start | bytes 1769480 | tf_op jit(solution)/shard_map/ppermute | solution.py:221
  4.9 26.5 %collective-permute-start.5 = (bf16[288,1024]{1,0:T(8,128)(2,1)}, bf16[288,1024]{1,0:T(8,128)(2,1)S(1)}, u32[]{:S(2)}, u32[]{:S(2)}) collective-permute-start(bf16[288,1024]{1,0:T(8,128)(2,1)} %refs_0_.1), channel_id=1, source_target_pairs={{0,4},{1,5},{2,6},{3,7},{4,0},{5,1},{6,2},{7,3},{8,12},{9,13},{10,... | collective-permute-start | bytes 1769480 | tf_op jit(solution)/shard_map/ppermute | solution.py:221
  6.5 26.7 %collective-permute-start.7 = (bf16[288,1024]{1,0:T(8,128)(2,1)}, bf16[288,1024]{1,0:T(8,128)(2,1)S(1)}, u32[]{:S(2)}, u32[]{:S(2)}) collective-permute-start(bf16[288,1024]{1,0:T(8,128)(2,1)} %refs_0_.1), channel_id=1, source_target_pairs={{0,6},{1,7},{2,4},{3,5},{4,2},{5,3},{6,0},{7,1},{8,14},{9,15},{10,... | collective-permute-start | bytes 1769480 | tf_op jit(solution)/shard_map/ppermute | solution.py:221
  27.6 17.7 %all-to-all-start = ((bf16[4,32,2304]{2,1,0:T(8,128)(2,1)}), bf16[4,32,2304]{2,1,0:T(8,128)(2,1)S(1)}, u32[]{:S(2)}, u32[]{:S(2)}) async-start(bf16[4,32,2304]{2,1,0:T(8,128)(2,1)} %bitcast.3), calls=%async_computation | async-start | bytes 1179648 | tf_op jit(solution)/shard_map/all_to_all | solution.py:653
  56.1 9.1 %collective-permute-start.10 = (bf16[64,1152]{1,0:T(8,128)(2,1)S(1)}, bf16[64,1152]{1,0:T(8,128)(2,1)S(1)}, u32[]{:S(2)}, u32[]{:S(2)}) collective-permute-start(bf16[64,1152]{1,0:T(8,128)(2,1)S(1)} %get-tuple-element.33.mine_ref), channel_id=1, source_target_pairs={{0,16},{1,17},{2,18},{3,19},{4,20},{5,21},{6,22},{7,23},{8,24},{9,... | collective-permute-start | bytes 442376 | tf_op jit(solution)/shard_map/ppermute | solution.py:221
  57.0 13.9 %collective-permute-start.24 = (bf16[64,1152]{1,0:T(8,128)(2,1)S(1)}, bf16[64,1152]{1,0:T(8,128)(2,1)S(1)}, u32[]{:S(2)}, u32[]{:S(2)}) collective-permute-start(bf16[64,1152]{1,0:T(8,128)(2,1)S(1)} %get-tuple-element.33.mine_ref), channel_id=1, source_target_pairs={{0,8},{1,9},{2,10},{3,11},{4,12},{5,13},{6,14},{7,15},{8,0},{9,1},... | collective-permute-start | bytes 442376 | tf_op jit(solution)/shard_map/ppermute | solution.py:221
  59.5 12.2 %collective-permute-start.33 = (bf16[64,1152]{1,0:T(8,128)(2,1)S(1)}, bf16[64,1152]{1,0:T(8,128)(2,1)S(1)}, u32[]{:S(2)}, u32[]{:S(2)}) collective-permute-start(bf16[64,1152]{1,0:T(8,128)(2,1)S(1)} %get-tuple-element.33.mine_ref), channel_id=1, source_target_pairs={{0,12},{1,13},{2,14},{3,15},{4,8},{5,9},{6,10},{7,11},{8,4},{9,5},... | collective-permute-start | bytes 442376 | tf_op jit(solution)/shard_map/ppermute | solution.py:221
  63.2 10.8 %collective-permute-start.17 = (bf16[64,1152]{1,0:T(8,128)(2,1)S(1)}, bf16[64,1152]{1,0:T(8,128)(2,1)S(1)}, u32[]{:S(2)}, u32[]{:S(2)}) collective-permute-start(bf16[64,1152]{1,0:T(8,128)(2,1)S(1)} %collective-permute-done.16), channel_id=1, source_target_pairs={{0,2},{1,3},{2,0},{3,1},{4,6},{5,7},{6,4},{7,5},{8,10},{9,11},{10,... | collective-permute-start | bytes 442376 | tf_op jit(solution)/shard_map/ppermute | solution.py:221
  65.3 14.2 %collective-permute-start.11 = (bf16[2,64,1152]{2,1,0:T(8,128)(2,1)S(1)}, bf16[2,64,1152]{2,1,0:T(8,128)(2,1)S(1)}, u32[]{:S(2)}, u32[]{:S(2)}) collective-permute-start(bf16[2,64,1152]{2,1,0:T(8,128)(2,1)S(1)} %get-tuple-element.50), channel_id=1, source_target_pairs={{0,2},{1,3},{2,0},{3,1},{4,6},{5,7},{6,4},{7,5},{8,10},{9,11},{10,... | collective-permute-start | bytes 884744 | tf_op jit(solution)/shard_map/ppermute | solution.py:221
  74.0 11.9 %collective-permute-start.18 = (bf16[2,64,1152]{2,1,0:T(8,128)(2,1)S(1)}, bf16[2,64,1152]{2,1,0:T(8,128)(2,1)S(1)}, u32[]{:S(2)}, u32[]{:S(2)}) collective-permute-start(bf16[2,64,1152]{2,1,0:T(8,128)(2,1)S(1)} %get-tuple-element.54), channel_id=1, source_target_pairs={{0,16},{1,17},{2,18},{3,19},{4,20},{5,21},{6,22},{7,23},{8,24},{9,... | collective-permute-start | bytes 884744 | tf_op jit(solution)/shard_map/ppermute | solution.py:221
  77.6 8.4 %collective-permute-start.26 = (bf16[2,64,1152]{2,1,0:T(8,128)(2,1)S(1)}, bf16[2,64,1152]{2,1,0:T(8,128)(2,1)S(1)}, u32[]{:S(2)}, u32[]{:S(2)}) collective-permute-start(bf16[2,64,1152]{2,1,0:T(8,128)(2,1)S(1)} %get-tuple-element.52), channel_id=1, source_target_pairs={{0,2},{1,3},{2,0},{3,1},{4,6},{5,7},{6,4},{7,5},{8,10},{9,11},{10,... | collective-permute-start | bytes 884744 | tf_op jit(solution)/shard_map/ppermute | solution.py:221
  79.6 10.5 %collective-permute-start.35 = (bf16[2,64,1152]{2,1,0:T(8,128)(2,1)S(1)}, bf16[2,64,1152]{2,1,0:T(8,128)(2,1)S(1)}, u32[]{:S(2)}, u32[]{:S(2)}) collective-permute-start(bf16[2,64,1152]{2,1,0:T(8,128)(2,1)S(1)} %get-tuple-element.56), channel_id=1, source_target_pairs={{0,16},{1,17},{2,18},{3,19},{4,20},{5,21},{6,22},{7,23},{8,24},{9,... | collective-permute-start | bytes 884744 | tf_op jit(solution)/shard_map/ppermute | solution.py:221
  86.1 8.1 %collective-permute-start.27 = (bf16[2,2,64,1152]{3,2,1,0:T(8,128)(2,1)S(1)}, bf16[2,2,64,1152]{3,2,1,0:T(8,128)(2,1)S(1)}, u32[]{:S(2)}, u32[]{:S(2)}) collective-permute-start(bf16[2,2,64,1152]{3,2,1,0:T(8,128)(2,1)S(1)} %pad_maximum_fusion.1.refs_1_), channel_id=1, source_target_pairs={{0,1},{1,0},{2,3},{3,2},{4,5},{5,4},{6,7},{7,6},{8,9},{9,8},{10,11... | collective-permute-start | bytes 1769480 | tf_op jit(solution)/shard_map/ppermute | solution.py:221
  90.0 8.3 %collective-permute-start.13 = (bf16[2,64,2048]{2,1,0:T(8,128)(2,1)S(1)}, bf16[2,64,2048]{2,1,0:T(8,128)(2,1)S(1)}, u32[]{:S(2)}, u32[]{:S(2)}) collective-permute-start(bf16[2,64,2048]{2,1,0:T(8,128)(2,1)S(1)} %get-tuple-element.35), channel_id=1, source_target_pairs={{0,1},{1,0},{2,3},{3,2},{4,5},{5,4},{6,7},{7,6},{8,9},{9,8},{10,11... | collective-permute-start | bytes 1572872 | tf_op jit(solution)/shard_map/ppermute | solution.py:221
  90.3 13.7 %collective-permute-start.36 = (bf16[2,2,64,1152]{3,2,1,0:T(8,128)(2,1)S(1)}, bf16[2,2,64,1152]{3,2,1,0:T(8,128)(2,1)S(1)}, u32[]{:S(2)}, u32[]{:S(2)}) collective-permute-start(bf16[2,2,64,1152]{3,2,1,0:T(8,128)(2,1)S(1)} %maximum_bitcast_fusion.1.refs_1_), channel_id=1, source_target_pairs={{0,1},{1,0},{2,3},{3,2},{4,5},{5,4},{6,7},{7,6},{8,9},{9,8},{10,11... | collective-permute-start | bytes 1769480 | tf_op jit(solution)/shard_map/ppermute | solution.py:221
  98.5 9.9 %collective-permute-start.14 = (bf16[2,32,2048]{2,1,0:T(8,128)(2,1)S(1)}, bf16[2,32,2048]{2,1,0:T(8,128)(2,1)S(1)}, u32[]{:S(2)}, u32[]{:S(2)}) collective-permute-start(bf16[2,32,2048]{2,1,0:T(8,128)(2,1)S(1)} %select_bitcast_fusion), channel_id=1, source_target_pairs={{0,16},{1,17},{2,18},{3,19},{4,20},{5,21},{6,22},{7,23},{8,24},{9,... | collective-permute-start | bytes 786440 | tf_op jit(solution)/shard_map/ppermute | solution.py:221
  100.1 15.4 %collective-permute-start.21 = (bf16[2,32,2048]{2,1,0:T(8,128)(2,1)S(1)}, bf16[2,32,2048]{2,1,0:T(8,128)(2,1)S(1)}, u32[]{:S(2)}, u32[]{:S(2)}) collective-permute-start(bf16[2,32,2048]{2,1,0:T(8,128)(2,1)S(1)} %bitcast.148), channel_id=1, source_target_pairs={{0,2},{1,3},{2,0},{3,1},{4,6},{5,7},{6,4},{7,5},{8,10},{9,11},{10,... | collective-permute-start | bytes 786440 | tf_op jit(solution)/shard_map/ppermute | solution.py:221
  101.5 9.1 %collective-permute-start.29 = (bf16[32,2048]{1,0:T(8,128)(2,1)S(1)}, bf16[32,2048]{1,0:T(8,128)(2,1)S(1)}, u32[]{:S(2)}, u32[]{:S(2)}) collective-permute-start(bf16[32,2048]{1,0:T(8,128)(2,1)S(1)} %get-tuple-element.59), channel_id=1, source_target_pairs={{0,16},{1,17},{2,18},{3,19},{4,20},{5,21},{6,22},{7,23},{8,24},{9,... | collective-permute-start | bytes 393224 | tf_op jit(solution)/shard_map/ppermute | solution.py:221
  103.2 10.8 %collective-permute-start.31 = (bf16[32,2048]{1,0:T(8,128)(2,1)S(1)}, bf16[32,2048]{1,0:T(8,128)(2,1)S(1)}, u32[]{:S(2)}, u32[]{:S(2)}) collective-permute-start(bf16[32,2048]{1,0:T(8,128)(2,1)S(1)} %get-tuple-element.60), channel_id=1, source_target_pairs={{0,18},{1,19},{2,16},{3,17},{4,22},{5,23},{6,20},{7,21},{8,26},{9,... | collective-permute-start | bytes 393224 | tf_op jit(solution)/shard_map/ppermute | solution.py:221
  104.0 10.1 %collective-permute-start.30 = (bf16[32,2048]{1,0:T(8,128)(2,1)S(1)}, bf16[32,2048]{1,0:T(8,128)(2,1)S(1)}, u32[]{:S(2)}, u32[]{:S(2)}) collective-permute-start(bf16[32,2048]{1,0:T(8,128)(2,1)S(1)} %slice_bitcast_fusion.5), channel_id=1, source_target_pairs={{0,2},{1,3},{2,0},{3,1},{4,6},{5,7},{6,4},{7,5},{8,10},{9,11},{10,... | collective-permute-start | bytes 393224 | tf_op jit(solution)/shard_map/ppermute | solution.py:221
  108.4 8.4 %collective-permute-start.37 = (bf16[2,64,2048]{2,1,0:T(8,128)(2,1)S(1)}, bf16[2,64,2048]{2,1,0:T(8,128)(2,1)S(1)}, u32[]{:S(2)}, u32[]{:S(2)}) collective-permute-start(bf16[2,64,2048]{2,1,0:T(8,128)(2,1)S(1)} %get-tuple-element.42), channel_id=1, source_target_pairs={{0,1},{1,0},{2,3},{3,2},{4,5},{5,4},{6,7},{7,6},{8,9},{9,8},{10,11... | collective-permute-start | bytes 1572872 | tf_op jit(solution)/shard_map/ppermute | solution.py:221
  110.6 18.9 %collective-permute-start.15 = (bf16[32,2048]{1,0:T(8,128)(2,1)S(1)}, bf16[32,2048]{1,0:T(8,128)(2,1)S(1)}, u32[]{:S(2)}, u32[]{:S(2)}) collective-permute-start(bf16[32,2048]{1,0:T(8,128)(2,1)S(1)} %slice_bitcast_fusion.8), channel_id=1, source_target_pairs={{0,2},{1,3},{2,0},{3,1},{4,6},{5,7},{6,4},{7,5},{8,10},{9,11},{10,... | collective-permute-start | bytes 393224 | tf_op jit(solution)/shard_map/ppermute | solution.py:221
  114.2 15.3 %collective-permute-start.32 = (bf16[32,2048]{1,0:T(8,128)(2,1)S(1)}, bf16[32,2048]{1,0:T(8,128)(2,1)S(1)}, u32[]{:S(2)}, u32[]{:S(2)}) collective-permute-start(bf16[32,2048]{1,0:T(8,128)(2,1)S(1)} %fusion.8), channel_id=1, source_target_pairs={{0,8},{1,9},{2,10},{3,11},{4,12},{5,13},{6,14},{7,15},{8,0},{9,1},... | collective-permute-start | bytes 393224 | tf_op jit(solution)/shard_map/ppermute | solution.py:221
  (37 other events, 257.9 us)
